TPU v7x, 256 devices: a whole 4x4x8 slice. The times are simulated.
256 devices in a mesh: row: 8 (over z), rep: 32 (over x, y, core).
Axes of the slice: x: 4, y: 4, z: 8, core: 2. Of those that a mesh axis runs over, the one named last changes fastest.
Arguments:
- feats: bfloat16 [131072, 128], P(('row', 'rep')), may hold values from -6 to 6
- w_self: bfloat16 [128, 256], replicated, may hold values from -0.5 to 0.5
- w_neigh: bfloat16 [128, 256], replicated, may hold values from -0.5 to 0.5
- bias: float32 [256], replicated, may hold values from -3 to 3
- tiles: bfloat16 [8, 32, 256, 128, 128], P('row', 'rep'), may hold values from 0 to 0.2
- tile_row: int32 [8, 32, 256], P('row', 'rep'), may hold values from 0 to 127
- tile_col: int32 [8, 32, 256], P('row', 'rep'), may hold values from 0 to 31
- tile_count: int32 [8, 32], P('row', 'rep'), may hold values from 64 to 256, as said below
- cotangent: bfloat16 [131072, 256], P(('row', 'rep')), may hold values from -6 to 6
Outputs:
- out: bfloat16 [131072, 256], P(('row', 'rep'))
- grad_feats: float32 [131072, 128], P(('row', 'rep'))
- grad_w_self: float32 [128, 256], replicated
- grad_w_neigh: float32 [128, 256], replicated
- grad_bias: float32 [256], replicated
Inputs may be any that keep to these rules, and one draw needn't show every extreme that they name: Tiles at or past tile_count of their device are ignored; on some device all 256 tiles are live.
All inputs are finite; a program needn't handle non-finite values.
Results may differ from a plain program's by a relative error of at most 0.025.
Values may be sent and summed in bfloat16 or wider, within the bound.
No kernel may reach another device: no remote copies, remote signals or barrier semaphores. Data moves between devices by JAX's collectives and lax.ppermute only.
A program may use at most 128 MiB of HBM per device.

v0:
```python
import jax
import jax.numpy as jnp
from jax import lax
from jax.experimental import pallas as pl
from jax.experimental.pallas import tpu as pltpu
from jax.sharding import PartitionSpec as P

T = 128
SLOTS = 256
CHUNK = 8
GROUP = 4
BF = jnp.bfloat16
F32 = jnp.float32
VMEM_LIMIT = 48 * 1024 * 1024

VM = pl.BlockSpec(memory_space=pltpu.VMEM)
SM = pl.BlockSpec(memory_space=pltpu.SMEM)
HB = pl.BlockSpec(memory_space=pl.ANY)


def shape(rows, cols, dtype):
    return jax.ShapeDtypeStruct((rows, cols), dtype)


def other_core(value):
    return lax.ppermute(value, "rep", [(i, i ^ 1) for i in range(32)])


def axis_move(value, which, k):
    return lax.ppermute(value, "rep", [(i, i ^ (k * (8 if i % 2 == which else 2))) for i in range(32)])


def row_move(value, step):
    return lax.ppermute(value, "row", [(i, (i + step) % 8) for i in range(8)])


def row_swap(value, bit):
    return lax.ppermute(value, "row", [(i, i ^ bit) for i in range(8)])


def tile_copy(tiles, tbuf, sem, i):
    part = pl.ds(pl.multiple_of(i * CHUNK, CHUNK), CHUNK)
    return pltpu.make_async_copy(tiles.at[part], tbuf.at[part], sem.at[i])


def start_tiles(count, tiles, tbuf, sem):
    chunks = (count[0] + CHUNK - 1) // CHUNK

    def start(i, carry):
        tile_copy(tiles, tbuf, sem, i).start()
        return carry

    lax.fori_loop(0, chunks, start, 0)
    return chunks


def zero(acc):
    def clear(i, carry):
        acc[i] = jnp.zeros((T, T), F32)
        return carry

    lax.fori_loop(0, acc.shape[0], clear, 0, unroll=4)


def add_products(chunks, tiles, tbuf, sem, product, place, acc):
    def step(i, carry):
        tile_copy(tiles, tbuf, sem, i).wait()
        for g in range(0, CHUNK, GROUP):
            slots = [i * CHUNK + g + k for k in range(GROUP)]
            prods = [product(t) for t in slots]
            for t, prod in zip(slots, prods):
                q = place[t]
                acc[q] = acc[q] + prod
        return carry

    lax.fori_loop(0, chunks, step, 0)


def forward_kernel(count, place, source, tiles, *rest):
    feats, outs = rest[:9], rest[9:17]
    tbuf, fbuf, acc, stage, tsem, fsem, osem = rest[17:]
    loads = []
    for d in range(8):
        if d == 4:
            loads.append(pltpu.make_async_copy(feats[4], fbuf.at[pl.ds(16, 2)], fsem.at[4]))
            loads.append(pltpu.make_async_copy(feats[8], fbuf.at[pl.ds(18, 2)], fsem.at[8]))
        else:
            loads.append(pltpu.make_async_copy(feats[d], fbuf.at[pl.ds(4 * d, 4)], fsem.at[d]))
    for load in loads:
        load.start()
    chunks = start_tiles(count, tiles, tbuf, tsem)
    zero(acc)
    for load in loads:
        load.wait()

    def product(t):
        return jnp.dot(tbuf[t], fbuf[source[t]], preferred_element_type=F32)

    add_products(chunks, tiles, tbuf, tsem, product, place, acc)
    stores = []
    for k in range(8):
        part = pl.ds(16 * k, 16)
        stage[part] = acc[part].astype(BF)
        stores.append(pltpu.make_async_copy(stage.at[part], outs[k], osem.at[k]))
        stores[-1].start()
    for store in stores:
        store.wait()


def forward(count, place, source, tiles, feats):
    blocks = [jax.ShapeDtypeStruct((16, T, T), BF)] * 8
    return pl.pallas_call(
        forward_kernel,
        out_shape=blocks,
        in_specs=[SM, SM, SM, HB] + [HB] * 9,
        out_specs=[HB] * 8,
        scratch_shapes=[
            pltpu.VMEM((SLOTS, T, T), BF),
            pltpu.VMEM((32, T, T), BF),
            pltpu.VMEM((129, T, T), F32),
            pltpu.VMEM((128, T, T), BF),
            pltpu.SemaphoreType.DMA((SLOTS // CHUNK,)),
            pltpu.SemaphoreType.DMA((9,)),
            pltpu.SemaphoreType.DMA((8,)),
        ],
        compiler_params=pltpu.CompilerParams(vmem_limit_bytes=VMEM_LIMIT),
        cost_estimate=pl.CostEstimate(flops=2 * SLOTS * T**3, bytes_accessed=16 * 2**20, transcendentals=0),
        name="tiles_forward",
    )(count, place, source, tiles, *feats)


def backward_kernel(count, place, source, tiles, *rest):
    grads, outs = rest[:8], rest[8:17]
    tbuf, gbuf, acc, stage, tsem, gsem, osem = rest[17:]
    loads = [
        pltpu.make_async_copy(grads[k].at[pl.ds(0, 16 * T)], gbuf.at[pl.ds(16 * T * k, 16 * T)], gsem.at[k])
        for k in range(8)
    ]
    for load in loads:
        load.start()
    chunks = start_tiles(count, tiles, tbuf, tsem)
    zero(acc)
    for load in loads:
        load.wait()

    def product(t):
        grad = gbuf[pl.ds(pl.multiple_of(source[t] * T, T), T)]
        return jnp.dot(grad, tbuf[t], preferred_element_type=F32)

    add_products(chunks, tiles, tbuf, tsem, product, place, acc)
    stores = [pltpu.make_async_copy(acc.at[pl.ds(0, 4)], outs[0], osem.at[0])]
    stores[0].start()
    for d in range(1, 8):
        stage[pl.ds(4 * d, 4)] = acc[pl.ds(4 * d, 4)].astype(BF)
        if d == 4:
            stores.append(pltpu.make_async_copy(stage.at[pl.ds(16, 2)], outs[4], osem.at[4]))
            stores.append(pltpu.make_async_copy(stage.at[pl.ds(18, 2)], outs[8], osem.at[8]))
            stores[-2].start()
        else:
            stores.append(pltpu.make_async_copy(stage.at[pl.ds(4 * d, 4)], outs[d], osem.at[d]))
        stores[-1].start()
    for store in stores:
        store.wait()


def backward(count, place, source, tiles, grads):
    four = jax.ShapeDtypeStruct((4, T, T), BF)
    two = jax.ShapeDtypeStruct((2, T, T), BF)
    outs = [jax.ShapeDtypeStruct((4, T, T), F32), four, four, four, two, four, four, four, two]
    return pl.pallas_call(
        backward_kernel,
        out_shape=outs,
        in_specs=[SM, SM, SM, HB] + [HB] * 8,
        out_specs=[HB] * 9,
        scratch_shapes=[
            pltpu.VMEM((SLOTS, T, T), BF),
            pltpu.VMEM((128 * T, T), BF),
            pltpu.VMEM((33, T, T), F32),
            pltpu.VMEM((32, T, T), BF),
            pltpu.SemaphoreType.DMA((SLOTS // CHUNK,)),
            pltpu.SemaphoreType.DMA((8,)),
            pltpu.SemaphoreType.DMA((9,)),
        ],
        compiler_params=pltpu.CompilerParams(vmem_limit_bytes=VMEM_LIMIT),
        cost_estimate=pl.CostEstimate(flops=2 * SLOTS * T**3, bytes_accessed=16 * 2**20, transcendentals=0),
        name="tiles_backward",
    )(count, place, source, tiles, *grads)


def layer_kernel(
    my_first, a0, a1, a2, a3, feats, w_self, w_neigh, bias, cot,
    out, base, dzn, pay1, pay2, pay3, own_w, gbuf,
):
    agg = (a0[...] + a1[...].astype(F32)) + (a2[...].astype(F32) + a3[...].astype(F32))
    agg = agg.astype(BF)
    x = feats[...]
    z = (
        jnp.dot(x, w_self[...], preferred_element_type=F32)
        + jnp.dot(agg, w_neigh[...], preferred_element_type=F32)
        + bias[...]
    )
    root = 0.7978845608028654
    t = jnp.tanh(root * (z + 0.044715 * (z * z * z)))
    cdf = 0.5 * (1.0 + t)
    out[...] = (z * cdf).astype(BF)
    slope = cdf + 0.5 * z * (1.0 - t * t) * (root * (1.0 + 3.0 * 0.044715 * (z * z)))
    dz = (cot[...].astype(F32) * slope).astype(BF)
    turned = lax.dot_general(w_neigh[...], dz, (((1,), (1,)), ((), ())), preferred_element_type=F32).astype(BF)
    for s in range(4):
        dzn[T * s : T * s + T] = turned[:, T * s : T * s + T]
    both = jnp.concatenate([x, agg], axis=1)
    grads = lax.dot_general(both, dz, (((0,), (0,)), ((), ())), preferred_element_type=F32)
    column = jnp.sum(dz.astype(F32), axis=0, keepdims=True)
    for y in range(4):
        gbuf[y, 0:64] = grads[64 * y : 64 * y + 64, 0:T].astype(BF)
        gbuf[y, 64:128] = grads[64 * y : 64 * y + 64, T : 2 * T].astype(BF)
    columns = jnp.concatenate([column[:, 0:T], column[:, T : 2 * T]], axis=0)
    high = columns.astype(BF)
    low = (columns - high.astype(F32)).astype(BF)
    tail = jnp.concatenate([high.astype(F32), low.astype(F32), jnp.zeros((12, T), F32)], axis=0).astype(BF)
    for k, pay in ((0, own_w), (1, pay1), (2, pay2), (3, pay3)):
        offset = 0
        if k:
            pay[0 : 4 * T] = dzn[...]
            offset = 4 * T
        pay[offset : offset + T] = gbuf[my_first[0] ^ k]
        pay[offset + T : offset + T + 16] = tail
    base[...] = lax.dot_general(dz, w_self[...], (((1,), (1,)), ((), ())), preferred_element_type=F32)


def layer(my_first, parts, feats, w_self, w_neigh, bias, cot):
    rows = feats.shape[0]
    pay = shape(rows + T + 16, T, BF)
    return pl.pallas_call(
        layer_kernel,
        out_shape=[shape(rows, 2 * T, BF), shape(rows, T, F32), shape(rows, T, BF), pay, pay, pay, shape(T + 16, T, BF)],
        in_specs=[SM] + [VM] * 9,
        out_specs=[VM] * 7,
        scratch_shapes=[pltpu.VMEM((4, T, T), BF)],
        compiler_params=pltpu.CompilerParams(vmem_limit_bytes=VMEM_LIMIT),
        name="layer",
    )(my_first, *parts, feats, w_self, w_neigh, bias, cot)


def weights_kernel(firsts, scale, *refs):
    chunks, (g_self, g_neigh, g_bias, mine, theirs) = refs[:8], refs[8:]
    for core, whole in ((0, mine), (1, theirs)):
        for k in range(4):
            c = chunks[4 * core + k]
            at = pl.ds(pl.multiple_of((firsts[core] ^ k) * 64, 64), 64)
            whole[at, 0:T] = c[0:64]
            whole[at, T : 2 * T] = c[64:128]
    total = (mine[...] + theirs[...]) * scale[0]
    g_self[...] = total[0:T]
    g_neigh[...] = total[T : 2 * T]
    a, b = chunks[0], chunks[4]
    g_bias[...] = ((a[T : T + 2] + a[T + 2 : T + 4]) + (b[T : T + 2] + b[T + 2 : T + 4])) * scale[0]


def weights(firsts, scale, chunks):
    return pl.pallas_call(
        weights_kernel,
        out_shape=[shape(T, 2 * T, F32), shape(T, 2 * T, F32), shape(2, T, F32)],
        in_specs=[SM, SM] + [VM] * 8,
        out_specs=[VM] * 3,
        scratch_shapes=[pltpu.VMEM((2 * T, 2 * T), F32)] * 2,
        name="weights",
    )(firsts, scale, *chunks)


def finish_kernel(base, p0, f1, b1, f2, b2, grad):
    for s in range(4):
        spread = (
            p0[s] + (f1[s].astype(F32) + b1[s].astype(F32)) + (f2[s].astype(F32) + b2[s].astype(F32))
        )
        grad[T * s : T * s + T] = base[T * s : T * s + T] + spread.T


def finish(base, p0, f1, b1, f2, b2):
    return pl.pallas_call(
        finish_kernel,
        out_shape=shape(base.shape[0], T, F32),
        in_specs=[VM] * 6,
        out_specs=VM,
        cost_estimate=pl.CostEstimate(flops=10**10, bytes_accessed=2**20, transcendentals=0),
        name="finish",
    )(base, p0, f1, b1, f2, b2)


def wide_sum(values):
    values = [value.astype(F32) for value in values]
    return (values[0] + values[1]) + (values[2] + values[3])


def per_device(feats, w_self, w_neigh, bias, tiles, tile_row, tile_col, tile_count, cotangent):
    rows_dev, width = feats.shape
    total_nodes = rows_dev * 256
    tiles = tiles.reshape(SLOTS, T, T)
    my_z = lax.axis_index("row")
    my_rep = lax.axis_index("rep")
    my_x, my_y, my_c = my_rep // 8, (my_rep // 2) % 4, my_rep % 2
    firsts = jnp.where(my_c == 0, jnp.stack([my_x, my_y]), jnp.stack([my_y, my_x]))
    count = tile_count.reshape(1)
    live = jnp.arange(SLOTS, dtype=jnp.int32) < count
    row = tile_row.reshape(SLOTS)
    col = tile_col.reshape(SLOTS)

    owner, sub = row // 4, row % 4
    kx, ky, kc = (owner // 8) ^ my_x, ((owner // 2) % 4) ^ my_y, (owner % 2) ^ my_c
    k1, k2 = jnp.where(owner % 2 == 0, kx, ky), jnp.where(owner % 2 == 0, ky, kx)
    slab_place = jnp.where(live, 64 * (1 - kc) + (k1 * 4 + k2) * 4 + sub, 128)
    slab_source = 64 * kc + (k2 * 4 + k1) * 4 + sub
    col_block = ((col // 4 - my_z) % 8) * 4 + col % 4
    section_place = jnp.where(live, col_block, 32)

    up2, down2 = row_move(feats, 2), row_move(feats, -2)
    up1, down1 = row_move(feats, 1), row_move(feats, -1)
    up4, down4 = row_move(up2[: rows_dev // 2], 2), row_move(down2[rows_dev // 2 :], -2)
    up3, down3 = row_move(up2, 1), row_move(down2, -1)
    blocks = [feats, down1, down2, down3, up4, up3, up2, up1, down4]
    blocks = [block.reshape(-1, T, T) for block in blocks]

    parts = forward(count, slab_place, col_block, tiles, blocks)
    both = [None] * 4
    for k in (2, 1, 3, 0):
        both[k] = parts[4 + k].astype(F32) + other_core(parts[k]).astype(F32)
    got = [axis_move(both[k].astype(BF), 0, k) for k in (2, 1, 3)]
    total = wide_sum([both[0]] + got)
    parts = [total[0:4]] + [axis_move(total[4 * k : 4 * k + 4].astype(BF), 1, k) for k in (1, 2, 3)]
    parts = [part.reshape(rows_dev, T) for part in parts]

    out, base, dzn, pay1, pay2, pay3, own_w = layer(
        firsts[:1], parts, feats, w_self, w_neigh, bias.reshape(1, -1), cotangent
    )

    got = [None] * 4
    for k, pay in ((2, pay2), (1, pay1), (3, pay3)):
        got[k] = axis_move(pay, 0, k)
    gw = wide_sum([own_w] + [got[k][rows_dev:] for k in (1, 2, 3)]).astype(BF)
    bundle = jnp.concatenate([dzn] + [got[k][:rows_dev] for k in (1, 2, 3)] + [gw], axis=0)
    own = [bundle, None, None, None]
    for k in (2, 1, 3):
        own[k] = axis_move(bundle, 1, k)
    far = [other_core(v) for v in own]
    gw = wide_sum([v[4 * rows_dev :] for v in own]).astype(BF)
    swapped = row_swap(gw, 1)

    p = backward(count, section_place, slab_source, tiles, own + far)
    gw, swapped, p = lax.optimization_barrier((gw, swapped, p))
    gw = (gw.astype(F32) + swapped.astype(F32)).astype(BF)
    up3, down3 = row_move(p[3], 1), row_move(p[5], -1)
    up4, down4 = row_move(p[4], 2), row_move(p[8], -2)
    swapped = row_swap(gw, 4)
    up3, down3, up4, down4, swapped, gw, p = lax.optimization_barrier((up3, down3, up4, down4, swapped, gw, p))
    zeros = jnp.zeros((2, T, T), F32)
    up2 = p[2].astype(F32) + up3.astype(F32) + jnp.concatenate([up4.astype(F32), zeros], axis=0)
    down2 = p[6].astype(F32) + down3.astype(F32) + jnp.concatenate([zeros, down4.astype(F32)], axis=0)
    up2, down2 = row_move(up2.astype(BF), 2), row_move(down2.astype(BF), -2)
    up1, down1 = row_move(p[1], 1), row_move(p[7], -1)
    grad_feats = finish(base, p[0], up1, down1, up2, down2)

    gw = (gw.astype(F32) + swapped.astype(F32)).astype(BF)
    gw = gw.astype(F32) + row_swap(gw, 2).astype(F32)
    quarters = [gw] + [axis_move(gw, 0, k) for k in (1, 2, 3)]
    quarters += [other_core(quarter) for quarter in quarters]
    scale = (1.0 / jnp.sqrt(jnp.float32(total_nodes))).reshape(1)
    grad_self, grad_neigh, grad_bias = weights(firsts, scale, quarters)
    return out, grad_feats, grad_self, grad_neigh, grad_bias.reshape(-1)


def solution(mesh):
    placed = (
        P(("row", "rep"), None),
        P(),
        P(),
        P(),
        P("row", "rep", None, None, None),
        P("row", "rep", None),
        P("row", "rep", None),
        P("row", "rep"),
        P(("row", "rep"), None),
    )
    return jax.shard_map(
        per_device,
        mesh=mesh,
        in_specs=placed,
        out_specs=(P(("row", "rep"), None), P(("row", "rep"), None), P(), P(), P()),
        check_vma=False,
    )
```

profile of v0, /device:TPU:32, one launch (start us, length us, event | category | flops | bytes accessed | tf_op | source)
XLA Modules:
  0.0 152.6 jit_solution(1887453798589567212)
XLA Ops:
  0.6 5.5 %collective-permute-start.1 = (bf16[512,128]{1,0:T(8,128)(2,1)}, bf16[512,128]{1,0:T(8,128)(2,1)S(1)}, u32[]{:S(2)}, u32[]{:S(2)}) collective-permute-start(bf16[512,128]{1,0:T(8,128)(2,1)} %feats.1), channel_id=1, source_target_pairs={{0,192},{32,224},{64,0},{96,32},{128,64},{160,96},{192,128},{224,1... | collective-permute-start | bytes 393224 | tf_op jit(solution)/shard_map/ppermute | solution.py:34
  6.1 1.1 collective-permute-start.6
  7.2 0.9 collective-permute-start
  8.8 0.7 add_add_fusion.1
  9.5 7.1 %collective-permute-done.3 = bf16[512,128]{1,0:T(8,128)(2,1)S(1)} collective-permute-done((bf16[512,128]{1,0:T(8,128)(2,1)}, bf16[512,128]{1,0:T(8,128)(2,1)S(1)}, u32[]{:S(2)}, u32[]{:S(2)}) %collective-permute-start.3) | collective-permute-done | bytes 131104 | tf_op jit(solution)/shard_map/ppermute | solution.py:34
  16.7 4.2 %collective-permute-start.7 = (bf16[256,128]{1,0:T(8,128)(2,1)S(1)}, bf16[256,128]{1,0:T(8,128)(2,1)S(1)}, u32[]{:S(2)}, u32[]{:S(2)}) collective-permute-start(bf16[256,128]{1,0:T(8,128)(2,1)S(1)} %slice.68), channel_id=1, source_target_pairs={{0,192},{32,224},{64,0},{96,32},{128,64},{160,96},{192,128},{224,1... | collective-permute-start | bytes 196616 | tf_op jit(solution)/shard_map/ppermute | solution.py:34
  20.9 1.1 collective-permute-start.2
  22.0 0.9 collective-permute-start.5
  22.9 0.7 fusion.5
  23.6 0.8 collective-permute-done.4
  24.4 1.4 collective-permute-done.2
  25.8 1.1 collective-permute-done.5
  27.0 0.9 copy-done
  27.9 10.9 %tiles_forward.1 = (bf16[16,128,128]{2,1,0:T(8,128)(2,1)S(1)}, bf16[16,128,128]{2,1,0:T(8,128)(2,1)S(1)}, bf16[16,128,128]{2,1,0:T(8,128)(2,1)S(1)}, bf16[16,128...) custom-call(s32[1]{0:T(128)} %bitcast.23.count, ...), custom_call_target="tpu_custom_call" | custom-call | flops 1073741824 | bytes 16777216 | tf_op jit(solution)/shard_map/tiles_forward/pallas_call | solution.py:112
  38.9 0.5 collective-permute-start.11
  39.5 0.4 collective-permute-start.8
  40.0 0.9 collective-permute-done.9
  40.8 0.1 add_convert_fusion.2
  41.0 3.6 %collective-permute-start.10 = (bf16[16,128,128]{2,1,0:T(8,128)(2,1)S(1)}, bf16[16,128,128]{2,1,0:T(8,128)(2,1)S(1)}, u32[]{:S(2)}, u32[]{:S(2)}) collective-permute-start(bf16[16,128,128]{2,1,0:T(8,128)(2,1)S(1)} %add_convert_fusion.2), channel_id=1, source_target_pairs={{0,16},{1,5},{2,18},{3,7},{4,20},{5,1},{6,22},{7,3},{8,24},{9,13},... | collective-permute-start | bytes 1572872 | tf_op jit(solution)/shard_map/ppermute | solution.py:30
  44.6 0.1 add_convert_fusion.1
  44.7 0.7 collective-permute-start.12
  45.4 0.1 add_convert_fusion
  45.6 0.6 collective-permute-start.14
  46.1 5.7 %collective-permute-done.10 = bf16[16,128,128]{2,1,0:T(8,128)(2,1)S(1)} collective-permute-done((bf16[16,128,128]{2,1,0:T(8,128)(2,1)S(1)}, bf16[16,128,128]{2,1,0:T(8,128)(2,1)S(1)}, u32[]{:S(2)}, u32[]{:S(2)}) %collective-permute-start.10) | collective-permute-done | bytes 524320 | tf_op jit(solution)/shard_map/ppermute | solution.py:30
  51.9 6.1 %collective-permute-done.12 = bf16[16,128,128]{2,1,0:T(8,128)(2,1)S(1)} collective-permute-done((bf16[16,128,128]{2,1,0:T(8,128)(2,1)S(1)}, bf16[16,128,128]{2,1,0:T(8,128)(2,1)S(1)}, u32[]{:S(2)}, u32[]{:S(2)}) %collective-permute-start.12) | collective-permute-done | bytes 524320 | tf_op jit(solution)/shard_map/ppermute | solution.py:30
  58.0 0.5 fusion.11
  58.5 0.8 collective-permute-start.15
  59.3 4.2 %collective-permute-start.16 = (bf16[4,128,128]{2,1,0:T(8,128)(2,1)S(1)}, bf16[4,128,128]{2,1,0:T(8,128)(2,1)S(1)}, u32[]{:S(2)}, u32[]{:S(2)}) collective-permute-start(bf16[4,128,128]{2,1,0:T(8,128)(2,1)S(1)} %get-tuple-element.113), channel_id=1, source_target_pairs={{0,4},{1,17},{2,6},{3,19},{4,0},{5,21},{6,2},{7,23},{8,12},{9,25},... | collective-permute-start | bytes 393224 | tf_op jit(solution)/shard_map/ppermute | solution.py:30
  63.6 0.1 collective-permute-done.15
  63.7 4.1 %collective-permute-done.16 = bf16[4,128,128]{2,1,0:T(8,128)(2,1)S(1)} collective-permute-done((bf16[4,128,128]{2,1,0:T(8,128)(2,1)S(1)}, bf16[4,128,128]{2,1,0:T(8,128)(2,1)S(1)}, u32[]{:S(2)}, u32[]{:S(2)}) %collective-permute-start.16) | collective-permute-done | bytes 131104 | tf_op jit(solution)/shard_map/ppermute | solution.py:30
  67.8 1.8 %collective-permute-done.17 = bf16[4,128,128]{2,1,0:T(8,128)(2,1)S(1)} collective-permute-done((bf16[4,128,128]{2,1,0:T(8,128)(2,1)S(1)}, bf16[4,128,128]{2,1,0:T(8,128)(2,1)S(1)}, u32[]{:S(2)}, u32[]{:S(2)}) %collective-permute-start.17) | collective-permute-done | bytes 131104 | tf_op jit(solution)/shard_map/ppermute | solution.py:30
  69.7 1.3 layer.1
  71.1 4.1 %collective-permute-start.19 = (bf16[656,128]{1,0:T(8,128)(2,1)S(1)}, bf16[656,128]{1,0:T(8,128)(2,1)S(1)}, u32[]{:S(2)}, u32[]{:S(2)}) collective-permute-start(bf16[656,128]{1,0:T(8,128)(2,1)S(1)} %get-tuple-element.66), channel_id=1, source_target_pairs={{0,16},{1,5},{2,18},{3,7},{4,20},{5,1},{6,22},{7,3},{8,24},{9,13},... | collective-permute-start | bytes 503816 | tf_op jit(solution)/shard_map/ppermute | solution.py:30
  75.2 0.6 collective-permute-start.20
  75.8 0.7 collective-permute-done.18
  76.4 3.9 %collective-permute-done.19 = bf16[656,128]{1,0:T(8,128)(2,1)S(1)} collective-permute-done((bf16[656,128]{1,0:T(8,128)(2,1)S(1)}, bf16[656,128]{1,0:T(8,128)(2,1)S(1)}, u32[]{:S(2)}, u32[]{:S(2)}) %collective-permute-start.19) | collective-permute-done | bytes 167968 | tf_op jit(solution)/shard_map/ppermute | solution.py:30
  80.3 1.7 %collective-permute-done.20 = bf16[656,128]{1,0:T(8,128)(2,1)S(1)} collective-permute-done((bf16[656,128]{1,0:T(8,128)(2,1)S(1)}, bf16[656,128]{1,0:T(8,128)(2,1)S(1)}, u32[]{:S(2)}, u32[]{:S(2)}) %collective-permute-start.20) | collective-permute-done | bytes 167968 | tf_op jit(solution)/shard_map/ppermute | solution.py:30
  82.3 2.0 %collective-permute-start.22 = (bf16[2192,128]{1,0:T(8,128)(2,1)S(1)}, bf16[2192,128]{1,0:T(8,128)(2,1)S(1)}, u32[]{:S(2)}, u32[]{:S(2)}) collective-permute-start(bf16[2192,128]{1,0:T(8,128)(2,1)S(1)} %get-tuple-element.108.rest_0_), channel_id=1, source_target_pairs={{0,4},{1,17},{2,6},{3,19},{4,0},{5,21},{6,2},{7,23},{8,12},{9,25},... | collective-permute-start | bytes 1683464 | tf_op jit(solution)/shard_map/ppermute | solution.py:30
  84.2 2.7 %collective-permute-start.23 = (bf16[2192,128]{1,0:T(8,128)(2,1)S(1)}, bf16[2192,128]{1,0:T(8,128)(2,1)S(1)}, u32[]{:S(2)}, u32[]{:S(2)}) collective-permute-start(bf16[2192,128]{1,0:T(8,128)(2,1)S(1)} %get-tuple-element.108.rest_0_), channel_id=1, source_target_pairs={{0,6},{1,25},{2,4},{3,27},{4,2},{5,29},{6,0},{7,31},{8,14},{9,17},... | collective-permute-start | bytes 1683464 | tf_op jit(solution)/shard_map/ppermute | solution.py:30
  86.9 4.9 %collective-permute-done.21.rest_1_ = bf16[2192,128]{1,0:T(8,128)(2,1)S(1)} collective-permute-done((bf16[2192,128]{1,0:T(8,128)(2,1)S(1)}, bf16[2192,128]{1,0:T(8,128)(2,1)S(1)}, u32[]{:S(2)}, u32[]{:S(2)}) %collective-permute-start.21) | collective-permute-done | bytes 561184 | tf_op jit(solution)/shard_map/ppermute | solution.py:30
  91.8 6.1 %collective-permute-done.22.rest_2_ = bf16[2192,128]{1,0:T(8,128)(2,1)S(1)} collective-permute-done((bf16[2192,128]{1,0:T(8,128)(2,1)S(1)}, bf16[2192,128]{1,0:T(8,128)(2,1)S(1)}, u32[]{:S(2)}, u32[]{:S(2)}) %collective-permute-start.22) | collective-permute-done | bytes 561184 | tf_op jit(solution)/shard_map/ppermute | solution.py:30
  97.9 3.1 %collective-permute-done.23.rest_3_ = bf16[2192,128]{1,0:T(8,128)(2,1)S(1)} collective-permute-done((bf16[2192,128]{1,0:T(8,128)(2,1)S(1)}, bf16[2192,128]{1,0:T(8,128)(2,1)S(1)}, u32[]{:S(2)}, u32[]{:S(2)}) %collective-permute-start.23) | collective-permute-done | bytes 561184 | tf_op jit(solution)/shard_map/ppermute | solution.py:30
  101.0 0.8 collective-permute-start.24
  101.8 1.1 collective-permute-done.28.rest_7_
  103.0 10.2 %tiles_backward.1 = (f32[4,128,128]{2,1,0:T(8,128)S(1)}, bf16[4,128,128]{2,1,0:T(8,128)(2,1)S(1)}, bf16[4,128,128]{2,1,0:T(8,128)(2,1)S(1)}, bf16[4,128,128]{2,1...) custom-call(s32[1]{0:T(128)} %bitcast.24.count, ...), custom_call_target="tpu_custom_call" | custom-call | flops 1073741824 | bytes 16777216 | tf_op jit(solution)/shard_map/tiles_backward/pallas_call | solution.py:170
  113.3 2.0 %collective-permute-start.30 = (bf16[4,128,128]{2,1,0:T(8,128)(2,1)S(1)}, bf16[4,128,128]{2,1,0:T(8,128)(2,1)S(1)}, u32[]{:S(2)}, u32[]{:S(2)}) collective-permute-start(bf16[4,128,128]{2,1,0:T(8,128)(2,1)S(1)} %get-tuple-element.79), channel_id=1, source_target_pairs={{0,224},{32,0},{64,32},{96,64},{128,96},{160,128},{192,160},{224,1... | collective-permute-start | bytes 393224 | tf_op jit(solution)/shard_map/ppermute | solution.py:34
  115.3 4.1 %collective-permute-start.32 = (bf16[2,128,128]{2,1,0:T(8,128)(2,1)S(1)}, bf16[2,128,128]{2,1,0:T(8,128)(2,1)S(1)}, u32[]{:S(2)}, u32[]{:S(2)}) collective-permute-start(bf16[2,128,128]{2,1,0:T(8,128)(2,1)S(1)} %get-tuple-element.81), channel_id=1, source_target_pairs={{0,192},{32,224},{64,0},{96,32},{128,64},{160,96},{192,128},{224,1... | collective-permute-start | bytes 196616 | tf_op jit(solution)/shard_map/ppermute | solution.py:34
  119.4 0.3 collective-permute-start.33
  119.8 7.9 %collective-permute-done.33 = bf16[144,128]{1,0:T(8,128)(2,1)S(1)} collective-permute-done((bf16[144,128]{1,0:T(8,128)(2,1)S(1)}, bf16[144,128]{1,0:T(8,128)(2,1)S(1)}, u32[]{:S(2)}, u32[]{:S(2)}) %collective-permute-start.33) | collective-permute-done | bytes 36896 | tf_op jit(solution)/shard_map/ppermute | solution.py:38
  127.9 1.3 collective-permute-start.37
  129.2 3.4 %collective-permute-done.38 = bf16[144,128]{1,0:T(8,128)(2,1)S(1)} collective-permute-done((bf16[144,128]{1,0:T(8,128)(2,1)S(1)}, bf16[144,128]{1,0:T(8,128)(2,1)S(1)}, u32[]{:S(2)}, u32[]{:S(2)}) %collective-permute-start.38) | collective-permute-done | bytes 36896 | tf_op jit(solution)/shard_map/ppermute | solution.py:38
  132.8 3.2 %collective-permute-start.40 = (f32[144,128]{1,0:T(8,128)S(1)}, f32[144,128]{1,0:T(8,128)S(1)}, u32[]{:S(2)}, u32[]{:S(2)}) collective-permute-start(f32[144,128]{1,0:T(8,128)S(1)} %convert_add_fusion.refs_0_), channel_id=1, source_target_pairs={{0,16},{1,5},{2,18},{3,7},{4,20},{5,1},{6,22},{7,3},{8,24},{9,13},... | collective-permute-start | bytes 221192 | tf_op jit(solution)/shard_map/ppermute | solution.py:30
  136.1 1.3 collective-permute-start.34
  137.4 2.6 %collective-permute-start.35 = (bf16[4,128,128]{2,1,0:T(8,128)(2,1)S(1)}, bf16[4,128,128]{2,1,0:T(8,128)(2,1)S(1)}, u32[]{:S(2)}, u32[]{:S(2)}) collective-permute-start(bf16[4,128,128]{2,1,0:T(8,128)(2,1)S(1)} %get-tuple-element.91), channel_id=1, source_target_pairs={{0,224},{32,0},{64,32},{96,64},{128,96},{160,128},{192,160},{224,1... | collective-permute-start | bytes 393224 | tf_op jit(solution)/shard_map/ppermute | solution.py:34
  140.0 1.9 %collective-permute-start.41 = (f32[144,128]{1,0:T(8,128)S(1)}, f32[144,128]{1,0:T(8,128)S(1)}, u32[]{:S(2)}, u32[]{:S(2)}) collective-permute-start(f32[144,128]{1,0:T(8,128)S(1)} %convert_add_fusion.refs_0_), channel_id=1, source_target_pairs={{0,24},{1,7},{2,26},{3,5},{4,28},{5,3},{6,30},{7,1},{8,16},{9,15},... | collective-permute-start | bytes 221192 | tf_op jit(solution)/shard_map/ppermute | solution.py:30
  141.9 3.7 %collective-permute-done.41.refs_3_ = f32[144,128]{1,0:T(8,128)S(1)} collective-permute-done((f32[144,128]{1,0:T(8,128)S(1)}, f32[144,128]{1,0:T(8,128)S(1)}, u32[]{:S(2)}, u32[]{:S(2)}) %collective-permute-start.41) | collective-permute-done | bytes 73760 | tf_op jit(solution)/shard_map/ppermute | solution.py:30
  145.6 0.5 collective-permute-start.43
  146.2 0.4 collective-permute-start.45
  146.6 0.1 copy-done.18
  146.9 0.4 copy-done.20
  147.3 2.0 %finish.1 = f32[512,128]{1,0:T(8,128)} custom-call(f32[512,128]{1,0:T(8,128)} %copy-done.7, f32[4,128,128]{2,1,0:T(8,128)} %copy-done.8, bf16[4,128,128]{2,1,0:T(8,128)(2,1)} %copy-done.19, bf16[4,128,128]{2,1,0:T(8,128)(2,1)} %copy-done.20, bf16[4,128,128]{2,1,0:T(8,128)(2,1)} %copy-done.18, bf16[4,128,128]{2,1,0:T(8,128)(2,1)} %copy-done.17), custom_call_target="tpu_custom_call" | custom-call | flops 10000000000 | bytes 1048576 | tf_op jit(solution)/shard_map/finish/pallas_call | solution.py:280
  149.4 0.6 copy-done.13
  150.1 0.6 copy-done.16
  150.7 1.9 %weights.1 = (f32[128,256]{1,0:T(8,128)}, f32[128,256]{1,0:T(8,128)}, f32[2,128]{1,0:T(2,128)}) custom-call(s32[2]{0:T(128)} %copy-done.5, f32[1]{0:T(128)} %constant.136.clone.1.scale, f32[144,128]{1,0:T(8,128)} %copy-done.9, f32[144,128]{1,0:T(8,128)} %copy-done.10, f32[144,128]{1,0:T(8,128)} %copy-done.11, f32[144,128]{1,0:T(8,128)} %copy-done.12, ...), custom_call_target="tpu_custom_call" | custom-call | tf_op jit(solution)/shard_map/weights/pallas_call | solution.py:261
  (97 shorter events, 1.5 us)
Async XLA Ops:
  0.6 16.0 %collective-permute-start.1 = (bf16[512,128]{1,0:T(8,128)(2,1)}, bf16[512,128]{1,0:T(8,128)(2,1)S(1)}, u32[]{:S(2)}, u32[]{:S(2)}) collective-permute-start(bf16[512,128]{1,0:T(8,128)(2,1)} %feats.1), channel_id=1, source_target_pairs={{0,192},{32,224},{64,0},{96,32},{128,64},{160,96},{192,128},{224,1... | collective-permute-start | bytes 393224 | tf_op jit(solution)/shard_map/ppermute | solution.py:34
  6.1 10.5 %collective-permute-start.3 = (bf16[512,128]{1,0:T(8,128)(2,1)}, bf16[512,128]{1,0:T(8,128)(2,1)S(1)}, u32[]{:S(2)}, u32[]{:S(2)}) collective-permute-start(bf16[512,128]{1,0:T(8,128)(2,1)} %feats.1), channel_id=1, source_target_pairs={{0,64},{32,96},{64,128},{96,160},{128,192},{160,224},{192,0},{224,... | collective-permute-start | bytes 393224 | tf_op jit(solution)/shard_map/ppermute | solution.py:34
  6.1 15.9 %collective-permute-start.6 = (bf16[512,128]{1,0:T(8,128)(2,1)}, bf16[512,128]{1,0:T(8,128)(2,1)S(1)}, u32[]{:S(2)}, u32[]{:S(2)}) collective-permute-start(bf16[512,128]{1,0:T(8,128)(2,1)} %feats.1), channel_id=1, source_target_pairs={{0,32},{32,64},{64,96},{96,128},{128,160},{160,192},{192,224},{224... | collective-permute-start | bytes 393224 | tf_op jit(solution)/shard_map/ppermute | solution.py:34
  7.2 16.4 %collective-permute-start = (bf16[512,128]{1,0:T(8,128)(2,1)}, bf16[512,128]{1,0:T(8,128)(2,1)S(1)}, u32[]{:S(2)}, u32[]{:S(2)}) collective-permute-start(bf16[512,128]{1,0:T(8,128)(2,1)} %feats.1), channel_id=1, source_target_pairs={{0,224},{32,0},{64,32},{96,64},{128,96},{160,128},{192,160},{224,1... | collective-permute-start | bytes 393224 | tf_op jit(solution)/shard_map/ppermute | solution.py:34
  16.6 7.8 %collective-permute-start.4 = (bf16[256,128]{1,0:T(8,128)(2,1)S(1)}, bf16[256,128]{1,0:T(8,128)(2,1)S(1)}, u32[]{:S(2)}, u32[]{:S(2)}) collective-permute-start(bf16[256,128]{1,0:T(8,128)(2,1)S(1)} %slice.67), channel_id=1, source_target_pairs={{0,64},{32,96},{64,128},{96,160},{128,192},{160,224},{192,0},{224,... | collective-permute-start | bytes 196616 | tf_op jit(solution)/shard_map/ppermute | solution.py:34
  16.7 7.7 %collective-permute-start.7 = (bf16[256,128]{1,0:T(8,128)(2,1)S(1)}, bf16[256,128]{1,0:T(8,128)(2,1)S(1)}, u32[]{:S(2)}, u32[]{:S(2)}) collective-permute-start(bf16[256,128]{1,0:T(8,128)(2,1)S(1)} %slice.68), channel_id=1, source_target_pairs={{0,192},{32,224},{64,0},{96,32},{128,64},{160,96},{192,128},{224,1... | collective-permute-start | bytes 196616 | tf_op jit(solution)/shard_map/ppermute | solution.py:34
  20.9 5.0 %collective-permute-start.2 = (bf16[512,128]{1,0:T(8,128)(2,1)S(1)}, bf16[512,128]{1,0:T(8,128)(2,1)S(1)}, u32[]{:S(2)}, u32[]{:S(2)}) collective-permute-start(bf16[512,128]{1,0:T(8,128)(2,1)S(1)} %collective-permute-done.1), channel_id=1, source_target_pairs={{0,224},{32,0},{64,32},{96,64},{128,96},{160,128},{192,160},{224,1... | collective-permute-start | bytes 393224 | tf_op jit(solution)/shard_map/ppermute | solution.py:34
  22.0 5.0 %collective-permute-start.5 = (bf16[512,128]{1,0:T(8,128)(2,1)S(1)}, bf16[512,128]{1,0:T(8,128)(2,1)S(1)}, u32[]{:S(2)}, u32[]{:S(2)}) collective-permute-start(bf16[512,128]{1,0:T(8,128)(2,1)S(1)} %collective-permute-done.3), channel_id=1, source_target_pairs={{0,32},{32,64},{64,96},{96,128},{128,160},{160,192},{192,224},{224... | collective-permute-start | bytes 393224 | tf_op jit(solution)/shard_map/ppermute | solution.py:34
  27.0 0.9 copy-start
  27.9 41.8 %copy-start.1 = (bf16[512,128]{1,0:T(8,128)(2,1)S(1)}, bf16[512,128]{1,0:T(8,128)(2,1)}, u32[]{:S(2)}) copy-start(bf16[512,128]{1,0:T(8,128)(2,1)} %feats.1) | copy-start | bytes 393220
  27.9 41.8 %copy-start.2 = (bf16[512,256]{1,0:T(8,128)(2,1)S(1)}, bf16[512,256]{1,0:T(8,128)(2,1)}, u32[]{:S(2)}) copy-start(bf16[512,256]{1,0:T(8,128)(2,1)} %cot.1) | copy-start | bytes 786436
  27.9 41.8 %copy-start.3 = (bf16[128,256]{1,0:T(8,128)(2,1)S(1)}, bf16[128,256]{1,0:T(8,128)(2,1)}, u32[]{:S(2)}) copy-start(bf16[128,256]{1,0:T(8,128)(2,1)} %w_self.1) | copy-start | bytes 196612
  27.9 41.8 %copy-start.4 = (bf16[128,256]{1,0:T(8,128)(2,1)S(1)}, bf16[128,256]{1,0:T(8,128)(2,1)}, u32[]{:S(2)}) copy-start(bf16[128,256]{1,0:T(8,128)(2,1)} %w_neigh.1) | copy-start | bytes 196612
  27.9 41.8 %copy-start.6 = (f32[256]{0:T(256)S(1)}, f32[256]{0:T(256)}, u32[]{:S(2)}) copy-start(f32[256]{0:T(256)} %param.12) | copy-start | bytes 3076
  38.8 2.0 %collective-permute-start.9 = (bf16[16,128,128]{2,1,0:T(8,128)(2,1)S(1)}, bf16[16,128,128]{2,1,0:T(8,128)(2,1)S(1)}, u32[]{:S(2)}, u32[]{:S(2)}) collective-permute-start(bf16[16,128,128]{2,1,0:T(8,128)(2,1)S(1)} %get-tuple-element.57), channel_id=1, source_target_pairs={{0,1},{1,0},{2,3},{3,2},{4,5},{5,4},{6,7},{7,6},{8,9},{9,8},{10,11... | collective-permute-start | bytes 1572872 | tf_op jit(solution)/shard_map/ppermute | solution.py:26
  38.9 5.6 %collective-permute-start.11 = (bf16[16,128,128]{2,1,0:T(8,128)(2,1)S(1)}, bf16[16,128,128]{2,1,0:T(8,128)(2,1)S(1)}, u32[]{:S(2)}, u32[]{:S(2)}) collective-permute-start(bf16[16,128,128]{2,1,0:T(8,128)(2,1)S(1)} %get-tuple-element.59), channel_id=1, source_target_pairs={{0,1},{1,0},{2,3},{3,2},{4,5},{5,4},{6,7},{7,6},{8,9},{9,8},{10,11... | collective-permute-start | bytes 1572872 | tf_op jit(solution)/shard_map/ppermute | solution.py:26
  39.4 6.0 %collective-permute-start.13 = (bf16[16,128,128]{2,1,0:T(8,128)(2,1)S(1)}, bf16[16,128,128]{2,1,0:T(8,128)(2,1)S(1)}, u32[]{:S(2)}, u32[]{:S(2)}) collective-permute-start(bf16[16,128,128]{2,1,0:T(8,128)(2,1)S(1)} %get-tuple-element.61), channel_id=1, source_target_pairs={{0,1},{1,0},{2,3},{3,2},{4,5},{5,4},{6,7},{7,6},{8,9},{9,8},{10,11... | collective-permute-start | bytes 1572872 | tf_op jit(solution)/shard_map/ppermute | solution.py:26
  39.5 6.6 %collective-permute-start.8 = (bf16[16,128,128]{2,1,0:T(8,128)(2,1)S(1)}, bf16[16,128,128]{2,1,0:T(8,128)(2,1)S(1)}, u32[]{:S(2)}, u32[]{:S(2)}) collective-permute-start(bf16[16,128,128]{2,1,0:T(8,128)(2,1)S(1)} %get-tuple-element.55), channel_id=1, source_target_pairs={{0,1},{1,0},{2,3},{3,2},{4,5},{5,4},{6,7},{7,6},{8,9},{9,8},{10,11... | collective-permute-start | bytes 1572872 | tf_op jit(solution)/shard_map/ppermute | solution.py:26
  41.0 10.9 %collective-permute-start.10 = (bf16[16,128,128]{2,1,0:T(8,128)(2,1)S(1)}, bf16[16,128,128]{2,1,0:T(8,128)(2,1)S(1)}, u32[]{:S(2)}, u32[]{:S(2)}) collective-permute-start(bf16[16,128,128]{2,1,0:T(8,128)(2,1)S(1)} %add_convert_fusion.2), channel_id=1, source_target_pairs={{0,16},{1,5},{2,18},{3,7},{4,20},{5,1},{6,22},{7,3},{8,24},{9,13},... | collective-permute-start | bytes 1572872 | tf_op jit(solution)/shard_map/ppermute | solution.py:30
  44.7 13.3 %collective-permute-start.12 = (bf16[16,128,128]{2,1,0:T(8,128)(2,1)S(1)}, bf16[16,128,128]{2,1,0:T(8,128)(2,1)S(1)}, u32[]{:S(2)}, u32[]{:S(2)}) collective-permute-start(bf16[16,128,128]{2,1,0:T(8,128)(2,1)S(1)} %add_convert_fusion.1), channel_id=1, source_target_pairs={{0,8},{1,3},{2,10},{3,1},{4,12},{5,7},{6,14},{7,5},{8,0},{9,11},{1... | collective-permute-start | bytes 1572872 | tf_op jit(solution)/shard_map/ppermute | solution.py:30
  45.6 12.4 %collective-permute-start.14 = (bf16[16,128,128]{2,1,0:T(8,128)(2,1)S(1)}, bf16[16,128,128]{2,1,0:T(8,128)(2,1)S(1)}, u32[]{:S(2)}, u32[]{:S(2)}) collective-permute-start(bf16[16,128,128]{2,1,0:T(8,128)(2,1)S(1)} %add_convert_fusion), channel_id=1, source_target_pairs={{0,24},{1,7},{2,26},{3,5},{4,28},{5,3},{6,30},{7,1},{8,16},{9,15},... | collective-permute-start | bytes 1572872 | tf_op jit(solution)/shard_map/ppermute | solution.py:30
  58.5 5.2 %collective-permute-start.15 = (bf16[4,128,128]{2,1,0:T(8,128)(2,1)S(1)}, bf16[4,128,128]{2,1,0:T(8,128)(2,1)S(1)}, u32[]{:S(2)}, u32[]{:S(2)}) collective-permute-start(bf16[4,128,128]{2,1,0:T(8,128)(2,1)S(1)} %get-tuple-element.114), channel_id=1, source_target_pairs={{0,2},{1,9},{2,0},{3,11},{4,6},{5,13},{6,4},{7,15},{8,10},{9,1},{1... | collective-permute-start | bytes 393224 | tf_op jit(solution)/shard_map/ppermute | solution.py:30
  59.3 8.6 %collective-permute-start.16 = (bf16[4,128,128]{2,1,0:T(8,128)(2,1)S(1)}, bf16[4,128,128]{2,1,0:T(8,128)(2,1)S(1)}, u32[]{:S(2)}, u32[]{:S(2)}) collective-permute-start(bf16[4,128,128]{2,1,0:T(8,128)(2,1)S(1)} %get-tuple-element.113), channel_id=1, source_target_pairs={{0,4},{1,17},{2,6},{3,19},{4,0},{5,21},{6,2},{7,23},{8,12},{9,25},... | collective-permute-start | bytes 393224 | tf_op jit(solution)/shard_map/ppermute | solution.py:30
  63.5 6.2 %collective-permute-start.17 = (bf16[4,128,128]{2,1,0:T(8,128)(2,1)S(1)}, bf16[4,128,128]{2,1,0:T(8,128)(2,1)S(1)}, u32[]{:S(2)}, u32[]{:S(2)}) collective-permute-start(bf16[4,128,128]{2,1,0:T(8,128)(2,1)S(1)} %get-tuple-element.112), channel_id=1, source_target_pairs={{0,6},{1,25},{2,4},{3,27},{4,2},{5,29},{6,0},{7,31},{8,14},{9,17},... | collective-permute-start | bytes 393224 | tf_op jit(solution)/shard_map/ppermute | solution.py:30
  63.6 69.1 %copy-start.5 = (s32[2]{0:T(128)}, s32[2]{0:T(128)S(1)}, u32[]{:S(2)}) copy-start(s32[2]{0:T(128)S(1)} %broadcast_select_fusion.firsts) | copy-start | bytes 28
  71.1 11.1 %copy-start.7 = (f32[512,128]{1,0:T(8,128)}, f32[512,128]{1,0:T(8,128)S(1)}, u32[]{:S(2)}) copy-start(f32[512,128]{1,0:T(8,128)S(1)} %get-tuple-element.63.base) | copy-start | bytes 786436
  71.1 5.4 %collective-permute-start.18 = (bf16[656,128]{1,0:T(8,128)(2,1)S(1)}, bf16[656,128]{1,0:T(8,128)(2,1)S(1)}, u32[]{:S(2)}, u32[]{:S(2)}) collective-permute-start(bf16[656,128]{1,0:T(8,128)(2,1)S(1)} %get-tuple-element.65), channel_id=1, source_target_pairs={{0,8},{1,3},{2,10},{3,1},{4,12},{5,7},{6,14},{7,5},{8,0},{9,11},{1... | collective-permute-start | bytes 503816 | tf_op jit(solution)/shard_map/ppermute | solution.py:30
  71.1 9.3 %collective-permute-start.19 = (bf16[656,128]{1,0:T(8,128)(2,1)S(1)}, bf16[656,128]{1,0:T(8,128)(2,1)S(1)}, u32[]{:S(2)}, u32[]{:S(2)}) collective-permute-start(bf16[656,128]{1,0:T(8,128)(2,1)S(1)} %get-tuple-element.66), channel_id=1, source_target_pairs={{0,16},{1,5},{2,18},{3,7},{4,20},{5,1},{6,22},{7,3},{8,24},{9,13},... | collective-permute-start | bytes 503816 | tf_op jit(solution)/shard_map/ppermute | solution.py:30
  75.2 6.9 %collective-permute-start.20 = (bf16[656,128]{1,0:T(8,128)(2,1)S(1)}, bf16[656,128]{1,0:T(8,128)(2,1)S(1)}, u32[]{:S(2)}, u32[]{:S(2)}) collective-permute-start(bf16[656,128]{1,0:T(8,128)(2,1)S(1)} %get-tuple-element.67), channel_id=1, source_target_pairs={{0,24},{1,7},{2,26},{3,5},{4,28},{5,3},{6,30},{7,1},{8,16},{9,15},... | collective-permute-start | bytes 503816 | tf_op jit(solution)/shard_map/ppermute | solution.py:30
  82.2 9.7 %collective-permute-start.21 = (bf16[2192,128]{1,0:T(8,128)(2,1)S(1)}, bf16[2192,128]{1,0:T(8,128)(2,1)S(1)}, u32[]{:S(2)}, u32[]{:S(2)}) collective-permute-start(bf16[2192,128]{1,0:T(8,128)(2,1)S(1)} %get-tuple-element.108.rest_0_), channel_id=1, source_target_pairs={{0,2},{1,9},{2,0},{3,11},{4,6},{5,13},{6,4},{7,15},{8,10},{9,1},{1... | collective-permute-start | bytes 1683464 | tf_op jit(solution)/shard_map/ppermute | solution.py:30
  82.3 15.6 %collective-permute-start.22 = (bf16[2192,128]{1,0:T(8,128)(2,1)S(1)}, bf16[2192,128]{1,0:T(8,128)(2,1)S(1)}, u32[]{:S(2)}, u32[]{:S(2)}) collective-permute-start(bf16[2192,128]{1,0:T(8,128)(2,1)S(1)} %get-tuple-element.108.rest_0_), channel_id=1, source_target_pairs={{0,4},{1,17},{2,6},{3,19},{4,0},{5,21},{6,2},{7,23},{8,12},{9,25},... | collective-permute-start | bytes 1683464 | tf_op jit(solution)/shard_map/ppermute | solution.py:30
  84.2 16.8 %collective-permute-start.23 = (bf16[2192,128]{1,0:T(8,128)(2,1)S(1)}, bf16[2192,128]{1,0:T(8,128)(2,1)S(1)}, u32[]{:S(2)}, u32[]{:S(2)}) collective-permute-start(bf16[2192,128]{1,0:T(8,128)(2,1)S(1)} %get-tuple-element.108.rest_0_), channel_id=1, source_target_pairs={{0,6},{1,25},{2,4},{3,27},{4,2},{5,29},{6,0},{7,31},{8,14},{9,17},... | collective-permute-start | bytes 1683464 | tf_op jit(solution)/shard_map/ppermute | solution.py:30
  86.9 14.9 %collective-permute-start.25 = (bf16[2192,128]{1,0:T(8,128)(2,1)S(1)}, bf16[2192,128]{1,0:T(8,128)(2,1)S(1)}, u32[]{:S(2)}, u32[]{:S(2)}) collective-permute-start(bf16[2192,128]{1,0:T(8,128)(2,1)S(1)} %get-tuple-element.108.rest_0_), channel_id=1, source_target_pairs={{0,1},{1,0},{2,3},{3,2},{4,5},{5,4},{6,7},{7,6},{8,9},{9,8},{10,11... | collective-permute-start | bytes 1683464 | tf_op jit(solution)/shard_map/ppermute | solution.py:26
  91.8 10.0 %collective-permute-start.26 = (bf16[2192,128]{1,0:T(8,128)(2,1)S(1)}, bf16[2192,128]{1,0:T(8,128)(2,1)S(1)}, u32[]{:S(2)}, u32[]{:S(2)}) collective-permute-start(bf16[2192,128]{1,0:T(8,128)(2,1)S(1)} %collective-permute-done.21.rest_1_), channel_id=1, source_target_pairs={{0,1},{1,0},{2,3},{3,2},{4,5},{5,4},{6,7},{7,6},{8,9},{9,8},{10,11... | collective-permute-start | bytes 1683464 | tf_op jit(solution)/shard_map/ppermute | solution.py:26
  97.9 3.9 %collective-permute-start.27 = (bf16[2192,128]{1,0:T(8,128)(2,1)S(1)}, bf16[2192,128]{1,0:T(8,128)(2,1)S(1)}, u32[]{:S(2)}, u32[]{:S(2)}) collective-permute-start(bf16[2192,128]{1,0:T(8,128)(2,1)S(1)} %collective-permute-done.22.rest_2_), channel_id=1, source_target_pairs={{0,1},{1,0},{2,3},{3,2},{4,5},{5,4},{6,7},{7,6},{8,9},{9,8},{10,11... | collective-permute-start | bytes 1683464 | tf_op jit(solution)/shard_map/ppermute | solution.py:26
  101.0 2.0 %collective-permute-start.28 = (bf16[2192,128]{1,0:T(8,128)(2,1)S(1)}, bf16[2192,128]{1,0:T(8,128)(2,1)S(1)}, u32[]{:S(2)}, u32[]{:S(2)}) collective-permute-start(bf16[2192,128]{1,0:T(8,128)(2,1)S(1)} %collective-permute-done.23.rest_3_), channel_id=1, source_target_pairs={{0,1},{1,0},{2,3},{3,2},{4,5},{5,4},{6,7},{7,6},{8,9},{9,8},{10,11... | collective-permute-start | bytes 1683464 | tf_op jit(solution)/shard_map/ppermute | solution.py:26
  101.0 12.1 %collective-permute-start.24 = (bf16[144,128]{1,0:T(8,128)(2,1)S(1)}, bf16[144,128]{1,0:T(8,128)(2,1)S(1)}, u32[]{:S(2)}, u32[]{:S(2)}) collective-permute-start(bf16[144,128]{1,0:T(8,128)(2,1)S(1)} %add_convert_fusion.7), channel_id=1, source_target_pairs={{0,32},{32,0},{64,96},{96,64},{128,160},{160,128},{192,224},{224,1... | collective-permute-start | bytes 110600 | tf_op jit(solution)/shard_map/ppermute | solution.py:38
  113.2 22.8 %copy-start.8 = (f32[4,128,128]{2,1,0:T(8,128)}, f32[4,128,128]{2,1,0:T(8,128)S(1)}, u32[]{:S(2)}) copy-start(f32[4,128,128]{2,1,0:T(8,128)S(1)} %get-tuple-element.89.p0) | copy-start | bytes 786436
  113.2 14.5 %collective-permute-start.29 = (bf16[4,128,128]{2,1,0:T(8,128)(2,1)S(1)}, bf16[4,128,128]{2,1,0:T(8,128)(2,1)S(1)}, u32[]{:S(2)}, u32[]{:S(2)}) collective-permute-start(bf16[4,128,128]{2,1,0:T(8,128)(2,1)S(1)} %get-tuple-element.78), channel_id=1, source_target_pairs={{0,32},{32,64},{64,96},{96,128},{128,160},{160,192},{192,224},{224... | collective-permute-start | bytes 393224 | tf_op jit(solution)/shard_map/ppermute | solution.py:34
  113.3 14.4 %collective-permute-start.30 = (bf16[4,128,128]{2,1,0:T(8,128)(2,1)S(1)}, bf16[4,128,128]{2,1,0:T(8,128)(2,1)S(1)}, u32[]{:S(2)}, u32[]{:S(2)}) collective-permute-start(bf16[4,128,128]{2,1,0:T(8,128)(2,1)S(1)} %get-tuple-element.79), channel_id=1, source_target_pairs={{0,224},{32,0},{64,32},{96,64},{128,96},{160,128},{192,160},{224,1... | collective-permute-start | bytes 393224 | tf_op jit(solution)/shard_map/ppermute | solution.py:34
  115.3 12.4 %collective-permute-start.31 = (bf16[2,128,128]{2,1,0:T(8,128)(2,1)S(1)}, bf16[2,128,128]{2,1,0:T(8,128)(2,1)S(1)}, u32[]{:S(2)}, u32[]{:S(2)}) collective-permute-start(bf16[2,128,128]{2,1,0:T(8,128)(2,1)S(1)} %get-tuple-element.80), channel_id=1, source_target_pairs={{0,64},{32,96},{64,128},{96,160},{128,192},{160,224},{192,0},{224,... | collective-permute-start | bytes 196616 | tf_op jit(solution)/shard_map/ppermute | solution.py:34
  115.3 12.4 %collective-permute-start.32 = (bf16[2,128,128]{2,1,0:T(8,128)(2,1)S(1)}, bf16[2,128,128]{2,1,0:T(8,128)(2,1)S(1)}, u32[]{:S(2)}, u32[]{:S(2)}) collective-permute-start(bf16[2,128,128]{2,1,0:T(8,128)(2,1)S(1)} %get-tuple-element.81), channel_id=1, source_target_pairs={{0,192},{32,224},{64,0},{96,32},{128,64},{160,96},{192,128},{224,1... | collective-permute-start | bytes 196616 | tf_op jit(solution)/shard_map/ppermute | solution.py:34
  119.4 8.2 %collective-permute-start.33 = (bf16[144,128]{1,0:T(8,128)(2,1)S(1)}, bf16[144,128]{1,0:T(8,128)(2,1)S(1)}, u32[]{:S(2)}, u32[]{:S(2)}) collective-permute-start(bf16[144,128]{1,0:T(8,128)(2,1)S(1)} %add_convert_fusion.6), channel_id=1, source_target_pairs={{0,128},{32,160},{64,192},{96,224},{128,0},{160,32},{192,64},{224,... | collective-permute-start | bytes 110600 | tf_op jit(solution)/shard_map/ppermute | solution.py:38
  127.7 4.9 %collective-permute-start.38 = (bf16[144,128]{1,0:T(8,128)(2,1)S(1)}, bf16[144,128]{1,0:T(8,128)(2,1)S(1)}, u32[]{:S(2)}, u32[]{:S(2)}) collective-permute-start(bf16[144,128]{1,0:T(8,128)(2,1)S(1)} %add_convert_fusion.5), channel_id=1, source_target_pairs={{0,64},{32,96},{64,0},{96,32},{128,192},{160,224},{192,128},{224,1... | collective-permute-start | bytes 110600 | tf_op jit(solution)/shard_map/ppermute | solution.py:38
  127.9 17.7 %collective-permute-start.37 = (bf16[4,128,128]{2,1,0:T(8,128)(2,1)S(1)}, bf16[4,128,128]{2,1,0:T(8,128)(2,1)S(1)}, u32[]{:S(2)}, u32[]{:S(2)}) collective-permute-start(bf16[4,128,128]{2,1,0:T(8,128)(2,1)S(1)} %add_convert_fusion.3), channel_id=1, source_target_pairs={{0,192},{32,224},{64,0},{96,32},{128,64},{160,96},{192,128},{224,1... | collective-permute-start | bytes 393224 | tf_op jit(solution)/shard_map/ppermute | solution.py:34
  132.7 16.7 %copy-start.9 = (f32[144,128]{1,0:T(8,128)}, f32[144,128]{1,0:T(8,128)S(1)}, u32[]{:S(2)}) copy-start(f32[144,128]{1,0:T(8,128)S(1)} %convert_add_fusion.refs_0_) | copy-start | bytes 221188
  132.7 4.7 %collective-permute-start.39 = (f32[144,128]{1,0:T(8,128)S(1)}, f32[144,128]{1,0:T(8,128)S(1)}, u32[]{:S(2)}, u32[]{:S(2)}) collective-permute-start(f32[144,128]{1,0:T(8,128)S(1)} %convert_add_fusion.refs_0_), channel_id=1, source_target_pairs={{0,8},{1,3},{2,10},{3,1},{4,12},{5,7},{6,14},{7,5},{8,0},{9,11},{1... | collective-permute-start | bytes 221192 | tf_op jit(solution)/shard_map/ppermute | solution.py:30
  132.8 7.2 %collective-permute-start.40 = (f32[144,128]{1,0:T(8,128)S(1)}, f32[144,128]{1,0:T(8,128)S(1)}, u32[]{:S(2)}, u32[]{:S(2)}) collective-permute-start(f32[144,128]{1,0:T(8,128)S(1)} %convert_add_fusion.refs_0_), channel_id=1, source_target_pairs={{0,16},{1,5},{2,18},{3,7},{4,20},{5,1},{6,22},{7,3},{8,24},{9,13},... | collective-permute-start | bytes 221192 | tf_op jit(solution)/shard_map/ppermute | solution.py:30
  136.0 10.1 %collective-permute-start.36 = (bf16[4,128,128]{2,1,0:T(8,128)(2,1)S(1)}, bf16[4,128,128]{2,1,0:T(8,128)(2,1)S(1)}, u32[]{:S(2)}, u32[]{:S(2)}) collective-permute-start(bf16[4,128,128]{2,1,0:T(8,128)(2,1)S(1)} %add_convert_fusion.4), channel_id=1, source_target_pairs={{0,64},{32,96},{64,128},{96,160},{128,192},{160,224},{192,0},{224,... | collective-permute-start | bytes 393224 | tf_op jit(solution)/shard_map/ppermute | solution.py:34
  136.1 10.1 %collective-permute-start.34 = (bf16[4,128,128]{2,1,0:T(8,128)(2,1)S(1)}, bf16[4,128,128]{2,1,0:T(8,128)(2,1)S(1)}, u32[]{:S(2)}, u32[]{:S(2)}) collective-permute-start(bf16[4,128,128]{2,1,0:T(8,128)(2,1)S(1)} %get-tuple-element.90), channel_id=1, source_target_pairs={{0,32},{32,64},{64,96},{96,128},{128,160},{160,192},{192,224},{224... | collective-permute-start | bytes 393224 | tf_op jit(solution)/shard_map/ppermute | solution.py:34
  137.4 12.0 %copy-start.10 = (f32[144,128]{1,0:T(8,128)}, f32[144,128]{1,0:T(8,128)S(1)}, u32[]{:S(2)}) copy-start(f32[144,128]{1,0:T(8,128)S(1)} %collective-permute-done.39.refs_1_) | copy-start | bytes 221188
  137.4 9.3 %collective-permute-start.35 = (bf16[4,128,128]{2,1,0:T(8,128)(2,1)S(1)}, bf16[4,128,128]{2,1,0:T(8,128)(2,1)S(1)}, u32[]{:S(2)}, u32[]{:S(2)}) collective-permute-start(bf16[4,128,128]{2,1,0:T(8,128)(2,1)S(1)} %get-tuple-element.91), channel_id=1, source_target_pairs={{0,224},{32,0},{64,32},{96,64},{128,96},{160,128},{192,160},{224,1... | collective-permute-start | bytes 393224 | tf_op jit(solution)/shard_map/ppermute | solution.py:34
  140.0 9.3 %copy-start.11 = (f32[144,128]{1,0:T(8,128)}, f32[144,128]{1,0:T(8,128)S(1)}, u32[]{:S(2)}) copy-start(f32[144,128]{1,0:T(8,128)S(1)} %collective-permute-done.40.refs_2_) | copy-start | bytes 221188
  140.0 5.6 %collective-permute-start.41 = (f32[144,128]{1,0:T(8,128)S(1)}, f32[144,128]{1,0:T(8,128)S(1)}, u32[]{:S(2)}, u32[]{:S(2)}) collective-permute-start(f32[144,128]{1,0:T(8,128)S(1)} %convert_add_fusion.refs_0_), channel_id=1, source_target_pairs={{0,24},{1,7},{2,26},{3,5},{4,28},{5,3},{6,30},{7,1},{8,16},{9,15},... | collective-permute-start | bytes 221192 | tf_op jit(solution)/shard_map/ppermute | solution.py:30
  145.6 3.8 %copy-start.12 = (f32[144,128]{1,0:T(8,128)}, f32[144,128]{1,0:T(8,128)S(1)}, u32[]{:S(2)}) copy-start(f32[144,128]{1,0:T(8,128)S(1)} %collective-permute-done.41.refs_3_) | copy-start | bytes 221188
  145.6 3.8 %collective-permute-start.42 = (f32[144,128]{1,0:T(8,128)S(1)}, f32[144,128]{1,0:T(8,128)S(1)}, u32[]{:S(2)}, u32[]{:S(2)}) collective-permute-start(f32[144,128]{1,0:T(8,128)S(1)} %convert_add_fusion.refs_0_), channel_id=1, source_target_pairs={{0,1},{1,0},{2,3},{3,2},{4,5},{5,4},{6,7},{7,6},{8,9},{9,8},{10,11... | collective-permute-start | bytes 221192 | tf_op jit(solution)/shard_map/ppermute | solution.py:26
  145.6 1.0 copy-start.17
  145.6 3.8 %collective-permute-start.43 = (f32[144,128]{1,0:T(8,128)S(1)}, f32[144,128]{1,0:T(8,128)S(1)}, u32[]{:S(2)}, u32[]{:S(2)}) collective-permute-start(f32[144,128]{1,0:T(8,128)S(1)} %collective-permute-done.39.refs_1_), channel_id=1, source_target_pairs={{0,1},{1,0},{2,3},{3,2},{4,5},{5,4},{6,7},{7,6},{8,9},{9,8},{10,11... | collective-permute-start | bytes 221192 | tf_op jit(solution)/shard_map/ppermute | solution.py:26
  146.1 0.7 copy-start.18
  146.1 3.3 %collective-permute-start.44 = (f32[144,128]{1,0:T(8,128)S(1)}, f32[144,128]{1,0:T(8,128)S(1)}, u32[]{:S(2)}, u32[]{:S(2)}) collective-permute-start(f32[144,128]{1,0:T(8,128)S(1)} %collective-permute-done.40.refs_2_), channel_id=1, source_target_pairs={{0,1},{1,0},{2,3},{3,2},{4,5},{5,4},{6,7},{7,6},{8,9},{9,8},{10,11... | collective-permute-start | bytes 221192 | tf_op jit(solution)/shard_map/ppermute | solution.py:26
  146.2 0.7 copy-start.19
  146.2 3.2 %collective-permute-start.45 = (f32[144,128]{1,0:T(8,128)S(1)}, f32[144,128]{1,0:T(8,128)S(1)}, u32[]{:S(2)}, u32[]{:S(2)}) collective-permute-start(f32[144,128]{1,0:T(8,128)S(1)} %collective-permute-done.41.refs_3_), channel_id=1, source_target_pairs={{0,1},{1,0},{2,3},{3,2},{4,5},{5,4},{6,7},{7,6},{8,9},{9,8},{10,11... | collective-permute-start | bytes 221192 | tf_op jit(solution)/shard_map/ppermute | solution.py:26
  146.6 0.7 copy-start.20
  149.4 0.7 copy-start.15
  (3 other events, 1.9 us)
where the time goes:
time: 155 us; the launch traced here: 153 us
  waiting for transfers between devices  65.8 us (42%)
  starting transfers between devices  53.1 us (34%)
  Pallas kernels  26.4 us (17%)
  local copies, waits for them, and re-layouts  3.01 us (2%)
  other arithmetic  2.6 us (2%)
  between operations  1.69 us (1%)
    ppermute x15, waiting for transfers between devices, axis_move(): lax.ppermute(value, 'rep', [(i, i ^ k * (8 if i % 2 == which else 2)) for...  41.9 us
    ppermute x16, starting transfers between devices, row_move(): return lax.ppermute(value, 'row', [(i, (i + step) % 8) for i in range(8)])  25.3 us
    ppermute x15, starting transfers between devices, axis_move(): lax.ppermute(value, 'rep', [(i, i ^ k * (8 if i % 2 == which else 2)) for...  24.4 us
    ppermute x3, waiting for transfers between devices, row_swap(): return lax.ppermute(value, 'row', [(i, i ^ bit) for i in range(8)])  11.3 us
    pallas_call x1, Pallas kernels, forward(): pl.pallas_call(forward_kernel, out_shape=blocks, in_specs=[SM, SM, SM, HB...  10.9 us
    ppermute x16, waiting for transfers between devices, row_move(): return lax.ppermute(value, 'row', [(i, (i + step) % 8) for i in range(8)])  10.5 us
    pallas_call x1, Pallas kernels, backward(): pl.pallas_call(backward_kernel, out_shape=outs, in_specs=[SM, SM, SM, HB]...  10.2 us
  transfers between devices with their start and end apart: 46, of which 20 were waited for; matrix products, arithmetic and copies ran while one was open for 1% of the time, Pallas kernels for 8%

commit v1 on v0

--- a/solution.py
+++ b/solution.py
@@ -9,6 +9,7 @@
 SLOTS = 256
 CHUNK = 8
 GROUP = 4
+HALF = 2 * T + 16
 BF = jnp.bfloat16
 F32 = jnp.float32
 VMEM_LIMIT = 48 * 1024 * 1024
@@ -187,10 +188,7 @@
     )(count, place, source, tiles, *grads)
 
 
-def layer_kernel(
-    my_first, a0, a1, a2, a3, feats, w_self, w_neigh, bias, cot,
-    out, base, dzn, pay1, pay2, pay3, own_w, gbuf,
-):
+def layer_kernel(core, a0, a1, a2, a3, feats, w_self, w_neigh, bias, cot, out, base, dzn, keep, give, halves):
     agg = (a0[...] + a1[...].astype(F32)) + (a2[...].astype(F32) + a3[...].astype(F32))
     agg = agg.astype(BF)
     x = feats[...]
@@ -209,82 +207,59 @@
     for s in range(4):
         dzn[T * s : T * s + T] = turned[:, T * s : T * s + T]
     both = jnp.concatenate([x, agg], axis=1)
-    grads = lax.dot_general(both, dz, (((0,), (0,)), ((), ())), preferred_element_type=F32)
+    grads = lax.dot_general(both, dz, (((0,), (0,)), ((), ())), preferred_element_type=F32).astype(BF)
     column = jnp.sum(dz.astype(F32), axis=0, keepdims=True)
-    for y in range(4):
-        gbuf[y, 0:64] = grads[64 * y : 64 * y + 64, 0:T].astype(BF)
-        gbuf[y, 64:128] = grads[64 * y : 64 * y + 64, T : 2 * T].astype(BF)
     columns = jnp.concatenate([column[:, 0:T], column[:, T : 2 * T]], axis=0)
-    high = columns.astype(BF)
-    low = (columns - high.astype(F32)).astype(BF)
-    tail = jnp.concatenate([high.astype(F32), low.astype(F32), jnp.zeros((12, T), F32)], axis=0).astype(BF)
-    for k, pay in ((0, own_w), (1, pay1), (2, pay2), (3, pay3)):
-        offset = 0
-        if k:
-            pay[0 : 4 * T] = dzn[...]
-            offset = 4 * T
-        pay[offset : offset + T] = gbuf[my_first[0] ^ k]
-        pay[offset + T : offset + T + 16] = tail
+    high = columns.astype(BF).astype(F32)
+    tail = jnp.concatenate([high, columns - high, jnp.zeros((12, T), F32)], axis=0).astype(BF)
+    for m in range(2):
+        halves[m, 0:T] = grads[T * m : T * m + T, 0:T]
+        halves[m, T : 2 * T] = grads[T * m : T * m + T, T : 2 * T]
+        halves[m, 2 * T : HALF] = tail
+    keep[...] = halves[core[0]]
+    give[...] = halves[1 - core[0]]
     base[...] = lax.dot_general(dz, w_self[...], (((1,), (1,)), ((), ())), preferred_element_type=F32)
 
 
-def layer(my_first, parts, feats, w_self, w_neigh, bias, cot):
+def layer(core, parts, feats, w_self, w_neigh, bias, cot):
     rows = feats.shape[0]
-    pay = shape(rows + T + 16, T, BF)
+    half = shape(HALF, T, BF)
     return pl.pallas_call(
         layer_kernel,
-        out_shape=[shape(rows, 2 * T, BF), shape(rows, T, F32), shape(rows, T, BF), pay, pay, pay, shape(T + 16, T, BF)],
+        out_shape=[shape(rows, 2 * T, BF), shape(rows, T, F32), shape(rows, T, BF), half, half],
         in_specs=[SM] + [VM] * 9,
-        out_specs=[VM] * 7,
-        scratch_shapes=[pltpu.VMEM((4, T, T), BF)],
+        out_specs=[VM] * 5,
+        scratch_shapes=[pltpu.VMEM((2, HALF, T), BF)],
         compiler_params=pltpu.CompilerParams(vmem_limit_bytes=VMEM_LIMIT),
         name="layer",
-    )(my_first, *parts, feats, w_self, w_neigh, bias, cot)
-
-
-def weights_kernel(firsts, scale, *refs):
-    chunks, (g_self, g_neigh, g_bias, mine, theirs) = refs[:8], refs[8:]
-    for core, whole in ((0, mine), (1, theirs)):
-        for k in range(4):
-            c = chunks[4 * core + k]
-            at = pl.ds(pl.multiple_of((firsts[core] ^ k) * 64, 64), 64)
-            whole[at, 0:T] = c[0:64]
-            whole[at, T : 2 * T] = c[64:128]
-    total = (mine[...] + theirs[...]) * scale[0]
-    g_self[...] = total[0:T]
-    g_neigh[...] = total[T : 2 * T]
-    a, b = chunks[0], chunks[4]
-    g_bias[...] = ((a[T : T + 2] + a[T + 2 : T + 4]) + (b[T : T + 2] + b[T + 2 : T + 4])) * scale[0]
-
-
-def weights(firsts, scale, chunks):
-    return pl.pallas_call(
-        weights_kernel,
-        out_shape=[shape(T, 2 * T, F32), shape(T, 2 * T, F32), shape(2, T, F32)],
-        in_specs=[SM, SM] + [VM] * 8,
-        out_specs=[VM] * 3,
-        scratch_shapes=[pltpu.VMEM((2 * T, 2 * T), F32)] * 2,
-        name="weights",
-    )(firsts, scale, *chunks)
-
-
-def finish_kernel(base, p0, f1, b1, f2, b2, grad):
+    )(core, *parts, feats, w_self, w_neigh, bias, cot)
+
+
+def finish_kernel(core, scale, base, p0, f1, b1, f2, b2, mine, theirs, grad, g_self, g_neigh, g_bias):
     for s in range(4):
         spread = (
             p0[s] + (f1[s].astype(F32) + b1[s].astype(F32)) + (f2[s].astype(F32) + b2[s].astype(F32))
         )
         grad[T * s : T * s + T] = base[T * s : T * s + T] + spread.T
-
-
-def finish(base, p0, f1, b1, f2, b2):
+    first = core[0] == 0
+    own, other = mine[...] * scale[0], theirs[...] * scale[0]
+    low, high = jnp.where(first, own, other), jnp.where(first, other, own)
+    for g, part in ((g_self, low), (g_neigh, high)):
+        g[:, 0:T] = part[0:T]
+        g[:, T : 2 * T] = part[T : 2 * T]
+    g_bias[...] = low[2 * T : 2 * T + 2] + low[2 * T + 2 : 2 * T + 4]
+
+
+def finish(core, scale, base, p0, f1, b1, f2, b2, mine, theirs):
     return pl.pallas_call(
         finish_kernel,
-        out_shape=shape(base.shape[0], T, F32),
-        in_specs=[VM] * 6,
-        out_specs=VM,
-        cost_estimate=pl.CostEstimate(flops=10**10, bytes_accessed=2**20, transcendentals=0),
+        out_shape=[
+            shape(base.shape[0], T, F32), shape(T, 2 * T, F32), shape(T, 2 * T, F32), shape(2, T, F32)
+        ],
+        in_specs=[SM, SM] + [VM] * 8,
+        out_specs=[VM] * 4,
         name="finish",
-    )(base, p0, f1, b1, f2, b2)
+    )(core, scale, base, p0, f1, b1, f2, b2, mine, theirs)
 
 
 def wide_sum(values):
@@ -299,7 +274,6 @@
     my_z = lax.axis_index("row")
     my_rep = lax.axis_index("rep")
     my_x, my_y, my_c = my_rep // 8, (my_rep // 2) % 4, my_rep % 2
-    firsts = jnp.where(my_c == 0, jnp.stack([my_x, my_y]), jnp.stack([my_y, my_x]))
     count = tile_count.reshape(1)
     live = jnp.arange(SLOTS, dtype=jnp.int32) < count
     row = tile_row.reshape(SLOTS)
@@ -329,42 +303,40 @@
     parts = [total[0:4]] + [axis_move(total[4 * k : 4 * k + 4].astype(BF), 1, k) for k in (1, 2, 3)]
     parts = [part.reshape(rows_dev, T) for part in parts]
 
-    out, base, dzn, pay1, pay2, pay3, own_w = layer(
-        firsts[:1], parts, feats, w_self, w_neigh, bias.reshape(1, -1), cotangent
-    )
-
-    got = [None] * 4
-    for k, pay in ((2, pay2), (1, pay1), (3, pay3)):
+    core = my_c.reshape(1)
+    out, base, dzn, keep, give = layer(core, parts, feats, w_self, w_neigh, bias.reshape(1, -1), cotangent)
+
+    half = (keep.astype(F32) + other_core(give).astype(F32)).astype(BF)
+    pay = jnp.concatenate([dzn, half], axis=0)
+    got = [pay, None, None, None]
+    for k in (2, 1, 3):
         got[k] = axis_move(pay, 0, k)
-    gw = wide_sum([own_w] + [got[k][rows_dev:] for k in (1, 2, 3)]).astype(BF)
-    bundle = jnp.concatenate([dzn] + [got[k][:rows_dev] for k in (1, 2, 3)] + [gw], axis=0)
+    gw = wide_sum([v[rows_dev:] for v in got]).astype(BF)
+    bundle = jnp.concatenate([v[:rows_dev] for v in got] + [gw], axis=0)
     own = [bundle, None, None, None]
     for k in (2, 1, 3):
         own[k] = axis_move(bundle, 1, k)
     far = [other_core(v) for v in own]
     gw = wide_sum([v[4 * rows_dev :] for v in own]).astype(BF)
-    swapped = row_swap(gw, 1)
+    swapped = [row_swap(gw, bits) for bits in (1, 4, 5)]
 
     p = backward(count, section_place, slab_source, tiles, own + far)
     gw, swapped, p = lax.optimization_barrier((gw, swapped, p))
-    gw = (gw.astype(F32) + swapped.astype(F32)).astype(BF)
+    gw = wide_sum([gw] + swapped).astype(BF)
     up3, down3 = row_move(p[3], 1), row_move(p[5], -1)
     up4, down4 = row_move(p[4], 2), row_move(p[8], -2)
-    swapped = row_swap(gw, 4)
-    up3, down3, up4, down4, swapped, gw, p = lax.optimization_barrier((up3, down3, up4, down4, swapped, gw, p))
+    swapped = row_swap(gw, 2)
+    up3, down3, up4, down4, p = lax.optimization_barrier((up3, down3, up4, down4, p))
     zeros = jnp.zeros((2, T, T), F32)
     up2 = p[2].astype(F32) + up3.astype(F32) + jnp.concatenate([up4.astype(F32), zeros], axis=0)
     down2 = p[6].astype(F32) + down3.astype(F32) + jnp.concatenate([zeros, down4.astype(F32)], axis=0)
     up2, down2 = row_move(up2.astype(BF), 2), row_move(down2.astype(BF), -2)
     up1, down1 = row_move(p[1], 1), row_move(p[7], -1)
-    grad_feats = finish(base, p[0], up1, down1, up2, down2)
-
-    gw = (gw.astype(F32) + swapped.astype(F32)).astype(BF)
-    gw = gw.astype(F32) + row_swap(gw, 2).astype(F32)
-    quarters = [gw] + [axis_move(gw, 0, k) for k in (1, 2, 3)]
-    quarters += [other_core(quarter) for quarter in quarters]
+    gw = gw.astype(F32) + swapped.astype(F32)
     scale = (1.0 / jnp.sqrt(jnp.float32(total_nodes))).reshape(1)
-    grad_self, grad_neigh, grad_bias = weights(firsts, scale, quarters)
+    grad_feats, grad_self, grad_neigh, grad_bias = finish(
+        core, scale, base, p[0], up1, down1, up2, down2, gw, other_core(gw)
+    )
     return out, grad_feats, grad_self, grad_neigh, grad_bias.reshape(-1)
 
 

time: 155 us -> 149 us (0.961)
  waiting for transfers between devices: 65.8 us -> 57.9 us
  starting transfers between devices: 53.1 us -> 60 us
  Pallas kernels: 26.4 us -> 23.1 us
    ppermute x3 -> x4, waiting for transfers between devices: 11.3 us -> 0.01 us  [row_swap(): return lax.ppermute(value, 'row', [(i, i ^ bit) for i in range(8)])]
    ppermute x3 -> x4, starting transfers between devices: 1.21 us -> 12.4 us  [row_swap(): return lax.ppermute(value, 'row', [(i, i ^ bit) for i in range(8)])]
    ppermute x16, waiting for transfers between devices: 10.5 us -> 17.5 us  [row_move(): return lax.ppermute(value, 'row', [(i, (i + step) % 8) for i in range(8)])]
    ppermute x15 -> x12, waiting for transfers between devices: 41.9 us -> 38.2 us  [axis_move(): lax.ppermute(value, 'rep', [(i, i ^ k * (8 if i % 2 == which else 2)) for...]
    ppermute x15 -> x12, starting transfers between devices: 24.4 us -> 21.3 us  [axis_move(): lax.ppermute(value, 'rep', [(i, i ^ k * (8 if i % 2 == which else 2)) for...]
    pallas_call x2 -> x1, Pallas kernels: 3.95 us -> 2.2 us  [finish(): pl.pallas_call(finish_kernel, out_shape=[shape(base.shape[0], T, F32), sh...]
  transfers between devices with their start and end apart: 46 -> 42, of which waited for: 20 -> 21; matrix products, arithmetic and copies ran while one was open for 1% -> 1% of each run, Pallas kernels for 8% -> 6%
where the time goes in v1:
time: 149 us; the launch traced here: 148 us
  starting transfers between devices  60 us (40%)
  waiting for transfers between devices  57.9 us (39%)
  Pallas kernels  23.1 us (16%)
  other arithmetic  2.62 us (2%)
  local copies, waits for them, and re-layouts  2.49 us (2%)
  between operations  1.62 us (1%)
    ppermute x12, waiting for transfers between devices, axis_move(): lax.ppermute(value, 'rep', [(i, i ^ k * (8 if i % 2 == which else 2)) for...  38.2 us
    ppermute x16, starting transfers between devices, row_move(): return lax.ppermute(value, 'row', [(i, (i + step) % 8) for i in range(8)])  25.1 us
    ppermute x12, starting transfers between devices, axis_move(): lax.ppermute(value, 'rep', [(i, i ^ k * (8 if i % 2 == which else 2)) for...  21.3 us
    ppermute x16, waiting for transfers between devices, row_move(): return lax.ppermute(value, 'row', [(i, (i + step) % 8) for i in range(8)])  17.5 us
    ppermute x4, starting transfers between devices, row_swap(): return lax.ppermute(value, 'row', [(i, i ^ bit) for i in range(8)])  12.4 us
    pallas_call x1, Pallas kernels, forward(): pl.pallas_call(forward_kernel, out_shape=blocks, in_specs=[SM, SM, SM, HB...  10 us
    pallas_call x1, Pallas kernels, backward(): pl.pallas_call(backward_kernel, out_shape=outs, in_specs=[SM, SM, SM, HB]...  9.43 us
  transfers between devices with their start and end apart: 42, of which 21 were waited for; matrix products, arithmetic and copies ran while one was open for 1% of the time, Pallas kernels for 6%

profile of v1, /device:TPU:32, one launch (start us, length us, event | category | flops | bytes accessed | tf_op | source)
XLA Modules:
  0.0 147.8 jit_solution(8999778957153933656)
XLA Ops:
  0.6 3.3 %collective-permute-start.3 = (bf16[512,128]{1,0:T(8,128)(2,1)}, bf16[512,128]{1,0:T(8,128)(2,1)S(1)}, u32[]{:S(2)}, u32[]{:S(2)}) collective-permute-start(bf16[512,128]{1,0:T(8,128)(2,1)} %feats.1), channel_id=1, source_target_pairs={{0,64},{32,96},{64,128},{96,160},{128,192},{160,224},{192,0},{224,... | collective-permute-start | bytes 393224 | tf_op jit(solution)/shard_map/ppermute | solution.py:35
  4.0 2.2 %collective-permute-start.1 = (bf16[512,128]{1,0:T(8,128)(2,1)}, bf16[512,128]{1,0:T(8,128)(2,1)S(1)}, u32[]{:S(2)}, u32[]{:S(2)}) collective-permute-start(bf16[512,128]{1,0:T(8,128)(2,1)} %feats.1), channel_id=1, source_target_pairs={{0,192},{32,224},{64,0},{96,32},{128,64},{160,96},{192,128},{224,1... | collective-permute-start | bytes 393224 | tf_op jit(solution)/shard_map/ppermute | solution.py:35
  6.2 0.9 collective-permute-start.6
  7.1 1.1 collective-permute-start
  8.9 0.7 add_add_fusion.1
  9.6 3.5 %collective-permute-done.3 = bf16[512,128]{1,0:T(8,128)(2,1)S(1)} collective-permute-done((bf16[512,128]{1,0:T(8,128)(2,1)}, bf16[512,128]{1,0:T(8,128)(2,1)S(1)}, u32[]{:S(2)}, u32[]{:S(2)}) %collective-permute-start.3) | collective-permute-done | bytes 131104 | tf_op jit(solution)/shard_map/ppermute | solution.py:35
  13.2 4.2 %collective-permute-start.7 = (bf16[256,128]{1,0:T(8,128)(2,1)S(1)}, bf16[256,128]{1,0:T(8,128)(2,1)S(1)}, u32[]{:S(2)}, u32[]{:S(2)}) collective-permute-start(bf16[256,128]{1,0:T(8,128)(2,1)S(1)} %slice.64), channel_id=1, source_target_pairs={{0,192},{32,224},{64,0},{96,32},{128,64},{160,96},{192,128},{224,1... | collective-permute-start | bytes 196616 | tf_op jit(solution)/shard_map/ppermute | solution.py:35
  17.4 0.8 collective-permute-start.5
  18.2 1.2 collective-permute-start.2
  19.4 0.7 fusion.5
  20.1 0.2 collective-permute-done.7
  20.3 2.0 %collective-permute-done.5 = bf16[512,128]{1,0:T(8,128)(2,1)S(1)} collective-permute-done((bf16[512,128]{1,0:T(8,128)(2,1)S(1)}, bf16[512,128]{1,0:T(8,128)(2,1)S(1)}, u32[]{:S(2)}, u32[]{:S(2)}) %collective-permute-start.5) | collective-permute-done | bytes 131104 | tf_op jit(solution)/shard_map/ppermute | solution.py:35
  22.3 1.1 collective-permute-done.2
  23.4 0.9 copy-done
  24.3 10.0 %tiles_forward.1 = (bf16[16,128,128]{2,1,0:T(8,128)(2,1)S(1)}, bf16[16,128,128]{2,1,0:T(8,128)(2,1)S(1)}, bf16[16,128,128]{2,1,0:T(8,128)(2,1)S(1)}, bf16[16,128...) custom-call(s32[1]{0:T(128)} %bitcast.21.count, ...), custom_call_target="tpu_custom_call" | custom-call | flops 1073741824 | bytes 16777216 | tf_op jit(solution)/shard_map/tiles_forward/pallas_call | solution.py:113
  34.4 0.5 collective-permute-start.11
  34.9 0.1 collective-permute-start.13
  35.0 0.4 collective-permute-start.8
  35.5 0.9 collective-permute-done.9
  36.3 0.1 add_convert_fusion.2
  36.5 3.8 %collective-permute-start.10 = (bf16[16,128,128]{2,1,0:T(8,128)(2,1)S(1)}, bf16[16,128,128]{2,1,0:T(8,128)(2,1)S(1)}, u32[]{:S(2)}, u32[]{:S(2)}) collective-permute-start(bf16[16,128,128]{2,1,0:T(8,128)(2,1)S(1)} %add_convert_fusion.2), channel_id=1, source_target_pairs={{0,16},{1,5},{2,18},{3,7},{4,20},{5,1},{6,22},{7,3},{8,24},{9,13},... | collective-permute-start | bytes 1572872 | tf_op jit(solution)/shard_map/ppermute | solution.py:31
  40.3 0.1 add_convert_fusion.1
  40.6 0.2 add_convert_fusion
  40.8 1.7 %collective-permute-start.14 = (bf16[16,128,128]{2,1,0:T(8,128)(2,1)S(1)}, bf16[16,128,128]{2,1,0:T(8,128)(2,1)S(1)}, u32[]{:S(2)}, u32[]{:S(2)}) collective-permute-start(bf16[16,128,128]{2,1,0:T(8,128)(2,1)S(1)} %add_convert_fusion), channel_id=1, source_target_pairs={{0,24},{1,7},{2,26},{3,5},{4,28},{5,3},{6,30},{7,1},{8,16},{9,15},... | collective-permute-start | bytes 1572872 | tf_op jit(solution)/shard_map/ppermute | solution.py:31
  42.5 5.1 %collective-permute-done.10 = bf16[16,128,128]{2,1,0:T(8,128)(2,1)S(1)} collective-permute-done((bf16[16,128,128]{2,1,0:T(8,128)(2,1)S(1)}, bf16[16,128,128]{2,1,0:T(8,128)(2,1)S(1)}, u32[]{:S(2)}, u32[]{:S(2)}) %collective-permute-start.10) | collective-permute-done | bytes 524320 | tf_op jit(solution)/shard_map/ppermute | solution.py:31
  47.6 5.1 %collective-permute-done.12 = bf16[16,128,128]{2,1,0:T(8,128)(2,1)S(1)} collective-permute-done((bf16[16,128,128]{2,1,0:T(8,128)(2,1)S(1)}, bf16[16,128,128]{2,1,0:T(8,128)(2,1)S(1)}, u32[]{:S(2)}, u32[]{:S(2)}) %collective-permute-start.12) | collective-permute-done | bytes 524320 | tf_op jit(solution)/shard_map/ppermute | solution.py:31
  52.7 0.4 collective-permute-done.14
  53.1 0.4 fusion.11
  53.6 3.2 %collective-permute-start.15 = (bf16[4,128,128]{2,1,0:T(8,128)(2,1)S(1)}, bf16[4,128,128]{2,1,0:T(8,128)(2,1)S(1)}, u32[]{:S(2)}, u32[]{:S(2)}) collective-permute-start(bf16[4,128,128]{2,1,0:T(8,128)(2,1)S(1)} %get-tuple-element.112), channel_id=1, source_target_pairs={{0,2},{1,9},{2,0},{3,11},{4,6},{5,13},{6,4},{7,15},{8,10},{9,1},{1... | collective-permute-start | bytes 393224 | tf_op jit(solution)/shard_map/ppermute | solution.py:31
  56.7 2.3 %collective-permute-start.16 = (bf16[4,128,128]{2,1,0:T(8,128)(2,1)S(1)}, bf16[4,128,128]{2,1,0:T(8,128)(2,1)S(1)}, u32[]{:S(2)}, u32[]{:S(2)}) collective-permute-start(bf16[4,128,128]{2,1,0:T(8,128)(2,1)S(1)} %get-tuple-element.111), channel_id=1, source_target_pairs={{0,4},{1,17},{2,6},{3,19},{4,0},{5,21},{6,2},{7,23},{8,12},{9,25},... | collective-permute-start | bytes 393224 | tf_op jit(solution)/shard_map/ppermute | solution.py:31
  59.0 0.5 collective-permute-start.17
  59.5 0.2 collective-permute-done.15
  59.7 3.7 %collective-permute-done.16 = bf16[4,128,128]{2,1,0:T(8,128)(2,1)S(1)} collective-permute-done((bf16[4,128,128]{2,1,0:T(8,128)(2,1)S(1)}, bf16[4,128,128]{2,1,0:T(8,128)(2,1)S(1)}, u32[]{:S(2)}, u32[]{:S(2)}) %collective-permute-start.16) | collective-permute-done | bytes 131104 | tf_op jit(solution)/shard_map/ppermute | solution.py:31
  63.4 1.8 %collective-permute-done.17 = bf16[4,128,128]{2,1,0:T(8,128)(2,1)S(1)} collective-permute-done((bf16[4,128,128]{2,1,0:T(8,128)(2,1)S(1)}, bf16[4,128,128]{2,1,0:T(8,128)(2,1)S(1)}, u32[]{:S(2)}, u32[]{:S(2)}) %collective-permute-start.17) | collective-permute-done | bytes 131104 | tf_op jit(solution)/shard_map/ppermute | solution.py:31
  65.2 1.5 %layer.1 = (bf16[512,256]{1,0:T(8,128)(2,1)}, f32[512,128]{1,0:T(8,128)S(1)}, bf16[512,128]{1,0:T(8,128)(2,1)S(1)}, bf16[272,128]{1,0:T(8,128)(2,1)S(1)}, bf16[272,128]{1,0:T(8,128)(2,1)S(1)}) custom-call(s32[1]{0:T(128)} %bitcast.core, f32[512,128]{1,0:T(8,128)S(1)} %bitcast.24, bf16[512,128]{1,0:T(8,128)(2,1)S(1)} %bitcast.32, ...), custom_call_target="tpu_custom_call" | custom-call | tf_op jit(solution)/shard_map/layer/pallas_call | solution.py:227
  66.7 1.3 collective-permute-done.18
  68.0 2.2 %collective-permute-start.19 = (bf16[784,128]{1,0:T(8,128)(2,1)S(1)}, bf16[784,128]{1,0:T(8,128)(2,1)S(1)}, u32[]{:S(2)}, u32[]{:S(2)}) collective-permute-start(bf16[784,128]{1,0:T(8,128)(2,1)S(1)} %pad_maximum_fusion), channel_id=1, source_target_pairs={{0,8},{1,3},{2,10},{3,1},{4,12},{5,7},{6,14},{7,5},{8,0},{9,11},{1... | collective-permute-start | bytes 602120 | tf_op jit(solution)/shard_map/ppermute | solution.py:31
  70.2 1.6 %collective-permute-start.20 = (bf16[784,128]{1,0:T(8,128)(2,1)S(1)}, bf16[784,128]{1,0:T(8,128)(2,1)S(1)}, u32[]{:S(2)}, u32[]{:S(2)}) collective-permute-start(bf16[784,128]{1,0:T(8,128)(2,1)S(1)} %pad_maximum_fusion), channel_id=1, source_target_pairs={{0,16},{1,5},{2,18},{3,7},{4,20},{5,1},{6,22},{7,3},{8,24},{9,13},... | collective-permute-start | bytes 602120 | tf_op jit(solution)/shard_map/ppermute | solution.py:31
  71.8 1.2 collective-permute-start.21
  73.0 0.9 collective-permute-done.19
  73.9 3.7 %collective-permute-done.20 = bf16[784,128]{1,0:T(8,128)(2,1)S(1)} collective-permute-done((bf16[784,128]{1,0:T(8,128)(2,1)S(1)}, bf16[784,128]{1,0:T(8,128)(2,1)S(1)}, u32[]{:S(2)}, u32[]{:S(2)}) %collective-permute-start.20) | collective-permute-done | bytes 200736 | tf_op jit(solution)/shard_map/ppermute | solution.py:31
  77.6 2.0 %collective-permute-done.21 = bf16[784,128]{1,0:T(8,128)(2,1)S(1)} collective-permute-done((bf16[784,128]{1,0:T(8,128)(2,1)S(1)}, bf16[784,128]{1,0:T(8,128)(2,1)S(1)}, u32[]{:S(2)}, u32[]{:S(2)}) %collective-permute-start.21) | collective-permute-done | bytes 200736 | tf_op jit(solution)/shard_map/ppermute | solution.py:31
  79.8 2.5 %collective-permute-start.23 = (bf16[2320,128]{1,0:T(8,128)(2,1)S(1)}, bf16[2320,128]{1,0:T(8,128)(2,1)S(1)}, u32[]{:S(2)}, u32[]{:S(2)}) collective-permute-start(bf16[2320,128]{1,0:T(8,128)(2,1)S(1)} %get-tuple-element.106.rest_0_), channel_id=1, source_target_pairs={{0,4},{1,17},{2,6},{3,19},{4,0},{5,21},{6,2},{7,23},{8,12},{9,25},... | collective-permute-start | bytes 1781768 | tf_op jit(solution)/shard_map/ppermute | solution.py:31
  82.3 2.2 %collective-permute-start.24 = (bf16[2320,128]{1,0:T(8,128)(2,1)S(1)}, bf16[2320,128]{1,0:T(8,128)(2,1)S(1)}, u32[]{:S(2)}, u32[]{:S(2)}) collective-permute-start(bf16[2320,128]{1,0:T(8,128)(2,1)S(1)} %get-tuple-element.106.rest_0_), channel_id=1, source_target_pairs={{0,6},{1,25},{2,4},{3,27},{4,2},{5,29},{6,0},{7,31},{8,14},{9,17},... | collective-permute-start | bytes 1781768 | tf_op jit(solution)/shard_map/ppermute | solution.py:31
  84.5 5.2 %collective-permute-done.22.rest_1_ = bf16[2320,128]{1,0:T(8,128)(2,1)S(1)} collective-permute-done((bf16[2320,128]{1,0:T(8,128)(2,1)S(1)}, bf16[2320,128]{1,0:T(8,128)(2,1)S(1)}, u32[]{:S(2)}, u32[]{:S(2)}) %collective-permute-start.22) | collective-permute-done | bytes 593952 | tf_op jit(solution)/shard_map/ppermute | solution.py:31
  89.8 6.9 %collective-permute-done.23.rest_2_ = bf16[2320,128]{1,0:T(8,128)(2,1)S(1)} collective-permute-done((bf16[2320,128]{1,0:T(8,128)(2,1)S(1)}, bf16[2320,128]{1,0:T(8,128)(2,1)S(1)}, u32[]{:S(2)}, u32[]{:S(2)}) %collective-permute-start.23) | collective-permute-done | bytes 593952 | tf_op jit(solution)/shard_map/ppermute | solution.py:31
  96.7 3.1 %collective-permute-done.24.rest_3_ = bf16[2320,128]{1,0:T(8,128)(2,1)S(1)} collective-permute-done((bf16[2320,128]{1,0:T(8,128)(2,1)S(1)}, bf16[2320,128]{1,0:T(8,128)(2,1)S(1)}, u32[]{:S(2)}, u32[]{:S(2)}) %collective-permute-start.24) | collective-permute-done | bytes 593952 | tf_op jit(solution)/shard_map/ppermute | solution.py:31
  99.9 0.7 collective-permute-start.25
  100.6 4.5 %collective-permute-start.26 = (bf16[272,128]{1,0:T(8,128)(2,1)S(1)}, bf16[272,128]{1,0:T(8,128)(2,1)S(1)}, u32[]{:S(2)}, u32[]{:S(2)}) collective-permute-start(bf16[272,128]{1,0:T(8,128)(2,1)S(1)} %add_convert_fusion.6), channel_id=1, source_target_pairs={{0,128},{32,160},{64,192},{96,224},{128,0},{160,32},{192,64},{224,... | collective-permute-start | bytes 208904 | tf_op jit(solution)/shard_map/ppermute | solution.py:39
  105.1 1.4 collective-permute-start.27
  106.5 9.4 %tiles_backward.1 = (f32[4,128,128]{2,1,0:T(8,128)S(1)}, bf16[4,128,128]{2,1,0:T(8,128)(2,1)S(1)}, bf16[4,128,128]{2,1,0:T(8,128)(2,1)S(1)}, bf16[4,128,128]{2,1...) custom-call(s32[1]{0:T(128)} %bitcast.22.count, ...), custom_call_target="tpu_custom_call" | custom-call | flops 1073741824 | bytes 16777216 | tf_op jit(solution)/shard_map/tiles_backward/pallas_call | solution.py:171
  115.9 0.7 copy-done.4
  116.7 5.9 %collective-permute-start.40 = (bf16[272,128]{1,0:T(8,128)(2,1)S(1)}, bf16[272,128]{1,0:T(8,128)(2,1)S(1)}, u32[]{:S(2)}, u32[]{:S(2)}) collective-permute-start(bf16[272,128]{1,0:T(8,128)(2,1)S(1)} %add_convert_fusion.5), channel_id=1, source_target_pairs={{0,64},{32,96},{64,0},{96,32},{128,192},{160,224},{192,128},{224,1... | collective-permute-start | bytes 208904 | tf_op jit(solution)/shard_map/ppermute | solution.py:39
  122.6 2.0 %collective-permute-start.33 = (bf16[4,128,128]{2,1,0:T(8,128)(2,1)S(1)}, bf16[4,128,128]{2,1,0:T(8,128)(2,1)S(1)}, u32[]{:S(2)}, u32[]{:S(2)}) collective-permute-start(bf16[4,128,128]{2,1,0:T(8,128)(2,1)S(1)} %get-tuple-element.76), channel_id=1, source_target_pairs={{0,224},{32,0},{64,32},{96,64},{128,96},{160,128},{192,160},{224,1... | collective-permute-start | bytes 393224 | tf_op jit(solution)/shard_map/ppermute | solution.py:35
  124.7 4.0 %collective-permute-start.35 = (bf16[2,128,128]{2,1,0:T(8,128)(2,1)S(1)}, bf16[2,128,128]{2,1,0:T(8,128)(2,1)S(1)}, u32[]{:S(2)}, u32[]{:S(2)}) collective-permute-start(bf16[2,128,128]{2,1,0:T(8,128)(2,1)S(1)} %get-tuple-element.78), channel_id=1, source_target_pairs={{0,192},{32,224},{64,0},{96,32},{128,64},{160,96},{192,128},{224,1... | collective-permute-start | bytes 196616 | tf_op jit(solution)/shard_map/ppermute | solution.py:35
  128.9 3.4 %collective-permute-done.34 = bf16[2,128,128]{2,1,0:T(8,128)(2,1)S(1)} collective-permute-done((bf16[2,128,128]{2,1,0:T(8,128)(2,1)S(1)}, bf16[2,128,128]{2,1,0:T(8,128)(2,1)S(1)}, u32[]{:S(2)}, u32[]{:S(2)}) %collective-permute-start.34) | collective-permute-done | bytes 65568 | tf_op jit(solution)/shard_map/ppermute | solution.py:35
  132.3 2.9 %collective-permute-start.39 = (bf16[4,128,128]{2,1,0:T(8,128)(2,1)S(1)}, bf16[4,128,128]{2,1,0:T(8,128)(2,1)S(1)}, u32[]{:S(2)}, u32[]{:S(2)}) collective-permute-start(bf16[4,128,128]{2,1,0:T(8,128)(2,1)S(1)} %add_convert_fusion.3), channel_id=1, source_target_pairs={{0,192},{32,224},{64,0},{96,32},{128,64},{160,96},{192,128},{224,1... | collective-permute-start | bytes 393224 | tf_op jit(solution)/shard_map/ppermute | solution.py:35
  135.3 0.1 collective-permute-start.38
  135.4 1.6 %collective-permute-start.36 = (bf16[4,128,128]{2,1,0:T(8,128)(2,1)S(1)}, bf16[4,128,128]{2,1,0:T(8,128)(2,1)S(1)}, u32[]{:S(2)}, u32[]{:S(2)}) collective-permute-start(bf16[4,128,128]{2,1,0:T(8,128)(2,1)S(1)} %get-tuple-element.85), channel_id=1, source_target_pairs={{0,32},{32,64},{64,96},{96,128},{128,160},{160,192},{192,224},{224... | collective-permute-start | bytes 393224 | tf_op jit(solution)/shard_map/ppermute | solution.py:35
  137.0 0.5 collective-permute-start.37
  137.5 2.5 %collective-permute-done.39.b2 = bf16[4,128,128]{2,1,0:T(8,128)(2,1)S(1)} collective-permute-done((bf16[4,128,128]{2,1,0:T(8,128)(2,1)S(1)}, bf16[4,128,128]{2,1,0:T(8,128)(2,1)S(1)}, u32[]{:S(2)}, u32[]{:S(2)}) %collective-permute-start.39) | collective-permute-done | bytes 131104 | tf_op jit(solution)/shard_map/ppermute | solution.py:35
  140.0 4.8 %collective-permute-done.38.f2 = bf16[4,128,128]{2,1,0:T(8,128)(2,1)S(1)} collective-permute-done((bf16[4,128,128]{2,1,0:T(8,128)(2,1)S(1)}, bf16[4,128,128]{2,1,0:T(8,128)(2,1)S(1)}, u32[]{:S(2)}, u32[]{:S(2)}) %collective-permute-start.38) | collective-permute-done | bytes 131104 | tf_op jit(solution)/shard_map/ppermute | solution.py:35
  144.9 0.6 copy-done.11
  145.6 2.2 %finish.1 = (f32[512,128]{1,0:T(8,128)}, f32[128,256]{1,0:T(8,128)}, f32[128,256]{1,0:T(8,128)}, f32[2,128]{1,0:T(2,128)}) custom-call(s32[1]{0:T(128)} %bitcast.core, f32[1]{0:T(128)} %constant.133.clone.1.scale, f32[512,128]{1,0:T(8,128)} %copy-done.3, f32[4,128,128]{2,1,0:T(8,128)} %copy-done.4, bf16[4,128,128]{2,1,0:T(8,128)(2,1)} %copy-done.12, ...), custom_call_target="tpu_custom_call" | custom-call | tf_op jit(solution)/shard_map/finish/pallas_call | solution.py:254
  (74 shorter events, 1.1 us)
Async XLA Ops:
  0.6 12.5 %collective-permute-start.3 = (bf16[512,128]{1,0:T(8,128)(2,1)}, bf16[512,128]{1,0:T(8,128)(2,1)S(1)}, u32[]{:S(2)}, u32[]{:S(2)}) collective-permute-start(bf16[512,128]{1,0:T(8,128)(2,1)} %feats.1), channel_id=1, source_target_pairs={{0,64},{32,96},{64,128},{96,160},{128,192},{160,224},{192,0},{224,... | collective-permute-start | bytes 393224 | tf_op jit(solution)/shard_map/ppermute | solution.py:35
  4.0 9.2 %collective-permute-start.1 = (bf16[512,128]{1,0:T(8,128)(2,1)}, bf16[512,128]{1,0:T(8,128)(2,1)S(1)}, u32[]{:S(2)}, u32[]{:S(2)}) collective-permute-start(bf16[512,128]{1,0:T(8,128)(2,1)} %feats.1), channel_id=1, source_target_pairs={{0,192},{32,224},{64,0},{96,32},{128,64},{160,96},{192,128},{224,1... | collective-permute-start | bytes 393224 | tf_op jit(solution)/shard_map/ppermute | solution.py:35
  6.2 12.0 %collective-permute-start.6 = (bf16[512,128]{1,0:T(8,128)(2,1)}, bf16[512,128]{1,0:T(8,128)(2,1)S(1)}, u32[]{:S(2)}, u32[]{:S(2)}) collective-permute-start(bf16[512,128]{1,0:T(8,128)(2,1)} %feats.1), channel_id=1, source_target_pairs={{0,32},{32,64},{64,96},{96,128},{128,160},{160,192},{192,224},{224... | collective-permute-start | bytes 393224 | tf_op jit(solution)/shard_map/ppermute | solution.py:35
  7.1 13.0 %collective-permute-start = (bf16[512,128]{1,0:T(8,128)(2,1)}, bf16[512,128]{1,0:T(8,128)(2,1)S(1)}, u32[]{:S(2)}, u32[]{:S(2)}) collective-permute-start(bf16[512,128]{1,0:T(8,128)(2,1)} %feats.1), channel_id=1, source_target_pairs={{0,224},{32,0},{64,32},{96,64},{128,96},{160,128},{192,160},{224,1... | collective-permute-start | bytes 393224 | tf_op jit(solution)/shard_map/ppermute | solution.py:35
  13.2 7.0 %collective-permute-start.4 = (bf16[256,128]{1,0:T(8,128)(2,1)S(1)}, bf16[256,128]{1,0:T(8,128)(2,1)S(1)}, u32[]{:S(2)}, u32[]{:S(2)}) collective-permute-start(bf16[256,128]{1,0:T(8,128)(2,1)S(1)} %slice.63), channel_id=1, source_target_pairs={{0,64},{32,96},{64,128},{96,160},{128,192},{160,224},{192,0},{224,... | collective-permute-start | bytes 196616 | tf_op jit(solution)/shard_map/ppermute | solution.py:35
  13.2 7.1 %collective-permute-start.7 = (bf16[256,128]{1,0:T(8,128)(2,1)S(1)}, bf16[256,128]{1,0:T(8,128)(2,1)S(1)}, u32[]{:S(2)}, u32[]{:S(2)}) collective-permute-start(bf16[256,128]{1,0:T(8,128)(2,1)S(1)} %slice.64), channel_id=1, source_target_pairs={{0,192},{32,224},{64,0},{96,32},{128,64},{160,96},{192,128},{224,1... | collective-permute-start | bytes 196616 | tf_op jit(solution)/shard_map/ppermute | solution.py:35
  17.4 5.0 %collective-permute-start.5 = (bf16[512,128]{1,0:T(8,128)(2,1)S(1)}, bf16[512,128]{1,0:T(8,128)(2,1)S(1)}, u32[]{:S(2)}, u32[]{:S(2)}) collective-permute-start(bf16[512,128]{1,0:T(8,128)(2,1)S(1)} %collective-permute-done.3), channel_id=1, source_target_pairs={{0,32},{32,64},{64,96},{96,128},{128,160},{160,192},{192,224},{224... | collective-permute-start | bytes 393224 | tf_op jit(solution)/shard_map/ppermute | solution.py:35
  18.2 5.2 %collective-permute-start.2 = (bf16[512,128]{1,0:T(8,128)(2,1)S(1)}, bf16[512,128]{1,0:T(8,128)(2,1)S(1)}, u32[]{:S(2)}, u32[]{:S(2)}) collective-permute-start(bf16[512,128]{1,0:T(8,128)(2,1)S(1)} %collective-permute-done.1), channel_id=1, source_target_pairs={{0,224},{32,0},{64,32},{96,64},{128,96},{160,128},{192,160},{224,1... | collective-permute-start | bytes 393224 | tf_op jit(solution)/shard_map/ppermute | solution.py:35
  23.4 0.9 copy-start
  24.3 40.9 %copy-start.1 = (bf16[512,128]{1,0:T(8,128)(2,1)S(1)}, bf16[512,128]{1,0:T(8,128)(2,1)}, u32[]{:S(2)}) copy-start(bf16[512,128]{1,0:T(8,128)(2,1)} %feats.1) | copy-start | bytes 393220
  24.3 40.9 %copy-start.2 = (bf16[512,256]{1,0:T(8,128)(2,1)S(1)}, bf16[512,256]{1,0:T(8,128)(2,1)}, u32[]{:S(2)}) copy-start(bf16[512,256]{1,0:T(8,128)(2,1)} %cot.1) | copy-start | bytes 786436
  24.3 40.9 %copy-start.5 = (bf16[128,256]{1,0:T(8,128)(2,1)S(1)}, bf16[128,256]{1,0:T(8,128)(2,1)}, u32[]{:S(2)}) copy-start(bf16[128,256]{1,0:T(8,128)(2,1)} %w_self.1) | copy-start | bytes 196612
  24.3 40.9 %copy-start.6 = (bf16[128,256]{1,0:T(8,128)(2,1)S(1)}, bf16[128,256]{1,0:T(8,128)(2,1)}, u32[]{:S(2)}) copy-start(bf16[128,256]{1,0:T(8,128)(2,1)} %w_neigh.1) | copy-start | bytes 196612
  24.3 40.9 %copy-start.7 = (f32[256]{0:T(256)S(1)}, f32[256]{0:T(256)}, u32[]{:S(2)}) copy-start(f32[256]{0:T(256)} %param.12) | copy-start | bytes 3076
  34.3 2.0 %collective-permute-start.9 = (bf16[16,128,128]{2,1,0:T(8,128)(2,1)S(1)}, bf16[16,128,128]{2,1,0:T(8,128)(2,1)S(1)}, u32[]{:S(2)}, u32[]{:S(2)}) collective-permute-start(bf16[16,128,128]{2,1,0:T(8,128)(2,1)S(1)} %get-tuple-element.56), channel_id=1, source_target_pairs={{0,1},{1,0},{2,3},{3,2},{4,5},{5,4},{6,7},{7,6},{8,9},{9,8},{10,11... | collective-permute-start | bytes 1572872 | tf_op jit(solution)/shard_map/ppermute | solution.py:27
  34.4 5.9 %collective-permute-start.11 = (bf16[16,128,128]{2,1,0:T(8,128)(2,1)S(1)}, bf16[16,128,128]{2,1,0:T(8,128)(2,1)S(1)}, u32[]{:S(2)}, u32[]{:S(2)}) collective-permute-start(bf16[16,128,128]{2,1,0:T(8,128)(2,1)S(1)} %get-tuple-element.58), channel_id=1, source_target_pairs={{0,1},{1,0},{2,3},{3,2},{4,5},{5,4},{6,7},{7,6},{8,9},{9,8},{10,11... | collective-permute-start | bytes 1572872 | tf_op jit(solution)/shard_map/ppermute | solution.py:27
  34.9 5.6 %collective-permute-start.13 = (bf16[16,128,128]{2,1,0:T(8,128)(2,1)S(1)}, bf16[16,128,128]{2,1,0:T(8,128)(2,1)S(1)}, u32[]{:S(2)}, u32[]{:S(2)}) collective-permute-start(bf16[16,128,128]{2,1,0:T(8,128)(2,1)S(1)} %get-tuple-element.60), channel_id=1, source_target_pairs={{0,1},{1,0},{2,3},{3,2},{4,5},{5,4},{6,7},{7,6},{8,9},{9,8},{10,11... | collective-permute-start | bytes 1572872 | tf_op jit(solution)/shard_map/ppermute | solution.py:27
  35.0 7.4 %collective-permute-start.8 = (bf16[16,128,128]{2,1,0:T(8,128)(2,1)S(1)}, bf16[16,128,128]{2,1,0:T(8,128)(2,1)S(1)}, u32[]{:S(2)}, u32[]{:S(2)}) collective-permute-start(bf16[16,128,128]{2,1,0:T(8,128)(2,1)S(1)} %get-tuple-element.54), channel_id=1, source_target_pairs={{0,1},{1,0},{2,3},{3,2},{4,5},{5,4},{6,7},{7,6},{8,9},{9,8},{10,11... | collective-permute-start | bytes 1572872 | tf_op jit(solution)/shard_map/ppermute | solution.py:27
  36.5 11.1 %collective-permute-start.10 = (bf16[16,128,128]{2,1,0:T(8,128)(2,1)S(1)}, bf16[16,128,128]{2,1,0:T(8,128)(2,1)S(1)}, u32[]{:S(2)}, u32[]{:S(2)}) collective-permute-start(bf16[16,128,128]{2,1,0:T(8,128)(2,1)S(1)} %add_convert_fusion.2), channel_id=1, source_target_pairs={{0,16},{1,5},{2,18},{3,7},{4,20},{5,1},{6,22},{7,3},{8,24},{9,13},... | collective-permute-start | bytes 1572872 | tf_op jit(solution)/shard_map/ppermute | solution.py:31
  40.5 12.2 %collective-permute-start.12 = (bf16[16,128,128]{2,1,0:T(8,128)(2,1)S(1)}, bf16[16,128,128]{2,1,0:T(8,128)(2,1)S(1)}, u32[]{:S(2)}, u32[]{:S(2)}) collective-permute-start(bf16[16,128,128]{2,1,0:T(8,128)(2,1)S(1)} %add_convert_fusion.1), channel_id=1, source_target_pairs={{0,8},{1,3},{2,10},{3,1},{4,12},{5,7},{6,14},{7,5},{8,0},{9,11},{1... | collective-permute-start | bytes 1572872 | tf_op jit(solution)/shard_map/ppermute | solution.py:31
  40.8 12.3 %collective-permute-start.14 = (bf16[16,128,128]{2,1,0:T(8,128)(2,1)S(1)}, bf16[16,128,128]{2,1,0:T(8,128)(2,1)S(1)}, u32[]{:S(2)}, u32[]{:S(2)}) collective-permute-start(bf16[16,128,128]{2,1,0:T(8,128)(2,1)S(1)} %add_convert_fusion), channel_id=1, source_target_pairs={{0,24},{1,7},{2,26},{3,5},{4,28},{5,3},{6,30},{7,1},{8,16},{9,15},... | collective-permute-start | bytes 1572872 | tf_op jit(solution)/shard_map/ppermute | solution.py:31
  53.6 6.1 %collective-permute-start.15 = (bf16[4,128,128]{2,1,0:T(8,128)(2,1)S(1)}, bf16[4,128,128]{2,1,0:T(8,128)(2,1)S(1)}, u32[]{:S(2)}, u32[]{:S(2)}) collective-permute-start(bf16[4,128,128]{2,1,0:T(8,128)(2,1)S(1)} %get-tuple-element.112), channel_id=1, source_target_pairs={{0,2},{1,9},{2,0},{3,11},{4,6},{5,13},{6,4},{7,15},{8,10},{9,1},{1... | collective-permute-start | bytes 393224 | tf_op jit(solution)/shard_map/ppermute | solution.py:31
  56.7 6.6 %collective-permute-start.16 = (bf16[4,128,128]{2,1,0:T(8,128)(2,1)S(1)}, bf16[4,128,128]{2,1,0:T(8,128)(2,1)S(1)}, u32[]{:S(2)}, u32[]{:S(2)}) collective-permute-start(bf16[4,128,128]{2,1,0:T(8,128)(2,1)S(1)} %get-tuple-element.111), channel_id=1, source_target_pairs={{0,4},{1,17},{2,6},{3,19},{4,0},{5,21},{6,2},{7,23},{8,12},{9,25},... | collective-permute-start | bytes 393224 | tf_op jit(solution)/shard_map/ppermute | solution.py:31
  59.0 6.2 %collective-permute-start.17 = (bf16[4,128,128]{2,1,0:T(8,128)(2,1)S(1)}, bf16[4,128,128]{2,1,0:T(8,128)(2,1)S(1)}, u32[]{:S(2)}, u32[]{:S(2)}) collective-permute-start(bf16[4,128,128]{2,1,0:T(8,128)(2,1)S(1)} %get-tuple-element.110), channel_id=1, source_target_pairs={{0,6},{1,25},{2,4},{3,27},{4,2},{5,29},{6,0},{7,31},{8,14},{9,17},... | collective-permute-start | bytes 393224 | tf_op jit(solution)/shard_map/ppermute | solution.py:31
  66.7 13.0 %copy-start.3 = (f32[512,128]{1,0:T(8,128)}, f32[512,128]{1,0:T(8,128)S(1)}, u32[]{:S(2)}) copy-start(f32[512,128]{1,0:T(8,128)S(1)} %get-tuple-element.62.base) | copy-start | bytes 786436
  66.7 1.3 collective-permute-start.18
  68.0 5.8 %collective-permute-start.19 = (bf16[784,128]{1,0:T(8,128)(2,1)S(1)}, bf16[784,128]{1,0:T(8,128)(2,1)S(1)}, u32[]{:S(2)}, u32[]{:S(2)}) collective-permute-start(bf16[784,128]{1,0:T(8,128)(2,1)S(1)} %pad_maximum_fusion), channel_id=1, source_target_pairs={{0,8},{1,3},{2,10},{3,1},{4,12},{5,7},{6,14},{7,5},{8,0},{9,11},{1... | collective-permute-start | bytes 602120 | tf_op jit(solution)/shard_map/ppermute | solution.py:31
  70.2 7.4 %collective-permute-start.20 = (bf16[784,128]{1,0:T(8,128)(2,1)S(1)}, bf16[784,128]{1,0:T(8,128)(2,1)S(1)}, u32[]{:S(2)}, u32[]{:S(2)}) collective-permute-start(bf16[784,128]{1,0:T(8,128)(2,1)S(1)} %pad_maximum_fusion), channel_id=1, source_target_pairs={{0,16},{1,5},{2,18},{3,7},{4,20},{5,1},{6,22},{7,3},{8,24},{9,13},... | collective-permute-start | bytes 602120 | tf_op jit(solution)/shard_map/ppermute | solution.py:31
  71.8 7.9 %collective-permute-start.21 = (bf16[784,128]{1,0:T(8,128)(2,1)S(1)}, bf16[784,128]{1,0:T(8,128)(2,1)S(1)}, u32[]{:S(2)}, u32[]{:S(2)}) collective-permute-start(bf16[784,128]{1,0:T(8,128)(2,1)S(1)} %pad_maximum_fusion), channel_id=1, source_target_pairs={{0,24},{1,7},{2,26},{3,5},{4,28},{5,3},{6,30},{7,1},{8,16},{9,15},... | collective-permute-start | bytes 602120 | tf_op jit(solution)/shard_map/ppermute | solution.py:31
  79.7 10.0 %collective-permute-start.22 = (bf16[2320,128]{1,0:T(8,128)(2,1)S(1)}, bf16[2320,128]{1,0:T(8,128)(2,1)S(1)}, u32[]{:S(2)}, u32[]{:S(2)}) collective-permute-start(bf16[2320,128]{1,0:T(8,128)(2,1)S(1)} %get-tuple-element.106.rest_0_), channel_id=1, source_target_pairs={{0,2},{1,9},{2,0},{3,11},{4,6},{5,13},{6,4},{7,15},{8,10},{9,1},{1... | collective-permute-start | bytes 1781768 | tf_op jit(solution)/shard_map/ppermute | solution.py:31
  79.8 16.9 %collective-permute-start.23 = (bf16[2320,128]{1,0:T(8,128)(2,1)S(1)}, bf16[2320,128]{1,0:T(8,128)(2,1)S(1)}, u32[]{:S(2)}, u32[]{:S(2)}) collective-permute-start(bf16[2320,128]{1,0:T(8,128)(2,1)S(1)} %get-tuple-element.106.rest_0_), channel_id=1, source_target_pairs={{0,4},{1,17},{2,6},{3,19},{4,0},{5,21},{6,2},{7,23},{8,12},{9,25},... | collective-permute-start | bytes 1781768 | tf_op jit(solution)/shard_map/ppermute | solution.py:31
  82.3 17.5 %collective-permute-start.24 = (bf16[2320,128]{1,0:T(8,128)(2,1)S(1)}, bf16[2320,128]{1,0:T(8,128)(2,1)S(1)}, u32[]{:S(2)}, u32[]{:S(2)}) collective-permute-start(bf16[2320,128]{1,0:T(8,128)(2,1)S(1)} %get-tuple-element.106.rest_0_), channel_id=1, source_target_pairs={{0,6},{1,25},{2,4},{3,27},{4,2},{5,29},{6,0},{7,31},{8,14},{9,17},... | collective-permute-start | bytes 1781768 | tf_op jit(solution)/shard_map/ppermute | solution.py:31
  84.5 16.1 %collective-permute-start.28 = (bf16[2320,128]{1,0:T(8,128)(2,1)S(1)}, bf16[2320,128]{1,0:T(8,128)(2,1)S(1)}, u32[]{:S(2)}, u32[]{:S(2)}) collective-permute-start(bf16[2320,128]{1,0:T(8,128)(2,1)S(1)} %get-tuple-element.106.rest_0_), channel_id=1, source_target_pairs={{0,1},{1,0},{2,3},{3,2},{4,5},{5,4},{6,7},{7,6},{8,9},{9,8},{10,11... | collective-permute-start | bytes 1781768 | tf_op jit(solution)/shard_map/ppermute | solution.py:27
  89.8 15.4 %collective-permute-start.29 = (bf16[2320,128]{1,0:T(8,128)(2,1)S(1)}, bf16[2320,128]{1,0:T(8,128)(2,1)S(1)}, u32[]{:S(2)}, u32[]{:S(2)}) collective-permute-start(bf16[2320,128]{1,0:T(8,128)(2,1)S(1)} %collective-permute-done.22.rest_1_), channel_id=1, source_target_pairs={{0,1},{1,0},{2,3},{3,2},{4,5},{5,4},{6,7},{7,6},{8,9},{9,8},{10,11... | collective-permute-start | bytes 1781768 | tf_op jit(solution)/shard_map/ppermute | solution.py:27
  96.7 9.8 %collective-permute-start.30 = (bf16[2320,128]{1,0:T(8,128)(2,1)S(1)}, bf16[2320,128]{1,0:T(8,128)(2,1)S(1)}, u32[]{:S(2)}, u32[]{:S(2)}) collective-permute-start(bf16[2320,128]{1,0:T(8,128)(2,1)S(1)} %collective-permute-done.23.rest_2_), channel_id=1, source_target_pairs={{0,1},{1,0},{2,3},{3,2},{4,5},{5,4},{6,7},{7,6},{8,9},{9,8},{10,11... | collective-permute-start | bytes 1781768 | tf_op jit(solution)/shard_map/ppermute | solution.py:27
  99.8 6.6 %collective-permute-start.31 = (bf16[2320,128]{1,0:T(8,128)(2,1)S(1)}, bf16[2320,128]{1,0:T(8,128)(2,1)S(1)}, u32[]{:S(2)}, u32[]{:S(2)}) collective-permute-start(bf16[2320,128]{1,0:T(8,128)(2,1)S(1)} %collective-permute-done.24.rest_3_), channel_id=1, source_target_pairs={{0,1},{1,0},{2,3},{3,2},{4,5},{5,4},{6,7},{7,6},{8,9},{9,8},{10,11... | collective-permute-start | bytes 1781768 | tf_op jit(solution)/shard_map/ppermute | solution.py:27
  99.9 16.8 %collective-permute-start.25 = (bf16[272,128]{1,0:T(8,128)(2,1)S(1)}, bf16[272,128]{1,0:T(8,128)(2,1)S(1)}, u32[]{:S(2)}, u32[]{:S(2)}) collective-permute-start(bf16[272,128]{1,0:T(8,128)(2,1)S(1)} %add_convert_fusion.6), channel_id=1, source_target_pairs={{0,32},{32,0},{64,96},{96,64},{128,160},{160,128},{192,224},{224,1... | collective-permute-start | bytes 208904 | tf_op jit(solution)/shard_map/ppermute | solution.py:39
  100.6 16.1 %collective-permute-start.26 = (bf16[272,128]{1,0:T(8,128)(2,1)S(1)}, bf16[272,128]{1,0:T(8,128)(2,1)S(1)}, u32[]{:S(2)}, u32[]{:S(2)}) collective-permute-start(bf16[272,128]{1,0:T(8,128)(2,1)S(1)} %add_convert_fusion.6), channel_id=1, source_target_pairs={{0,128},{32,160},{64,192},{96,224},{128,0},{160,32},{192,64},{224,... | collective-permute-start | bytes 208904 | tf_op jit(solution)/shard_map/ppermute | solution.py:39
  105.1 11.5 %collective-permute-start.27 = (bf16[272,128]{1,0:T(8,128)(2,1)S(1)}, bf16[272,128]{1,0:T(8,128)(2,1)S(1)}, u32[]{:S(2)}, u32[]{:S(2)}) collective-permute-start(bf16[272,128]{1,0:T(8,128)(2,1)S(1)} %add_convert_fusion.6), channel_id=1, source_target_pairs={{0,160},{32,128},{64,224},{96,192},{128,32},{160,0},{192,96},{224,... | collective-permute-start | bytes 208904 | tf_op jit(solution)/shard_map/ppermute | solution.py:39
  115.9 0.7 copy-start.4
  116.7 12.0 %collective-permute-start.40 = (bf16[272,128]{1,0:T(8,128)(2,1)S(1)}, bf16[272,128]{1,0:T(8,128)(2,1)S(1)}, u32[]{:S(2)}, u32[]{:S(2)}) collective-permute-start(bf16[272,128]{1,0:T(8,128)(2,1)S(1)} %add_convert_fusion.5), channel_id=1, source_target_pairs={{0,64},{32,96},{64,0},{96,32},{128,192},{160,224},{192,128},{224,1... | collective-permute-start | bytes 208904 | tf_op jit(solution)/shard_map/ppermute | solution.py:39
  122.6 9.7 %collective-permute-start.32 = (bf16[4,128,128]{2,1,0:T(8,128)(2,1)S(1)}, bf16[4,128,128]{2,1,0:T(8,128)(2,1)S(1)}, u32[]{:S(2)}, u32[]{:S(2)}) collective-permute-start(bf16[4,128,128]{2,1,0:T(8,128)(2,1)S(1)} %get-tuple-element.75), channel_id=1, source_target_pairs={{0,32},{32,64},{64,96},{96,128},{128,160},{160,192},{192,224},{224... | collective-permute-start | bytes 393224 | tf_op jit(solution)/shard_map/ppermute | solution.py:35
  122.6 9.7 %collective-permute-start.33 = (bf16[4,128,128]{2,1,0:T(8,128)(2,1)S(1)}, bf16[4,128,128]{2,1,0:T(8,128)(2,1)S(1)}, u32[]{:S(2)}, u32[]{:S(2)}) collective-permute-start(bf16[4,128,128]{2,1,0:T(8,128)(2,1)S(1)} %get-tuple-element.76), channel_id=1, source_target_pairs={{0,224},{32,0},{64,32},{96,64},{128,96},{160,128},{192,160},{224,1... | collective-permute-start | bytes 393224 | tf_op jit(solution)/shard_map/ppermute | solution.py:35
  124.6 7.6 %collective-permute-start.34 = (bf16[2,128,128]{2,1,0:T(8,128)(2,1)S(1)}, bf16[2,128,128]{2,1,0:T(8,128)(2,1)S(1)}, u32[]{:S(2)}, u32[]{:S(2)}) collective-permute-start(bf16[2,128,128]{2,1,0:T(8,128)(2,1)S(1)} %get-tuple-element.77), channel_id=1, source_target_pairs={{0,64},{32,96},{64,128},{96,160},{128,192},{160,224},{192,0},{224,... | collective-permute-start | bytes 196616 | tf_op jit(solution)/shard_map/ppermute | solution.py:35
  124.7 7.5 %collective-permute-start.35 = (bf16[2,128,128]{2,1,0:T(8,128)(2,1)S(1)}, bf16[2,128,128]{2,1,0:T(8,128)(2,1)S(1)}, u32[]{:S(2)}, u32[]{:S(2)}) collective-permute-start(bf16[2,128,128]{2,1,0:T(8,128)(2,1)S(1)} %get-tuple-element.78), channel_id=1, source_target_pairs={{0,192},{32,224},{64,0},{96,32},{128,64},{160,96},{192,128},{224,1... | collective-permute-start | bytes 196616 | tf_op jit(solution)/shard_map/ppermute | solution.py:35
  128.8 16.1 %copy-start.8 = (f32[272,128]{1,0:T(8,128)}, f32[272,128]{1,0:T(8,128)S(1)}, u32[]{:S(2)}) copy-start(f32[272,128]{1,0:T(8,128)S(1)} %convert_add_fusion.mine) | copy-start | bytes 417796
  128.8 8.7 %collective-permute-start.41 = (f32[272,128]{1,0:T(8,128)S(1)}, f32[272,128]{1,0:T(8,128)S(1)}, u32[]{:S(2)}, u32[]{:S(2)}) collective-permute-start(f32[272,128]{1,0:T(8,128)S(1)} %convert_add_fusion.mine), channel_id=1, source_target_pairs={{0,1},{1,0},{2,3},{3,2},{4,5},{5,4},{6,7},{7,6},{8,9},{9,8},{10,11... | collective-permute-start | bytes 417800 | tf_op jit(solution)/shard_map/ppermute | solution.py:27
  132.3 7.7 %collective-permute-start.39 = (bf16[4,128,128]{2,1,0:T(8,128)(2,1)S(1)}, bf16[4,128,128]{2,1,0:T(8,128)(2,1)S(1)}, u32[]{:S(2)}, u32[]{:S(2)}) collective-permute-start(bf16[4,128,128]{2,1,0:T(8,128)(2,1)S(1)} %add_convert_fusion.3), channel_id=1, source_target_pairs={{0,192},{32,224},{64,0},{96,32},{128,64},{160,96},{192,128},{224,1... | collective-permute-start | bytes 393224 | tf_op jit(solution)/shard_map/ppermute | solution.py:35
  135.3 9.5 %collective-permute-start.38 = (bf16[4,128,128]{2,1,0:T(8,128)(2,1)S(1)}, bf16[4,128,128]{2,1,0:T(8,128)(2,1)S(1)}, u32[]{:S(2)}, u32[]{:S(2)}) collective-permute-start(bf16[4,128,128]{2,1,0:T(8,128)(2,1)S(1)} %add_convert_fusion.4), channel_id=1, source_target_pairs={{0,64},{32,96},{64,128},{96,160},{128,192},{160,224},{192,0},{224,... | collective-permute-start | bytes 393224 | tf_op jit(solution)/shard_map/ppermute | solution.py:35
  135.4 9.4 %collective-permute-start.36 = (bf16[4,128,128]{2,1,0:T(8,128)(2,1)S(1)}, bf16[4,128,128]{2,1,0:T(8,128)(2,1)S(1)}, u32[]{:S(2)}, u32[]{:S(2)}) collective-permute-start(bf16[4,128,128]{2,1,0:T(8,128)(2,1)S(1)} %get-tuple-element.85), channel_id=1, source_target_pairs={{0,32},{32,64},{64,96},{96,128},{128,160},{160,192},{192,224},{224... | collective-permute-start | bytes 393224 | tf_op jit(solution)/shard_map/ppermute | solution.py:35
  137.0 7.8 %collective-permute-start.37 = (bf16[4,128,128]{2,1,0:T(8,128)(2,1)S(1)}, bf16[4,128,128]{2,1,0:T(8,128)(2,1)S(1)}, u32[]{:S(2)}, u32[]{:S(2)}) collective-permute-start(bf16[4,128,128]{2,1,0:T(8,128)(2,1)S(1)} %get-tuple-element.86), channel_id=1, source_target_pairs={{0,224},{32,0},{64,32},{96,64},{128,96},{160,128},{192,160},{224,1... | collective-permute-start | bytes 393224 | tf_op jit(solution)/shard_map/ppermute | solution.py:35
  137.5 7.4 %copy-start.9 = (f32[272,128]{1,0:T(8,128)}, f32[272,128]{1,0:T(8,128)S(1)}, u32[]{:S(2)}) copy-start(f32[272,128]{1,0:T(8,128)S(1)} %collective-permute-done.41.theirs) | copy-start | bytes 417796
  140.0 4.8 %copy-start.10 = (bf16[4,128,128]{2,1,0:T(8,128)(2,1)}, bf16[4,128,128]{2,1,0:T(8,128)(2,1)S(1)}, u32[]{:S(2)}) copy-start(bf16[4,128,128]{2,1,0:T(8,128)(2,1)S(1)} %collective-permute-done.39.b2) | copy-start | bytes 393220
  144.8 0.7 copy-start.11
  144.8 0.7 copy-start.12
  144.8 0.7 copy-start.13

commit v2 on v1

--- a/solution.py
+++ b/solution.py
@@ -326,7 +326,6 @@
     up3, down3 = row_move(p[3], 1), row_move(p[5], -1)
     up4, down4 = row_move(p[4], 2), row_move(p[8], -2)
     swapped = row_swap(gw, 2)
-    up3, down3, up4, down4, p = lax.optimization_barrier((up3, down3, up4, down4, p))
     zeros = jnp.zeros((2, T, T), F32)
     up2 = p[2].astype(F32) + up3.astype(F32) + jnp.concatenate([up4.astype(F32), zeros], axis=0)
     down2 = p[6].astype(F32) + down3.astype(F32) + jnp.concatenate([zeros, down4.astype(F32)], axis=0)

time: 149 us -> 146 us (0.980)
  Pallas kernels: 23.1 us -> 21.6 us
  transfers between devices with their start and end apart: 42 -> 42, of which waited for: 21 -> 22; matrix products, arithmetic and copies ran while one was open for 1% -> 1% of each run, Pallas kernels for 6% -> 6%
where the time goes in v2:
time: 146 us
  starting transfers between devices  60.6 us (42%)
  waiting for transfers between devices  57 us (39%)
  Pallas kernels  21.6 us (15%)
  other arithmetic  2.62 us (2%)
  local copies, waits for them, and re-layouts  2.42 us (2%)
  between operations  1.63 us (1%)
    ppermute x12, waiting for transfers between devices, axis_move(): lax.ppermute(value, 'rep', [(i, i ^ k * (8 if i % 2 == which else 2)) for...  38.2 us
    ppermute x16, starting transfers between devices, row_move(): return lax.ppermute(value, 'row', [(i, (i + step) % 8) for i in range(8)])  25.4 us
    ppermute x12, starting transfers between devices, axis_move(): lax.ppermute(value, 'rep', [(i, i ^ k * (8 if i % 2 == which else 2)) for...  21.1 us
    ppermute x16, waiting for transfers between devices, row_move(): return lax.ppermute(value, 'row', [(i, (i + step) % 8) for i in range(8)])  16.6 us
    ppermute x4, starting transfers between devices, row_swap(): return lax.ppermute(value, 'row', [(i, i ^ bit) for i in range(8)])  13 us
    pallas_call x1, Pallas kernels, forward(): pl.pallas_call(forward_kernel, out_shape=blocks, in_specs=[SM, SM, SM, HB...  9.3 us
    pallas_call x1, Pallas kernels, backward(): pl.pallas_call(backward_kernel, out_shape=outs, in_specs=[SM, SM, SM, HB]...  8.61 us
  transfers between devices with their start and end apart: 42, of which 22 were waited for; matrix products, arithmetic and copies ran while one was open for 1% of the time, Pallas kernels for 6%

profile of v2, /device:TPU:32, one launch (start us, length us, event | category | flops | bytes accessed | tf_op | source)
XLA Modules:
  0.0 145.9 jit_solution(347424652017522611)
XLA Ops:
  0.6 3.3 %collective-permute-start.3 = (bf16[512,128]{1,0:T(8,128)(2,1)}, bf16[512,128]{1,0:T(8,128)(2,1)S(1)}, u32[]{:S(2)}, u32[]{:S(2)}) collective-permute-start(bf16[512,128]{1,0:T(8,128)(2,1)} %feats.1), channel_id=1, source_target_pairs={{0,64},{32,96},{64,128},{96,160},{128,192},{160,224},{192,0},{224,... | collective-permute-start | bytes 393224 | tf_op jit(solution)/shard_map/ppermute | solution.py:35
  4.0 2.2 %collective-permute-start.1 = (bf16[512,128]{1,0:T(8,128)(2,1)}, bf16[512,128]{1,0:T(8,128)(2,1)S(1)}, u32[]{:S(2)}, u32[]{:S(2)}) collective-permute-start(bf16[512,128]{1,0:T(8,128)(2,1)} %feats.1), channel_id=1, source_target_pairs={{0,192},{32,224},{64,0},{96,32},{128,64},{160,96},{192,128},{224,1... | collective-permute-start | bytes 393224 | tf_op jit(solution)/shard_map/ppermute | solution.py:35
  6.2 0.9 collective-permute-start.6
  7.1 1.1 collective-permute-start
  8.9 0.7 add_add_fusion.1
  9.6 3.5 %collective-permute-done.3 = bf16[512,128]{1,0:T(8,128)(2,1)S(1)} collective-permute-done((bf16[512,128]{1,0:T(8,128)(2,1)}, bf16[512,128]{1,0:T(8,128)(2,1)S(1)}, u32[]{:S(2)}, u32[]{:S(2)}) %collective-permute-start.3) | collective-permute-done | bytes 131104 | tf_op jit(solution)/shard_map/ppermute | solution.py:35
  13.2 4.2 %collective-permute-start.7 = (bf16[256,128]{1,0:T(8,128)(2,1)S(1)}, bf16[256,128]{1,0:T(8,128)(2,1)S(1)}, u32[]{:S(2)}, u32[]{:S(2)}) collective-permute-start(bf16[256,128]{1,0:T(8,128)(2,1)S(1)} %slice.64), channel_id=1, source_target_pairs={{0,192},{32,224},{64,0},{96,32},{128,64},{160,96},{192,128},{224,1... | collective-permute-start | bytes 196616 | tf_op jit(solution)/shard_map/ppermute | solution.py:35
  17.4 0.8 collective-permute-start.5
  18.2 1.2 collective-permute-start.2
  19.4 0.7 fusion.5
  20.1 0.2 collective-permute-done.7
  20.3 2.0 %collective-permute-done.5 = bf16[512,128]{1,0:T(8,128)(2,1)S(1)} collective-permute-done((bf16[512,128]{1,0:T(8,128)(2,1)S(1)}, bf16[512,128]{1,0:T(8,128)(2,1)S(1)}, u32[]{:S(2)}, u32[]{:S(2)}) %collective-permute-start.5) | collective-permute-done | bytes 131104 | tf_op jit(solution)/shard_map/ppermute | solution.py:35
  22.3 1.1 collective-permute-done.2
  23.4 0.9 copy-done
  24.3 9.3 %tiles_forward.1 = (bf16[16,128,128]{2,1,0:T(8,128)(2,1)S(1)}, bf16[16,128,128]{2,1,0:T(8,128)(2,1)S(1)}, bf16[16,128,128]{2,1,0:T(8,128)(2,1)S(1)}, bf16[16,128...) custom-call(s32[1]{0:T(128)} %bitcast.21.count, ...), custom_call_target="tpu_custom_call" | custom-call | flops 1073741824 | bytes 16777216 | tf_op jit(solution)/shard_map/tiles_forward/pallas_call | solution.py:113
  33.6 0.1 collective-permute-start.9
  33.7 0.5 collective-permute-start.11
  34.2 0.1 collective-permute-start.13
  34.3 0.4 collective-permute-start.8
  34.7 0.9 collective-permute-done.9
  35.6 0.1 add_convert_fusion.2
  35.8 5.2 %collective-permute-start.10 = (bf16[16,128,128]{2,1,0:T(8,128)(2,1)S(1)}, bf16[16,128,128]{2,1,0:T(8,128)(2,1)S(1)}, u32[]{:S(2)}, u32[]{:S(2)}) collective-permute-start(bf16[16,128,128]{2,1,0:T(8,128)(2,1)S(1)} %add_convert_fusion.2), channel_id=1, source_target_pairs={{0,16},{1,5},{2,18},{3,7},{4,20},{5,1},{6,22},{7,3},{8,24},{9,13},... | collective-permute-start | bytes 1572872 | tf_op jit(solution)/shard_map/ppermute | solution.py:31
  41.0 0.1 add_convert_fusion.1
  41.3 0.2 add_convert_fusion
  41.5 1.1 collective-permute-start.14
  42.6 5.7 %collective-permute-done.10 = bf16[16,128,128]{2,1,0:T(8,128)(2,1)S(1)} collective-permute-done((bf16[16,128,128]{2,1,0:T(8,128)(2,1)S(1)}, bf16[16,128,128]{2,1,0:T(8,128)(2,1)S(1)}, u32[]{:S(2)}, u32[]{:S(2)}) %collective-permute-start.10) | collective-permute-done | bytes 524320 | tf_op jit(solution)/shard_map/ppermute | solution.py:31
  48.3 5.1 %collective-permute-done.12 = bf16[16,128,128]{2,1,0:T(8,128)(2,1)S(1)} collective-permute-done((bf16[16,128,128]{2,1,0:T(8,128)(2,1)S(1)}, bf16[16,128,128]{2,1,0:T(8,128)(2,1)S(1)}, u32[]{:S(2)}, u32[]{:S(2)}) %collective-permute-start.12) | collective-permute-done | bytes 524320 | tf_op jit(solution)/shard_map/ppermute | solution.py:31
  53.4 0.4 collective-permute-done.14
  53.8 0.4 fusion.11
  54.3 0.7 collective-permute-start.15
  55.0 4.3 %collective-permute-start.16 = (bf16[4,128,128]{2,1,0:T(8,128)(2,1)S(1)}, bf16[4,128,128]{2,1,0:T(8,128)(2,1)S(1)}, u32[]{:S(2)}, u32[]{:S(2)}) collective-permute-start(bf16[4,128,128]{2,1,0:T(8,128)(2,1)S(1)} %get-tuple-element.93), channel_id=1, source_target_pairs={{0,4},{1,17},{2,6},{3,19},{4,0},{5,21},{6,2},{7,23},{8,12},{9,25},... | collective-permute-start | bytes 393224 | tf_op jit(solution)/shard_map/ppermute | solution.py:31
  59.3 0.2 collective-permute-done.15
  59.5 4.1 %collective-permute-done.16 = bf16[4,128,128]{2,1,0:T(8,128)(2,1)S(1)} collective-permute-done((bf16[4,128,128]{2,1,0:T(8,128)(2,1)S(1)}, bf16[4,128,128]{2,1,0:T(8,128)(2,1)S(1)}, u32[]{:S(2)}, u32[]{:S(2)}) %collective-permute-start.16) | collective-permute-done | bytes 131104 | tf_op jit(solution)/shard_map/ppermute | solution.py:31
  63.6 1.8 %collective-permute-done.17 = bf16[4,128,128]{2,1,0:T(8,128)(2,1)S(1)} collective-permute-done((bf16[4,128,128]{2,1,0:T(8,128)(2,1)S(1)}, bf16[4,128,128]{2,1,0:T(8,128)(2,1)S(1)}, u32[]{:S(2)}, u32[]{:S(2)}) %collective-permute-start.17) | collective-permute-done | bytes 131104 | tf_op jit(solution)/shard_map/ppermute | solution.py:31
  65.5 1.5 %layer.1 = (bf16[512,256]{1,0:T(8,128)(2,1)}, f32[512,128]{1,0:T(8,128)S(1)}, bf16[512,128]{1,0:T(8,128)(2,1)S(1)}, bf16[272,128]{1,0:T(8,128)(2,1)S(1)}, bf16[272,128]{1,0:T(8,128)(2,1)S(1)}) custom-call(s32[1]{0:T(128)} %bitcast.core, f32[512,128]{1,0:T(8,128)S(1)} %bitcast.24, bf16[512,128]{1,0:T(8,128)(2,1)S(1)} %bitcast.32, ...), custom_call_target="tpu_custom_call" | custom-call | tf_op jit(solution)/shard_map/layer/pallas_call | solution.py:227
  67.0 1.3 collective-permute-done.18
  68.3 0.1 collective-permute-start.19
  68.4 2.1 %collective-permute-start.20 = (bf16[784,128]{1,0:T(8,128)(2,1)S(1)}, bf16[784,128]{1,0:T(8,128)(2,1)S(1)}, u32[]{:S(2)}, u32[]{:S(2)}) collective-permute-start(bf16[784,128]{1,0:T(8,128)(2,1)S(1)} %pad_maximum_fusion), channel_id=1, source_target_pairs={{0,16},{1,5},{2,18},{3,7},{4,20},{5,1},{6,22},{7,3},{8,24},{9,13},... | collective-permute-start | bytes 602120 | tf_op jit(solution)/shard_map/ppermute | solution.py:31
  70.6 2.6 %collective-permute-start.21 = (bf16[784,128]{1,0:T(8,128)(2,1)S(1)}, bf16[784,128]{1,0:T(8,128)(2,1)S(1)}, u32[]{:S(2)}, u32[]{:S(2)}) collective-permute-start(bf16[784,128]{1,0:T(8,128)(2,1)S(1)} %pad_maximum_fusion), channel_id=1, source_target_pairs={{0,24},{1,7},{2,26},{3,5},{4,28},{5,3},{6,30},{7,1},{8,16},{9,15},... | collective-permute-start | bytes 602120 | tf_op jit(solution)/shard_map/ppermute | solution.py:31
  73.2 0.9 collective-permute-done.19
  74.1 2.3 %collective-permute-done.20 = bf16[784,128]{1,0:T(8,128)(2,1)S(1)} collective-permute-done((bf16[784,128]{1,0:T(8,128)(2,1)S(1)}, bf16[784,128]{1,0:T(8,128)(2,1)S(1)}, u32[]{:S(2)}, u32[]{:S(2)}) %collective-permute-start.20) | collective-permute-done | bytes 200736 | tf_op jit(solution)/shard_map/ppermute | solution.py:31
  76.4 2.0 %collective-permute-done.21 = bf16[784,128]{1,0:T(8,128)(2,1)S(1)} collective-permute-done((bf16[784,128]{1,0:T(8,128)(2,1)S(1)}, bf16[784,128]{1,0:T(8,128)(2,1)S(1)}, u32[]{:S(2)}, u32[]{:S(2)}) %collective-permute-start.21) | collective-permute-done | bytes 200736 | tf_op jit(solution)/shard_map/ppermute | solution.py:31
  78.6 2.9 %collective-permute-start.23 = (bf16[2320,128]{1,0:T(8,128)(2,1)S(1)}, bf16[2320,128]{1,0:T(8,128)(2,1)S(1)}, u32[]{:S(2)}, u32[]{:S(2)}) collective-permute-start(bf16[2320,128]{1,0:T(8,128)(2,1)S(1)} %get-tuple-element.88.rest_0_), channel_id=1, source_target_pairs={{0,4},{1,17},{2,6},{3,19},{4,0},{5,21},{6,2},{7,23},{8,12},{9,25},... | collective-permute-start | bytes 1781768 | tf_op jit(solution)/shard_map/ppermute | solution.py:31
  81.5 1.8 %collective-permute-start.24 = (bf16[2320,128]{1,0:T(8,128)(2,1)S(1)}, bf16[2320,128]{1,0:T(8,128)(2,1)S(1)}, u32[]{:S(2)}, u32[]{:S(2)}) collective-permute-start(bf16[2320,128]{1,0:T(8,128)(2,1)S(1)} %get-tuple-element.88.rest_0_), channel_id=1, source_target_pairs={{0,6},{1,25},{2,4},{3,27},{4,2},{5,29},{6,0},{7,31},{8,14},{9,17},... | collective-permute-start | bytes 1781768 | tf_op jit(solution)/shard_map/ppermute | solution.py:31
  83.3 5.2 %collective-permute-done.22.rest_1_ = bf16[2320,128]{1,0:T(8,128)(2,1)S(1)} collective-permute-done((bf16[2320,128]{1,0:T(8,128)(2,1)S(1)}, bf16[2320,128]{1,0:T(8,128)(2,1)S(1)}, u32[]{:S(2)}, u32[]{:S(2)}) %collective-permute-start.22) | collective-permute-done | bytes 593952 | tf_op jit(solution)/shard_map/ppermute | solution.py:31
  88.6 7.3 %collective-permute-done.23.rest_2_ = bf16[2320,128]{1,0:T(8,128)(2,1)S(1)} collective-permute-done((bf16[2320,128]{1,0:T(8,128)(2,1)S(1)}, bf16[2320,128]{1,0:T(8,128)(2,1)S(1)}, u32[]{:S(2)}, u32[]{:S(2)}) %collective-permute-start.23) | collective-permute-done | bytes 593952 | tf_op jit(solution)/shard_map/ppermute | solution.py:31
  95.9 3.1 %collective-permute-done.24.rest_3_ = bf16[2320,128]{1,0:T(8,128)(2,1)S(1)} collective-permute-done((bf16[2320,128]{1,0:T(8,128)(2,1)S(1)}, bf16[2320,128]{1,0:T(8,128)(2,1)S(1)}, u32[]{:S(2)}, u32[]{:S(2)}) %collective-permute-start.24) | collective-permute-done | bytes 593952 | tf_op jit(solution)/shard_map/ppermute | solution.py:31
  99.1 1.6 %collective-permute-start.25 = (bf16[272,128]{1,0:T(8,128)(2,1)S(1)}, bf16[272,128]{1,0:T(8,128)(2,1)S(1)}, u32[]{:S(2)}, u32[]{:S(2)}) collective-permute-start(bf16[272,128]{1,0:T(8,128)(2,1)S(1)} %add_convert_fusion.6), channel_id=1, source_target_pairs={{0,32},{32,0},{64,96},{96,64},{128,160},{160,128},{192,224},{224,1... | collective-permute-start | bytes 208904 | tf_op jit(solution)/shard_map/ppermute | solution.py:39
  100.7 5.2 %collective-permute-start.26 = (bf16[272,128]{1,0:T(8,128)(2,1)S(1)}, bf16[272,128]{1,0:T(8,128)(2,1)S(1)}, u32[]{:S(2)}, u32[]{:S(2)}) collective-permute-start(bf16[272,128]{1,0:T(8,128)(2,1)S(1)} %add_convert_fusion.6), channel_id=1, source_target_pairs={{0,128},{32,160},{64,192},{96,224},{128,0},{160,32},{192,64},{224,... | collective-permute-start | bytes 208904 | tf_op jit(solution)/shard_map/ppermute | solution.py:39
  105.9 8.6 %tiles_backward.1 = (f32[4,128,128]{2,1,0:T(8,128)S(1)}, bf16[4,128,128]{2,1,0:T(8,128)(2,1)S(1)}, bf16[4,128,128]{2,1,0:T(8,128)(2,1)S(1)}, bf16[4,128,128]{2,1...) custom-call(s32[1]{0:T(128)} %bitcast.22.count, ...), custom_call_target="tpu_custom_call" | custom-call | flops 1073741824 | bytes 16777216 | tf_op jit(solution)/shard_map/tiles_backward/pallas_call | solution.py:171
  114.6 0.7 copy-done.4
  115.3 6.1 %collective-permute-start.40 = (bf16[272,128]{1,0:T(8,128)(2,1)S(1)}, bf16[272,128]{1,0:T(8,128)(2,1)S(1)}, u32[]{:S(2)}, u32[]{:S(2)}) collective-permute-start(bf16[272,128]{1,0:T(8,128)(2,1)S(1)} %add_convert_fusion.5), channel_id=1, source_target_pairs={{0,64},{32,96},{64,0},{96,32},{128,192},{160,224},{192,128},{224,1... | collective-permute-start | bytes 208904 | tf_op jit(solution)/shard_map/ppermute | solution.py:39
  121.5 1.5 %collective-permute-start.38 = (bf16[2,128,128]{2,1,0:T(8,128)(2,1)S(1)}, bf16[2,128,128]{2,1,0:T(8,128)(2,1)S(1)}, u32[]{:S(2)}, u32[]{:S(2)}) collective-permute-start(bf16[2,128,128]{2,1,0:T(8,128)(2,1)S(1)} %get-tuple-element.74), channel_id=1, source_target_pairs={{0,192},{32,224},{64,0},{96,32},{128,64},{160,96},{192,128},{224,1... | collective-permute-start | bytes 196616 | tf_op jit(solution)/shard_map/ppermute | solution.py:35
  123.0 1.5 %collective-permute-start.34 = (bf16[4,128,128]{2,1,0:T(8,128)(2,1)S(1)}, bf16[4,128,128]{2,1,0:T(8,128)(2,1)S(1)}, u32[]{:S(2)}, u32[]{:S(2)}) collective-permute-start(bf16[4,128,128]{2,1,0:T(8,128)(2,1)S(1)} %get-tuple-element.70), channel_id=1, source_target_pairs={{0,32},{32,64},{64,96},{96,128},{128,160},{160,192},{192,224},{224... | collective-permute-start | bytes 393224 | tf_op jit(solution)/shard_map/ppermute | solution.py:35
  124.5 3.1 %collective-permute-start.35 = (bf16[2,128,128]{2,1,0:T(8,128)(2,1)S(1)}, bf16[2,128,128]{2,1,0:T(8,128)(2,1)S(1)}, u32[]{:S(2)}, u32[]{:S(2)}) collective-permute-start(bf16[2,128,128]{2,1,0:T(8,128)(2,1)S(1)} %get-tuple-element.71), channel_id=1, source_target_pairs={{0,64},{32,96},{64,128},{96,160},{128,192},{160,224},{192,0},{224,... | collective-permute-start | bytes 196616 | tf_op jit(solution)/shard_map/ppermute | solution.py:35
  127.7 1.0 collective-permute-done.38
  128.7 2.4 %collective-permute-start.33 = (bf16[4,128,128]{2,1,0:T(8,128)(2,1)S(1)}, bf16[4,128,128]{2,1,0:T(8,128)(2,1)S(1)}, u32[]{:S(2)}, u32[]{:S(2)}) collective-permute-start(bf16[4,128,128]{2,1,0:T(8,128)(2,1)S(1)} %get-tuple-element.68), channel_id=1, source_target_pairs={{0,224},{32,0},{64,32},{96,64},{128,96},{160,128},{192,160},{224,1... | collective-permute-start | bytes 393224 | tf_op jit(solution)/shard_map/ppermute | solution.py:35
  131.2 2.8 %collective-permute-done.35 = bf16[2,128,128]{2,1,0:T(8,128)(2,1)S(1)} collective-permute-done((bf16[2,128,128]{2,1,0:T(8,128)(2,1)S(1)}, bf16[2,128,128]{2,1,0:T(8,128)(2,1)S(1)}, u32[]{:S(2)}, u32[]{:S(2)}) %collective-permute-start.35) | collective-permute-done | bytes 65568 | tf_op jit(solution)/shard_map/ppermute | solution.py:35
  134.0 0.4 collective-permute-start.39
  134.4 2.6 %collective-permute-start.36 = (bf16[4,128,128]{2,1,0:T(8,128)(2,1)S(1)}, bf16[4,128,128]{2,1,0:T(8,128)(2,1)S(1)}, u32[]{:S(2)}, u32[]{:S(2)}) collective-permute-start(bf16[4,128,128]{2,1,0:T(8,128)(2,1)S(1)} %add_convert_fusion.4), channel_id=1, source_target_pairs={{0,64},{32,96},{64,128},{96,160},{128,192},{160,224},{192,0},{224,... | collective-permute-start | bytes 393224 | tf_op jit(solution)/shard_map/ppermute | solution.py:35
  137.1 4.9 %collective-permute-done.39.b2 = bf16[4,128,128]{2,1,0:T(8,128)(2,1)S(1)} collective-permute-done((bf16[4,128,128]{2,1,0:T(8,128)(2,1)S(1)}, bf16[4,128,128]{2,1,0:T(8,128)(2,1)S(1)}, u32[]{:S(2)}, u32[]{:S(2)}) %collective-permute-start.39) | collective-permute-done | bytes 131104 | tf_op jit(solution)/shard_map/ppermute | solution.py:35
  142.0 1.1 collective-permute-done.36.f2
  143.1 0.6 copy-done.13
  143.7 2.2 %finish.1 = (f32[512,128]{1,0:T(8,128)}, f32[128,256]{1,0:T(8,128)}, f32[128,256]{1,0:T(8,128)}, f32[2,128]{1,0:T(2,128)}) custom-call(s32[1]{0:T(128)} %bitcast.core, f32[1]{0:T(128)} %constant.133.clone.1.scale, f32[512,128]{1,0:T(8,128)} %copy-done.3, f32[4,128,128]{2,1,0:T(8,128)} %copy-done.4, bf16[4,128,128]{2,1,0:T(8,128)(2,1)} %copy-done.10, ...), custom_call_target="tpu_custom_call" | custom-call | tf_op jit(solution)/shard_map/finish/pallas_call | solution.py:254
  (74 shorter events, 0.7 us)
Async XLA Ops:
  0.6 12.5 %collective-permute-start.3 = (bf16[512,128]{1,0:T(8,128)(2,1)}, bf16[512,128]{1,0:T(8,128)(2,1)S(1)}, u32[]{:S(2)}, u32[]{:S(2)}) collective-permute-start(bf16[512,128]{1,0:T(8,128)(2,1)} %feats.1), channel_id=1, source_target_pairs={{0,64},{32,96},{64,128},{96,160},{128,192},{160,224},{192,0},{224,... | collective-permute-start | bytes 393224 | tf_op jit(solution)/shard_map/ppermute | solution.py:35
  4.0 9.2 %collective-permute-start.1 = (bf16[512,128]{1,0:T(8,128)(2,1)}, bf16[512,128]{1,0:T(8,128)(2,1)S(1)}, u32[]{:S(2)}, u32[]{:S(2)}) collective-permute-start(bf16[512,128]{1,0:T(8,128)(2,1)} %feats.1), channel_id=1, source_target_pairs={{0,192},{32,224},{64,0},{96,32},{128,64},{160,96},{192,128},{224,1... | collective-permute-start | bytes 393224 | tf_op jit(solution)/shard_map/ppermute | solution.py:35
  6.2 12.0 %collective-permute-start.6 = (bf16[512,128]{1,0:T(8,128)(2,1)}, bf16[512,128]{1,0:T(8,128)(2,1)S(1)}, u32[]{:S(2)}, u32[]{:S(2)}) collective-permute-start(bf16[512,128]{1,0:T(8,128)(2,1)} %feats.1), channel_id=1, source_target_pairs={{0,32},{32,64},{64,96},{96,128},{128,160},{160,192},{192,224},{224... | collective-permute-start | bytes 393224 | tf_op jit(solution)/shard_map/ppermute | solution.py:35
  7.1 13.0 %collective-permute-start = (bf16[512,128]{1,0:T(8,128)(2,1)}, bf16[512,128]{1,0:T(8,128)(2,1)S(1)}, u32[]{:S(2)}, u32[]{:S(2)}) collective-permute-start(bf16[512,128]{1,0:T(8,128)(2,1)} %feats.1), channel_id=1, source_target_pairs={{0,224},{32,0},{64,32},{96,64},{128,96},{160,128},{192,160},{224,1... | collective-permute-start | bytes 393224 | tf_op jit(solution)/shard_map/ppermute | solution.py:35
  13.2 7.0 %collective-permute-start.4 = (bf16[256,128]{1,0:T(8,128)(2,1)S(1)}, bf16[256,128]{1,0:T(8,128)(2,1)S(1)}, u32[]{:S(2)}, u32[]{:S(2)}) collective-permute-start(bf16[256,128]{1,0:T(8,128)(2,1)S(1)} %slice.63), channel_id=1, source_target_pairs={{0,64},{32,96},{64,128},{96,160},{128,192},{160,224},{192,0},{224,... | collective-permute-start | bytes 196616 | tf_op jit(solution)/shard_map/ppermute | solution.py:35
  13.2 7.1 %collective-permute-start.7 = (bf16[256,128]{1,0:T(8,128)(2,1)S(1)}, bf16[256,128]{1,0:T(8,128)(2,1)S(1)}, u32[]{:S(2)}, u32[]{:S(2)}) collective-permute-start(bf16[256,128]{1,0:T(8,128)(2,1)S(1)} %slice.64), channel_id=1, source_target_pairs={{0,192},{32,224},{64,0},{96,32},{128,64},{160,96},{192,128},{224,1... | collective-permute-start | bytes 196616 | tf_op jit(solution)/shard_map/ppermute | solution.py:35
  17.4 5.0 %collective-permute-start.5 = (bf16[512,128]{1,0:T(8,128)(2,1)S(1)}, bf16[512,128]{1,0:T(8,128)(2,1)S(1)}, u32[]{:S(2)}, u32[]{:S(2)}) collective-permute-start(bf16[512,128]{1,0:T(8,128)(2,1)S(1)} %collective-permute-done.3), channel_id=1, source_target_pairs={{0,32},{32,64},{64,96},{96,128},{128,160},{160,192},{192,224},{224... | collective-permute-start | bytes 393224 | tf_op jit(solution)/shard_map/ppermute | solution.py:35
  18.2 5.2 %collective-permute-start.2 = (bf16[512,128]{1,0:T(8,128)(2,1)S(1)}, bf16[512,128]{1,0:T(8,128)(2,1)S(1)}, u32[]{:S(2)}, u32[]{:S(2)}) collective-permute-start(bf16[512,128]{1,0:T(8,128)(2,1)S(1)} %collective-permute-done.1), channel_id=1, source_target_pairs={{0,224},{32,0},{64,32},{96,64},{128,96},{160,128},{192,160},{224,1... | collective-permute-start | bytes 393224 | tf_op jit(solution)/shard_map/ppermute | solution.py:35
  23.4 0.9 copy-start
  24.3 41.2 %copy-start.1 = (bf16[512,128]{1,0:T(8,128)(2,1)S(1)}, bf16[512,128]{1,0:T(8,128)(2,1)}, u32[]{:S(2)}) copy-start(bf16[512,128]{1,0:T(8,128)(2,1)} %feats.1) | copy-start | bytes 393220
  24.3 41.2 %copy-start.2 = (bf16[512,256]{1,0:T(8,128)(2,1)S(1)}, bf16[512,256]{1,0:T(8,128)(2,1)}, u32[]{:S(2)}) copy-start(bf16[512,256]{1,0:T(8,128)(2,1)} %cot.1) | copy-start | bytes 786436
  24.3 41.2 %copy-start.5 = (bf16[128,256]{1,0:T(8,128)(2,1)S(1)}, bf16[128,256]{1,0:T(8,128)(2,1)}, u32[]{:S(2)}) copy-start(bf16[128,256]{1,0:T(8,128)(2,1)} %w_self.1) | copy-start | bytes 196612
  24.3 41.2 %copy-start.6 = (bf16[128,256]{1,0:T(8,128)(2,1)S(1)}, bf16[128,256]{1,0:T(8,128)(2,1)}, u32[]{:S(2)}) copy-start(bf16[128,256]{1,0:T(8,128)(2,1)} %w_neigh.1) | copy-start | bytes 196612
  24.3 41.2 %copy-start.7 = (f32[256]{0:T(256)S(1)}, f32[256]{0:T(256)}, u32[]{:S(2)}) copy-start(f32[256]{0:T(256)} %param.12) | copy-start | bytes 3076
  33.6 2.0 %collective-permute-start.9 = (bf16[16,128,128]{2,1,0:T(8,128)(2,1)S(1)}, bf16[16,128,128]{2,1,0:T(8,128)(2,1)S(1)}, u32[]{:S(2)}, u32[]{:S(2)}) collective-permute-start(bf16[16,128,128]{2,1,0:T(8,128)(2,1)S(1)} %get-tuple-element.47), channel_id=1, source_target_pairs={{0,1},{1,0},{2,3},{3,2},{4,5},{5,4},{6,7},{7,6},{8,9},{9,8},{10,11... | collective-permute-start | bytes 1572872 | tf_op jit(solution)/shard_map/ppermute | solution.py:27
  33.7 7.3 %collective-permute-start.11 = (bf16[16,128,128]{2,1,0:T(8,128)(2,1)S(1)}, bf16[16,128,128]{2,1,0:T(8,128)(2,1)S(1)}, u32[]{:S(2)}, u32[]{:S(2)}) collective-permute-start(bf16[16,128,128]{2,1,0:T(8,128)(2,1)S(1)} %get-tuple-element.49), channel_id=1, source_target_pairs={{0,1},{1,0},{2,3},{3,2},{4,5},{5,4},{6,7},{7,6},{8,9},{9,8},{10,11... | collective-permute-start | bytes 1572872 | tf_op jit(solution)/shard_map/ppermute | solution.py:27
  34.2 7.1 %collective-permute-start.13 = (bf16[16,128,128]{2,1,0:T(8,128)(2,1)S(1)}, bf16[16,128,128]{2,1,0:T(8,128)(2,1)S(1)}, u32[]{:S(2)}, u32[]{:S(2)}) collective-permute-start(bf16[16,128,128]{2,1,0:T(8,128)(2,1)S(1)} %get-tuple-element.51), channel_id=1, source_target_pairs={{0,1},{1,0},{2,3},{3,2},{4,5},{5,4},{6,7},{7,6},{8,9},{9,8},{10,11... | collective-permute-start | bytes 1572872 | tf_op jit(solution)/shard_map/ppermute | solution.py:27
  34.3 8.3 %collective-permute-start.8 = (bf16[16,128,128]{2,1,0:T(8,128)(2,1)S(1)}, bf16[16,128,128]{2,1,0:T(8,128)(2,1)S(1)}, u32[]{:S(2)}, u32[]{:S(2)}) collective-permute-start(bf16[16,128,128]{2,1,0:T(8,128)(2,1)S(1)} %get-tuple-element.45), channel_id=1, source_target_pairs={{0,1},{1,0},{2,3},{3,2},{4,5},{5,4},{6,7},{7,6},{8,9},{9,8},{10,11... | collective-permute-start | bytes 1572872 | tf_op jit(solution)/shard_map/ppermute | solution.py:27
  35.8 12.5 %collective-permute-start.10 = (bf16[16,128,128]{2,1,0:T(8,128)(2,1)S(1)}, bf16[16,128,128]{2,1,0:T(8,128)(2,1)S(1)}, u32[]{:S(2)}, u32[]{:S(2)}) collective-permute-start(bf16[16,128,128]{2,1,0:T(8,128)(2,1)S(1)} %add_convert_fusion.2), channel_id=1, source_target_pairs={{0,16},{1,5},{2,18},{3,7},{4,20},{5,1},{6,22},{7,3},{8,24},{9,13},... | collective-permute-start | bytes 1572872 | tf_op jit(solution)/shard_map/ppermute | solution.py:31
  41.2 12.2 %collective-permute-start.12 = (bf16[16,128,128]{2,1,0:T(8,128)(2,1)S(1)}, bf16[16,128,128]{2,1,0:T(8,128)(2,1)S(1)}, u32[]{:S(2)}, u32[]{:S(2)}) collective-permute-start(bf16[16,128,128]{2,1,0:T(8,128)(2,1)S(1)} %add_convert_fusion.1), channel_id=1, source_target_pairs={{0,8},{1,3},{2,10},{3,1},{4,12},{5,7},{6,14},{7,5},{8,0},{9,11},{1... | collective-permute-start | bytes 1572872 | tf_op jit(solution)/shard_map/ppermute | solution.py:31
  41.5 12.3 %collective-permute-start.14 = (bf16[16,128,128]{2,1,0:T(8,128)(2,1)S(1)}, bf16[16,128,128]{2,1,0:T(8,128)(2,1)S(1)}, u32[]{:S(2)}, u32[]{:S(2)}) collective-permute-start(bf16[16,128,128]{2,1,0:T(8,128)(2,1)S(1)} %add_convert_fusion), channel_id=1, source_target_pairs={{0,24},{1,7},{2,26},{3,5},{4,28},{5,3},{6,30},{7,1},{8,16},{9,15},... | collective-permute-start | bytes 1572872 | tf_op jit(solution)/shard_map/ppermute | solution.py:31
  54.3 5.2 %collective-permute-start.15 = (bf16[4,128,128]{2,1,0:T(8,128)(2,1)S(1)}, bf16[4,128,128]{2,1,0:T(8,128)(2,1)S(1)}, u32[]{:S(2)}, u32[]{:S(2)}) collective-permute-start(bf16[4,128,128]{2,1,0:T(8,128)(2,1)S(1)} %get-tuple-element.94), channel_id=1, source_target_pairs={{0,2},{1,9},{2,0},{3,11},{4,6},{5,13},{6,4},{7,15},{8,10},{9,1},{1... | collective-permute-start | bytes 393224 | tf_op jit(solution)/shard_map/ppermute | solution.py:31
  55.0 8.7 %collective-permute-start.16 = (bf16[4,128,128]{2,1,0:T(8,128)(2,1)S(1)}, bf16[4,128,128]{2,1,0:T(8,128)(2,1)S(1)}, u32[]{:S(2)}, u32[]{:S(2)}) collective-permute-start(bf16[4,128,128]{2,1,0:T(8,128)(2,1)S(1)} %get-tuple-element.93), channel_id=1, source_target_pairs={{0,4},{1,17},{2,6},{3,19},{4,0},{5,21},{6,2},{7,23},{8,12},{9,25},... | collective-permute-start | bytes 393224 | tf_op jit(solution)/shard_map/ppermute | solution.py:31
  59.3 6.2 %collective-permute-start.17 = (bf16[4,128,128]{2,1,0:T(8,128)(2,1)S(1)}, bf16[4,128,128]{2,1,0:T(8,128)(2,1)S(1)}, u32[]{:S(2)}, u32[]{:S(2)}) collective-permute-start(bf16[4,128,128]{2,1,0:T(8,128)(2,1)S(1)} %get-tuple-element.92), channel_id=1, source_target_pairs={{0,6},{1,25},{2,4},{3,27},{4,2},{5,29},{6,0},{7,31},{8,14},{9,17},... | collective-permute-start | bytes 393224 | tf_op jit(solution)/shard_map/ppermute | solution.py:31
  67.0 11.5 %copy-start.3 = (f32[512,128]{1,0:T(8,128)}, f32[512,128]{1,0:T(8,128)S(1)}, u32[]{:S(2)}) copy-start(f32[512,128]{1,0:T(8,128)S(1)} %get-tuple-element.53.base) | copy-start | bytes 786436
  67.0 1.3 collective-permute-start.18
  68.3 5.8 %collective-permute-start.19 = (bf16[784,128]{1,0:T(8,128)(2,1)S(1)}, bf16[784,128]{1,0:T(8,128)(2,1)S(1)}, u32[]{:S(2)}, u32[]{:S(2)}) collective-permute-start(bf16[784,128]{1,0:T(8,128)(2,1)S(1)} %pad_maximum_fusion), channel_id=1, source_target_pairs={{0,8},{1,3},{2,10},{3,1},{4,12},{5,7},{6,14},{7,5},{8,0},{9,11},{1... | collective-permute-start | bytes 602120 | tf_op jit(solution)/shard_map/ppermute | solution.py:31
  68.4 8.0 %collective-permute-start.20 = (bf16[784,128]{1,0:T(8,128)(2,1)S(1)}, bf16[784,128]{1,0:T(8,128)(2,1)S(1)}, u32[]{:S(2)}, u32[]{:S(2)}) collective-permute-start(bf16[784,128]{1,0:T(8,128)(2,1)S(1)} %pad_maximum_fusion), channel_id=1, source_target_pairs={{0,16},{1,5},{2,18},{3,7},{4,20},{5,1},{6,22},{7,3},{8,24},{9,13},... | collective-permute-start | bytes 602120 | tf_op jit(solution)/shard_map/ppermute | solution.py:31
  70.6 7.9 %collective-permute-start.21 = (bf16[784,128]{1,0:T(8,128)(2,1)S(1)}, bf16[784,128]{1,0:T(8,128)(2,1)S(1)}, u32[]{:S(2)}, u32[]{:S(2)}) collective-permute-start(bf16[784,128]{1,0:T(8,128)(2,1)S(1)} %pad_maximum_fusion), channel_id=1, source_target_pairs={{0,24},{1,7},{2,26},{3,5},{4,28},{5,3},{6,30},{7,1},{8,16},{9,15},... | collective-permute-start | bytes 602120 | tf_op jit(solution)/shard_map/ppermute | solution.py:31
  78.5 10.0 %collective-permute-start.22 = (bf16[2320,128]{1,0:T(8,128)(2,1)S(1)}, bf16[2320,128]{1,0:T(8,128)(2,1)S(1)}, u32[]{:S(2)}, u32[]{:S(2)}) collective-permute-start(bf16[2320,128]{1,0:T(8,128)(2,1)S(1)} %get-tuple-element.88.rest_0_), channel_id=1, source_target_pairs={{0,2},{1,9},{2,0},{3,11},{4,6},{5,13},{6,4},{7,15},{8,10},{9,1},{1... | collective-permute-start | bytes 1781768 | tf_op jit(solution)/shard_map/ppermute | solution.py:31
  78.6 17.2 %collective-permute-start.23 = (bf16[2320,128]{1,0:T(8,128)(2,1)S(1)}, bf16[2320,128]{1,0:T(8,128)(2,1)S(1)}, u32[]{:S(2)}, u32[]{:S(2)}) collective-permute-start(bf16[2320,128]{1,0:T(8,128)(2,1)S(1)} %get-tuple-element.88.rest_0_), channel_id=1, source_target_pairs={{0,4},{1,17},{2,6},{3,19},{4,0},{5,21},{6,2},{7,23},{8,12},{9,25},... | collective-permute-start | bytes 1781768 | tf_op jit(solution)/shard_map/ppermute | solution.py:31
  81.5 17.5 %collective-permute-start.24 = (bf16[2320,128]{1,0:T(8,128)(2,1)S(1)}, bf16[2320,128]{1,0:T(8,128)(2,1)S(1)}, u32[]{:S(2)}, u32[]{:S(2)}) collective-permute-start(bf16[2320,128]{1,0:T(8,128)(2,1)S(1)} %get-tuple-element.88.rest_0_), channel_id=1, source_target_pairs={{0,6},{1,25},{2,4},{3,27},{4,2},{5,29},{6,0},{7,31},{8,14},{9,17},... | collective-permute-start | bytes 1781768 | tf_op jit(solution)/shard_map/ppermute | solution.py:31
  83.3 17.4 %collective-permute-start.28 = (bf16[2320,128]{1,0:T(8,128)(2,1)S(1)}, bf16[2320,128]{1,0:T(8,128)(2,1)S(1)}, u32[]{:S(2)}, u32[]{:S(2)}) collective-permute-start(bf16[2320,128]{1,0:T(8,128)(2,1)S(1)} %get-tuple-element.88.rest_0_), channel_id=1, source_target_pairs={{0,1},{1,0},{2,3},{3,2},{4,5},{5,4},{6,7},{7,6},{8,9},{9,8},{10,11... | collective-permute-start | bytes 1781768 | tf_op jit(solution)/shard_map/ppermute | solution.py:27
  88.6 17.4 %collective-permute-start.29 = (bf16[2320,128]{1,0:T(8,128)(2,1)S(1)}, bf16[2320,128]{1,0:T(8,128)(2,1)S(1)}, u32[]{:S(2)}, u32[]{:S(2)}) collective-permute-start(bf16[2320,128]{1,0:T(8,128)(2,1)S(1)} %collective-permute-done.22.rest_1_), channel_id=1, source_target_pairs={{0,1},{1,0},{2,3},{3,2},{4,5},{5,4},{6,7},{7,6},{8,9},{9,8},{10,11... | collective-permute-start | bytes 1781768 | tf_op jit(solution)/shard_map/ppermute | solution.py:27
  95.9 10.0 %collective-permute-start.30 = (bf16[2320,128]{1,0:T(8,128)(2,1)S(1)}, bf16[2320,128]{1,0:T(8,128)(2,1)S(1)}, u32[]{:S(2)}, u32[]{:S(2)}) collective-permute-start(bf16[2320,128]{1,0:T(8,128)(2,1)S(1)} %collective-permute-done.23.rest_2_), channel_id=1, source_target_pairs={{0,1},{1,0},{2,3},{3,2},{4,5},{5,4},{6,7},{7,6},{8,9},{9,8},{10,11... | collective-permute-start | bytes 1781768 | tf_op jit(solution)/shard_map/ppermute | solution.py:27
  99.0 6.9 %collective-permute-start.31 = (bf16[2320,128]{1,0:T(8,128)(2,1)S(1)}, bf16[2320,128]{1,0:T(8,128)(2,1)S(1)}, u32[]{:S(2)}, u32[]{:S(2)}) collective-permute-start(bf16[2320,128]{1,0:T(8,128)(2,1)S(1)} %collective-permute-done.24.rest_3_), channel_id=1, source_target_pairs={{0,1},{1,0},{2,3},{3,2},{4,5},{5,4},{6,7},{7,6},{8,9},{9,8},{10,11... | collective-permute-start | bytes 1781768 | tf_op jit(solution)/shard_map/ppermute | solution.py:27
  99.1 16.2 %collective-permute-start.25 = (bf16[272,128]{1,0:T(8,128)(2,1)S(1)}, bf16[272,128]{1,0:T(8,128)(2,1)S(1)}, u32[]{:S(2)}, u32[]{:S(2)}) collective-permute-start(bf16[272,128]{1,0:T(8,128)(2,1)S(1)} %add_convert_fusion.6), channel_id=1, source_target_pairs={{0,32},{32,0},{64,96},{96,64},{128,160},{160,128},{192,224},{224,1... | collective-permute-start | bytes 208904 | tf_op jit(solution)/shard_map/ppermute | solution.py:39
  100.7 14.6 %collective-permute-start.26 = (bf16[272,128]{1,0:T(8,128)(2,1)S(1)}, bf16[272,128]{1,0:T(8,128)(2,1)S(1)}, u32[]{:S(2)}, u32[]{:S(2)}) collective-permute-start(bf16[272,128]{1,0:T(8,128)(2,1)S(1)} %add_convert_fusion.6), channel_id=1, source_target_pairs={{0,128},{32,160},{64,192},{96,224},{128,0},{160,32},{192,64},{224,... | collective-permute-start | bytes 208904 | tf_op jit(solution)/shard_map/ppermute | solution.py:39
  105.9 9.4 %collective-permute-start.27 = (bf16[272,128]{1,0:T(8,128)(2,1)S(1)}, bf16[272,128]{1,0:T(8,128)(2,1)S(1)}, u32[]{:S(2)}, u32[]{:S(2)}) collective-permute-start(bf16[272,128]{1,0:T(8,128)(2,1)S(1)} %add_convert_fusion.6), channel_id=1, source_target_pairs={{0,160},{32,128},{64,224},{96,192},{128,32},{160,0},{192,96},{224,... | collective-permute-start | bytes 208904 | tf_op jit(solution)/shard_map/ppermute | solution.py:39
  114.5 0.7 copy-start.4
  115.3 12.3 %collective-permute-start.40 = (bf16[272,128]{1,0:T(8,128)(2,1)S(1)}, bf16[272,128]{1,0:T(8,128)(2,1)S(1)}, u32[]{:S(2)}, u32[]{:S(2)}) collective-permute-start(bf16[272,128]{1,0:T(8,128)(2,1)S(1)} %add_convert_fusion.5), channel_id=1, source_target_pairs={{0,64},{32,96},{64,0},{96,32},{128,192},{160,224},{192,128},{224,1... | collective-permute-start | bytes 208904 | tf_op jit(solution)/shard_map/ppermute | solution.py:39
  121.5 9.7 %collective-permute-start.37 = (bf16[4,128,128]{2,1,0:T(8,128)(2,1)S(1)}, bf16[4,128,128]{2,1,0:T(8,128)(2,1)S(1)}, u32[]{:S(2)}, u32[]{:S(2)}) collective-permute-start(bf16[4,128,128]{2,1,0:T(8,128)(2,1)S(1)} %get-tuple-element.73), channel_id=1, source_target_pairs={{0,224},{32,0},{64,32},{96,64},{128,96},{160,128},{192,160},{224,1... | collective-permute-start | bytes 393224 | tf_op jit(solution)/shard_map/ppermute | solution.py:35
  121.5 7.2 %collective-permute-start.38 = (bf16[2,128,128]{2,1,0:T(8,128)(2,1)S(1)}, bf16[2,128,128]{2,1,0:T(8,128)(2,1)S(1)}, u32[]{:S(2)}, u32[]{:S(2)}) collective-permute-start(bf16[2,128,128]{2,1,0:T(8,128)(2,1)S(1)} %get-tuple-element.74), channel_id=1, source_target_pairs={{0,192},{32,224},{64,0},{96,32},{128,64},{160,96},{192,128},{224,1... | collective-permute-start | bytes 196616 | tf_op jit(solution)/shard_map/ppermute | solution.py:35
  123.0 11.4 %collective-permute-start.34 = (bf16[4,128,128]{2,1,0:T(8,128)(2,1)S(1)}, bf16[4,128,128]{2,1,0:T(8,128)(2,1)S(1)}, u32[]{:S(2)}, u32[]{:S(2)}) collective-permute-start(bf16[4,128,128]{2,1,0:T(8,128)(2,1)S(1)} %get-tuple-element.70), channel_id=1, source_target_pairs={{0,32},{32,64},{64,96},{96,128},{128,160},{160,192},{192,224},{224... | collective-permute-start | bytes 393224 | tf_op jit(solution)/shard_map/ppermute | solution.py:35
  124.5 9.5 %collective-permute-start.35 = (bf16[2,128,128]{2,1,0:T(8,128)(2,1)S(1)}, bf16[2,128,128]{2,1,0:T(8,128)(2,1)S(1)}, u32[]{:S(2)}, u32[]{:S(2)}) collective-permute-start(bf16[2,128,128]{2,1,0:T(8,128)(2,1)S(1)} %get-tuple-element.71), channel_id=1, source_target_pairs={{0,64},{32,96},{64,128},{96,160},{128,192},{160,224},{192,0},{224,... | collective-permute-start | bytes 196616 | tf_op jit(solution)/shard_map/ppermute | solution.py:35
  127.6 9.4 %collective-permute-start.32 = (bf16[4,128,128]{2,1,0:T(8,128)(2,1)S(1)}, bf16[4,128,128]{2,1,0:T(8,128)(2,1)S(1)}, u32[]{:S(2)}, u32[]{:S(2)}) collective-permute-start(bf16[4,128,128]{2,1,0:T(8,128)(2,1)S(1)} %get-tuple-element.67), channel_id=1, source_target_pairs={{0,32},{32,64},{64,96},{96,128},{128,160},{160,192},{192,224},{224... | collective-permute-start | bytes 393224 | tf_op jit(solution)/shard_map/ppermute | solution.py:35
  127.6 15.4 %copy-start.8 = (f32[272,128]{1,0:T(8,128)}, f32[272,128]{1,0:T(8,128)S(1)}, u32[]{:S(2)}) copy-start(f32[272,128]{1,0:T(8,128)S(1)} %convert_add_fusion.mine) | copy-start | bytes 417796
  128.7 8.3 %collective-permute-start.33 = (bf16[4,128,128]{2,1,0:T(8,128)(2,1)S(1)}, bf16[4,128,128]{2,1,0:T(8,128)(2,1)S(1)}, u32[]{:S(2)}, u32[]{:S(2)}) collective-permute-start(bf16[4,128,128]{2,1,0:T(8,128)(2,1)S(1)} %get-tuple-element.68), channel_id=1, source_target_pairs={{0,224},{32,0},{64,32},{96,64},{128,96},{160,128},{192,160},{224,1... | collective-permute-start | bytes 393224 | tf_op jit(solution)/shard_map/ppermute | solution.py:35
  131.1 5.9 %collective-permute-start.41 = (f32[272,128]{1,0:T(8,128)S(1)}, f32[272,128]{1,0:T(8,128)S(1)}, u32[]{:S(2)}, u32[]{:S(2)}) collective-permute-start(f32[272,128]{1,0:T(8,128)S(1)} %convert_add_fusion.mine), channel_id=1, source_target_pairs={{0,1},{1,0},{2,3},{3,2},{4,5},{5,4},{6,7},{7,6},{8,9},{9,8},{10,11... | collective-permute-start | bytes 417800 | tf_op jit(solution)/shard_map/ppermute | solution.py:27
  134.0 8.0 %collective-permute-start.39 = (bf16[4,128,128]{2,1,0:T(8,128)(2,1)S(1)}, bf16[4,128,128]{2,1,0:T(8,128)(2,1)S(1)}, u32[]{:S(2)}, u32[]{:S(2)}) collective-permute-start(bf16[4,128,128]{2,1,0:T(8,128)(2,1)S(1)} %add_convert_fusion.3), channel_id=1, source_target_pairs={{0,192},{32,224},{64,0},{96,32},{128,64},{160,96},{192,128},{224,1... | collective-permute-start | bytes 393224 | tf_op jit(solution)/shard_map/ppermute | solution.py:35
  134.4 8.6 %collective-permute-start.36 = (bf16[4,128,128]{2,1,0:T(8,128)(2,1)S(1)}, bf16[4,128,128]{2,1,0:T(8,128)(2,1)S(1)}, u32[]{:S(2)}, u32[]{:S(2)}) collective-permute-start(bf16[4,128,128]{2,1,0:T(8,128)(2,1)S(1)} %add_convert_fusion.4), channel_id=1, source_target_pairs={{0,64},{32,96},{64,128},{96,160},{128,192},{160,224},{192,0},{224,... | collective-permute-start | bytes 393224 | tf_op jit(solution)/shard_map/ppermute | solution.py:35
  137.0 6.0 %copy-start.10 = (bf16[4,128,128]{2,1,0:T(8,128)(2,1)}, bf16[4,128,128]{2,1,0:T(8,128)(2,1)S(1)}, u32[]{:S(2)}) copy-start(bf16[4,128,128]{2,1,0:T(8,128)(2,1)S(1)} %collective-permute-done.32.f1) | copy-start | bytes 393220
  137.0 6.0 %copy-start.11 = (bf16[4,128,128]{2,1,0:T(8,128)(2,1)}, bf16[4,128,128]{2,1,0:T(8,128)(2,1)S(1)}, u32[]{:S(2)}) copy-start(bf16[4,128,128]{2,1,0:T(8,128)(2,1)S(1)} %collective-permute-done.33.b1) | copy-start | bytes 393220
  137.0 6.0 %copy-start.9 = (f32[272,128]{1,0:T(8,128)}, f32[272,128]{1,0:T(8,128)S(1)}, u32[]{:S(2)}) copy-start(f32[272,128]{1,0:T(8,128)S(1)} %collective-permute-done.41.theirs) | copy-start | bytes 417796
  141.9 1.1 copy-start.12
  143.0 0.7 copy-start.13

commit v3 on v2

--- a/solution.py
+++ b/solution.py
@@ -318,14 +318,14 @@
         own[k] = axis_move(bundle, 1, k)
     far = [other_core(v) for v in own]
     gw = wide_sum([v[4 * rows_dev :] for v in own]).astype(BF)
-    swapped = [row_swap(gw, bits) for bits in (1, 4, 5)]
+    swapped = [row_swap(gw, bits) for bits in (2, 4, 6)]
 
     p = backward(count, section_place, slab_source, tiles, own + far)
     gw, swapped, p = lax.optimization_barrier((gw, swapped, p))
     gw = wide_sum([gw] + swapped).astype(BF)
     up3, down3 = row_move(p[3], 1), row_move(p[5], -1)
     up4, down4 = row_move(p[4], 2), row_move(p[8], -2)
-    swapped = row_swap(gw, 2)
+    swapped = row_swap(gw, 1)
     zeros = jnp.zeros((2, T, T), F32)
     up2 = p[2].astype(F32) + up3.astype(F32) + jnp.concatenate([up4.astype(F32), zeros], axis=0)
     down2 = p[6].astype(F32) + down3.astype(F32) + jnp.concatenate([zeros, down4.astype(F32)], axis=0)

time: 146 us -> 146 us (level)
  starting transfers between devices: 60.6 us -> 55.7 us
  Pallas kernels: 21.6 us -> 25.7 us
    ppermute x4, starting transfers between devices: 13 us -> 10.2 us  [row_swap(): return lax.ppermute(value, 'row', [(i, i ^ bit) for i in range(8)])]
    pallas_call x1, Pallas kernels: 9.3 us -> 11.4 us  [forward(): pl.pallas_call(forward_kernel, out_shape=blocks, in_specs=[SM, SM, SM, HB...]
    pallas_call x1, Pallas kernels: 8.61 us -> 10.6 us  [backward(): pl.pallas_call(backward_kernel, out_shape=outs, in_specs=[SM, SM, SM, HB]...]
    ppermute x12, starting transfers between devices: 21.1 us -> 19.5 us  [axis_move(): lax.ppermute(value, 'rep', [(i, i ^ k * (8 if i % 2 == which else 2)) for...]
  transfers between devices with their start and end apart: 42 -> 42, of which waited for: 22 -> 22; matrix products, arithmetic and copies ran while one was open for 1% -> 1% of each run, Pallas kernels for 6% -> 7%
where the time goes in v3:
time: 146 us
  waiting for transfers between devices  57.8 us (40%)
  starting transfers between devices  55.7 us (38%)
  Pallas kernels  25.7 us (18%)
  other arithmetic  2.62 us (2%)
  local copies, waits for them, and re-layouts  2.42 us (2%)
  between operations  1.61 us (1%)
    ppermute x12, waiting for transfers between devices, axis_move(): lax.ppermute(value, 'rep', [(i, i ^ k * (8 if i % 2 == which else 2)) for...  37.9 us
    ppermute x16, starting transfers between devices, row_move(): return lax.ppermute(value, 'row', [(i, (i + step) % 8) for i in range(8)])  24.9 us
    ppermute x12, starting transfers between devices, axis_move(): lax.ppermute(value, 'rep', [(i, i ^ k * (8 if i % 2 == which else 2)) for...  19.5 us
    ppermute x16, waiting for transfers between devices, row_move(): return lax.ppermute(value, 'row', [(i, (i + step) % 8) for i in range(8)])  17.7 us
    pallas_call x1, Pallas kernels, forward(): pl.pallas_call(forward_kernel, out_shape=blocks, in_specs=[SM, SM, SM, HB...  11.4 us
    pallas_call x1, Pallas kernels, backward(): pl.pallas_call(backward_kernel, out_shape=outs, in_specs=[SM, SM, SM, HB]...  10.6 us
    ppermute x4, starting transfers between devices, row_swap(): return lax.ppermute(value, 'row', [(i, i ^ bit) for i in range(8)])  10.2 us
  transfers between devices with their start and end apart: 42, of which 22 were waited for; matrix products, arithmetic and copies ran while one was open for 1% of the time, Pallas kernels for 7%

profile of v3, /device:TPU:32, one launch (start us, length us, event | category | flops | bytes accessed | tf_op | source)
XLA Modules:
  0.0 145.8 jit_solution(17429109225753288943)
XLA Ops:
  0.6 3.3 %collective-permute-start.3 = (bf16[512,128]{1,0:T(8,128)(2,1)}, bf16[512,128]{1,0:T(8,128)(2,1)S(1)}, u32[]{:S(2)}, u32[]{:S(2)}) collective-permute-start(bf16[512,128]{1,0:T(8,128)(2,1)} %feats.1), channel_id=1, source_target_pairs={{0,64},{32,96},{64,128},{96,160},{128,192},{160,224},{192,0},{224,... | collective-permute-start | bytes 393224 | tf_op jit(solution)/shard_map/ppermute | solution.py:35
  4.0 2.2 %collective-permute-start.1 = (bf16[512,128]{1,0:T(8,128)(2,1)}, bf16[512,128]{1,0:T(8,128)(2,1)S(1)}, u32[]{:S(2)}, u32[]{:S(2)}) collective-permute-start(bf16[512,128]{1,0:T(8,128)(2,1)} %feats.1), channel_id=1, source_target_pairs={{0,192},{32,224},{64,0},{96,32},{128,64},{160,96},{192,128},{224,1... | collective-permute-start | bytes 393224 | tf_op jit(solution)/shard_map/ppermute | solution.py:35
  6.2 0.9 collective-permute-start.6
  7.1 1.1 collective-permute-start
  8.9 0.7 add_add_fusion.1
  9.6 3.5 %collective-permute-done.3 = bf16[512,128]{1,0:T(8,128)(2,1)S(1)} collective-permute-done((bf16[512,128]{1,0:T(8,128)(2,1)}, bf16[512,128]{1,0:T(8,128)(2,1)S(1)}, u32[]{:S(2)}, u32[]{:S(2)}) %collective-permute-start.3) | collective-permute-done | bytes 131104 | tf_op jit(solution)/shard_map/ppermute | solution.py:35
  13.2 4.2 %collective-permute-start.7 = (bf16[256,128]{1,0:T(8,128)(2,1)S(1)}, bf16[256,128]{1,0:T(8,128)(2,1)S(1)}, u32[]{:S(2)}, u32[]{:S(2)}) collective-permute-start(bf16[256,128]{1,0:T(8,128)(2,1)S(1)} %slice.64), channel_id=1, source_target_pairs={{0,192},{32,224},{64,0},{96,32},{128,64},{160,96},{192,128},{224,1... | collective-permute-start | bytes 196616 | tf_op jit(solution)/shard_map/ppermute | solution.py:35
  17.4 0.8 collective-permute-start.5
  18.2 1.2 collective-permute-start.2
  19.4 0.7 fusion.5
  20.1 0.2 collective-permute-done.7
  20.3 2.0 %collective-permute-done.5 = bf16[512,128]{1,0:T(8,128)(2,1)S(1)} collective-permute-done((bf16[512,128]{1,0:T(8,128)(2,1)S(1)}, bf16[512,128]{1,0:T(8,128)(2,1)S(1)}, u32[]{:S(2)}, u32[]{:S(2)}) %collective-permute-start.5) | collective-permute-done | bytes 131104 | tf_op jit(solution)/shard_map/ppermute | solution.py:35
  22.3 1.1 collective-permute-done.2
  23.4 0.9 copy-done
  24.3 11.4 %tiles_forward.1 = (bf16[16,128,128]{2,1,0:T(8,128)(2,1)S(1)}, bf16[16,128,128]{2,1,0:T(8,128)(2,1)S(1)}, bf16[16,128,128]{2,1,0:T(8,128)(2,1)S(1)}, bf16[16,128...) custom-call(s32[1]{0:T(128)} %bitcast.21.count, ...), custom_call_target="tpu_custom_call" | custom-call | flops 1073741824 | bytes 16777216 | tf_op jit(solution)/shard_map/tiles_forward/pallas_call | solution.py:113
  35.9 0.5 collective-permute-start.11
  36.5 0.4 collective-permute-start.8
  36.9 0.9 collective-permute-done.9
  37.9 1.1 collective-permute-start.10
  39.2 1.3 collective-permute-start.12
  40.5 0.2 add_convert_fusion
  40.7 2.3 %collective-permute-start.14 = (bf16[16,128,128]{2,1,0:T(8,128)(2,1)S(1)}, bf16[16,128,128]{2,1,0:T(8,128)(2,1)S(1)}, u32[]{:S(2)}, u32[]{:S(2)}) collective-permute-start(bf16[16,128,128]{2,1,0:T(8,128)(2,1)S(1)} %add_convert_fusion), channel_id=1, source_target_pairs={{0,24},{1,7},{2,26},{3,5},{4,28},{5,3},{6,30},{7,1},{8,16},{9,15},... | collective-permute-start | bytes 1572872 | tf_op jit(solution)/shard_map/ppermute | solution.py:31
  43.0 5.8 %collective-permute-done.10 = bf16[16,128,128]{2,1,0:T(8,128)(2,1)S(1)} collective-permute-done((bf16[16,128,128]{2,1,0:T(8,128)(2,1)S(1)}, bf16[16,128,128]{2,1,0:T(8,128)(2,1)S(1)}, u32[]{:S(2)}, u32[]{:S(2)}) %collective-permute-start.10) | collective-permute-done | bytes 524320 | tf_op jit(solution)/shard_map/ppermute | solution.py:31
  48.8 3.8 %collective-permute-done.12 = bf16[16,128,128]{2,1,0:T(8,128)(2,1)S(1)} collective-permute-done((bf16[16,128,128]{2,1,0:T(8,128)(2,1)S(1)}, bf16[16,128,128]{2,1,0:T(8,128)(2,1)S(1)}, u32[]{:S(2)}, u32[]{:S(2)}) %collective-permute-start.12) | collective-permute-done | bytes 524320 | tf_op jit(solution)/shard_map/ppermute | solution.py:31
  52.5 1.8 %collective-permute-done.14 = bf16[16,128,128]{2,1,0:T(8,128)(2,1)S(1)} collective-permute-done((bf16[16,128,128]{2,1,0:T(8,128)(2,1)S(1)}, bf16[16,128,128]{2,1,0:T(8,128)(2,1)S(1)}, u32[]{:S(2)}, u32[]{:S(2)}) %collective-permute-start.14) | collective-permute-done | bytes 524320 | tf_op jit(solution)/shard_map/ppermute | solution.py:31
  54.3 0.4 fusion.11
  54.8 0.3 collective-permute-start.15
  55.1 2.6 %collective-permute-start.16 = (bf16[4,128,128]{2,1,0:T(8,128)(2,1)S(1)}, bf16[4,128,128]{2,1,0:T(8,128)(2,1)S(1)}, u32[]{:S(2)}, u32[]{:S(2)}) collective-permute-start(bf16[4,128,128]{2,1,0:T(8,128)(2,1)S(1)} %get-tuple-element.93), channel_id=1, source_target_pairs={{0,4},{1,17},{2,6},{3,19},{4,0},{5,21},{6,2},{7,23},{8,12},{9,25},... | collective-permute-start | bytes 393224 | tf_op jit(solution)/shard_map/ppermute | solution.py:31
  57.6 2.1 %collective-permute-start.17 = (bf16[4,128,128]{2,1,0:T(8,128)(2,1)S(1)}, bf16[4,128,128]{2,1,0:T(8,128)(2,1)S(1)}, u32[]{:S(2)}, u32[]{:S(2)}) collective-permute-start(bf16[4,128,128]{2,1,0:T(8,128)(2,1)S(1)} %get-tuple-element.92), channel_id=1, source_target_pairs={{0,6},{1,25},{2,4},{3,27},{4,2},{5,29},{6,0},{7,31},{8,14},{9,17},... | collective-permute-start | bytes 393224 | tf_op jit(solution)/shard_map/ppermute | solution.py:31
  59.8 0.2 collective-permute-done.15
  60.0 1.9 %collective-permute-done.16 = bf16[4,128,128]{2,1,0:T(8,128)(2,1)S(1)} collective-permute-done((bf16[4,128,128]{2,1,0:T(8,128)(2,1)S(1)}, bf16[4,128,128]{2,1,0:T(8,128)(2,1)S(1)}, u32[]{:S(2)}, u32[]{:S(2)}) %collective-permute-start.16) | collective-permute-done | bytes 131104 | tf_op jit(solution)/shard_map/ppermute | solution.py:31
  62.0 1.8 %collective-permute-done.17 = bf16[4,128,128]{2,1,0:T(8,128)(2,1)S(1)} collective-permute-done((bf16[4,128,128]{2,1,0:T(8,128)(2,1)S(1)}, bf16[4,128,128]{2,1,0:T(8,128)(2,1)S(1)}, u32[]{:S(2)}, u32[]{:S(2)}) %collective-permute-start.17) | collective-permute-done | bytes 131104 | tf_op jit(solution)/shard_map/ppermute | solution.py:31
  63.8 1.5 %layer.1 = (bf16[512,256]{1,0:T(8,128)(2,1)}, f32[512,128]{1,0:T(8,128)S(1)}, bf16[512,128]{1,0:T(8,128)(2,1)S(1)}, bf16[272,128]{1,0:T(8,128)(2,1)S(1)}, bf16[272,128]{1,0:T(8,128)(2,1)S(1)}) custom-call(s32[1]{0:T(128)} %bitcast.core, f32[512,128]{1,0:T(8,128)S(1)} %bitcast.24, bf16[512,128]{1,0:T(8,128)(2,1)S(1)} %bitcast.32, ...), custom_call_target="tpu_custom_call" | custom-call | tf_op jit(solution)/shard_map/layer/pallas_call | solution.py:227
  65.3 1.3 collective-permute-done.18
  66.6 2.3 %collective-permute-start.19 = (bf16[784,128]{1,0:T(8,128)(2,1)S(1)}, bf16[784,128]{1,0:T(8,128)(2,1)S(1)}, u32[]{:S(2)}, u32[]{:S(2)}) collective-permute-start(bf16[784,128]{1,0:T(8,128)(2,1)S(1)} %pad_maximum_fusion), channel_id=1, source_target_pairs={{0,8},{1,3},{2,10},{3,1},{4,12},{5,7},{6,14},{7,5},{8,0},{9,11},{1... | collective-permute-start | bytes 602120 | tf_op jit(solution)/shard_map/ppermute | solution.py:31
  68.9 1.4 collective-permute-start.20
  70.3 1.4 collective-permute-start.21
  71.7 0.9 collective-permute-done.19
  72.6 3.7 %collective-permute-done.20 = bf16[784,128]{1,0:T(8,128)(2,1)S(1)} collective-permute-done((bf16[784,128]{1,0:T(8,128)(2,1)S(1)}, bf16[784,128]{1,0:T(8,128)(2,1)S(1)}, u32[]{:S(2)}, u32[]{:S(2)}) %collective-permute-start.20) | collective-permute-done | bytes 200736 | tf_op jit(solution)/shard_map/ppermute | solution.py:31
  76.4 2.0 %collective-permute-done.21 = bf16[784,128]{1,0:T(8,128)(2,1)S(1)} collective-permute-done((bf16[784,128]{1,0:T(8,128)(2,1)S(1)}, bf16[784,128]{1,0:T(8,128)(2,1)S(1)}, u32[]{:S(2)}, u32[]{:S(2)}) %collective-permute-start.21) | collective-permute-done | bytes 200736 | tf_op jit(solution)/shard_map/ppermute | solution.py:31
  78.5 0.2 collective-permute-start.22
  78.7 3.0 %collective-permute-start.23 = (bf16[2320,128]{1,0:T(8,128)(2,1)S(1)}, bf16[2320,128]{1,0:T(8,128)(2,1)S(1)}, u32[]{:S(2)}, u32[]{:S(2)}) collective-permute-start(bf16[2320,128]{1,0:T(8,128)(2,1)S(1)} %get-tuple-element.88.rest_0_), channel_id=1, source_target_pairs={{0,4},{1,17},{2,6},{3,19},{4,0},{5,21},{6,2},{7,23},{8,12},{9,25},... | collective-permute-start | bytes 1781768 | tf_op jit(solution)/shard_map/ppermute | solution.py:31
  81.7 1.6 %collective-permute-start.24 = (bf16[2320,128]{1,0:T(8,128)(2,1)S(1)}, bf16[2320,128]{1,0:T(8,128)(2,1)S(1)}, u32[]{:S(2)}, u32[]{:S(2)}) collective-permute-start(bf16[2320,128]{1,0:T(8,128)(2,1)S(1)} %get-tuple-element.88.rest_0_), channel_id=1, source_target_pairs={{0,6},{1,25},{2,4},{3,27},{4,2},{5,29},{6,0},{7,31},{8,14},{9,17},... | collective-permute-start | bytes 1781768 | tf_op jit(solution)/shard_map/ppermute | solution.py:31
  83.3 5.2 %collective-permute-done.22.rest_1_ = bf16[2320,128]{1,0:T(8,128)(2,1)S(1)} collective-permute-done((bf16[2320,128]{1,0:T(8,128)(2,1)S(1)}, bf16[2320,128]{1,0:T(8,128)(2,1)S(1)}, u32[]{:S(2)}, u32[]{:S(2)}) %collective-permute-start.22) | collective-permute-done | bytes 593952 | tf_op jit(solution)/shard_map/ppermute | solution.py:31
  88.5 7.5 %collective-permute-done.23.rest_2_ = bf16[2320,128]{1,0:T(8,128)(2,1)S(1)} collective-permute-done((bf16[2320,128]{1,0:T(8,128)(2,1)S(1)}, bf16[2320,128]{1,0:T(8,128)(2,1)S(1)}, u32[]{:S(2)}, u32[]{:S(2)}) %collective-permute-start.23) | collective-permute-done | bytes 593952 | tf_op jit(solution)/shard_map/ppermute | solution.py:31
  96.0 3.1 %collective-permute-done.24.rest_3_ = bf16[2320,128]{1,0:T(8,128)(2,1)S(1)} collective-permute-done((bf16[2320,128]{1,0:T(8,128)(2,1)S(1)}, bf16[2320,128]{1,0:T(8,128)(2,1)S(1)}, u32[]{:S(2)}, u32[]{:S(2)}) %collective-permute-start.24) | collective-permute-done | bytes 593952 | tf_op jit(solution)/shard_map/ppermute | solution.py:31
  99.2 5.4 %collective-permute-start.25 = (bf16[272,128]{1,0:T(8,128)(2,1)S(1)}, bf16[272,128]{1,0:T(8,128)(2,1)S(1)}, u32[]{:S(2)}, u32[]{:S(2)}) collective-permute-start(bf16[272,128]{1,0:T(8,128)(2,1)S(1)} %add_convert_fusion.6), channel_id=1, source_target_pairs={{0,64},{32,96},{64,0},{96,32},{128,192},{160,224},{192,128},{224,1... | collective-permute-start | bytes 208904 | tf_op jit(solution)/shard_map/ppermute | solution.py:39
  104.7 2.0 %collective-permute-start.26 = (bf16[272,128]{1,0:T(8,128)(2,1)S(1)}, bf16[272,128]{1,0:T(8,128)(2,1)S(1)}, u32[]{:S(2)}, u32[]{:S(2)}) collective-permute-start(bf16[272,128]{1,0:T(8,128)(2,1)S(1)} %add_convert_fusion.6), channel_id=1, source_target_pairs={{0,128},{32,160},{64,192},{96,224},{128,0},{160,32},{192,64},{224,... | collective-permute-start | bytes 208904 | tf_op jit(solution)/shard_map/ppermute | solution.py:39
  106.7 1.7 %collective-permute-start.27 = (bf16[272,128]{1,0:T(8,128)(2,1)S(1)}, bf16[272,128]{1,0:T(8,128)(2,1)S(1)}, u32[]{:S(2)}, u32[]{:S(2)}) collective-permute-start(bf16[272,128]{1,0:T(8,128)(2,1)S(1)} %add_convert_fusion.6), channel_id=1, source_target_pairs={{0,192},{32,224},{64,128},{96,160},{128,64},{160,96},{192,0},{224,... | collective-permute-start | bytes 208904 | tf_op jit(solution)/shard_map/ppermute | solution.py:39
  108.4 10.6 %tiles_backward.1 = (f32[4,128,128]{2,1,0:T(8,128)S(1)}, bf16[4,128,128]{2,1,0:T(8,128)(2,1)S(1)}, bf16[4,128,128]{2,1,0:T(8,128)(2,1)S(1)}, bf16[4,128,128]{2,1...) custom-call(s32[1]{0:T(128)} %bitcast.22.count, ...), custom_call_target="tpu_custom_call" | custom-call | flops 1073741824 | bytes 16777216 | tf_op jit(solution)/shard_map/tiles_backward/pallas_call | solution.py:171
  119.0 0.7 copy-done.4
  119.8 1.0 collective-permute-start.40
  120.8 1.1 collective-permute-start.37
  121.9 1.5 %collective-permute-start.34 = (bf16[4,128,128]{2,1,0:T(8,128)(2,1)S(1)}, bf16[4,128,128]{2,1,0:T(8,128)(2,1)S(1)}, u32[]{:S(2)}, u32[]{:S(2)}) collective-permute-start(bf16[4,128,128]{2,1,0:T(8,128)(2,1)S(1)} %get-tuple-element.70), channel_id=1, source_target_pairs={{0,32},{32,64},{64,96},{96,128},{128,160},{160,192},{192,224},{224... | collective-permute-start | bytes 393224 | tf_op jit(solution)/shard_map/ppermute | solution.py:35
  123.4 3.6 %collective-permute-start.35 = (bf16[2,128,128]{2,1,0:T(8,128)(2,1)S(1)}, bf16[2,128,128]{2,1,0:T(8,128)(2,1)S(1)}, u32[]{:S(2)}, u32[]{:S(2)}) collective-permute-start(bf16[2,128,128]{2,1,0:T(8,128)(2,1)S(1)} %get-tuple-element.71), channel_id=1, source_target_pairs={{0,64},{32,96},{64,128},{96,160},{128,192},{160,224},{192,0},{224,... | collective-permute-start | bytes 196616 | tf_op jit(solution)/shard_map/ppermute | solution.py:35
  127.0 1.0 collective-permute-done.38
  128.0 1.9 %collective-permute-start.33 = (bf16[4,128,128]{2,1,0:T(8,128)(2,1)S(1)}, bf16[4,128,128]{2,1,0:T(8,128)(2,1)S(1)}, u32[]{:S(2)}, u32[]{:S(2)}) collective-permute-start(bf16[4,128,128]{2,1,0:T(8,128)(2,1)S(1)} %get-tuple-element.68), channel_id=1, source_target_pairs={{0,224},{32,0},{64,32},{96,64},{128,96},{160,128},{192,160},{224,1... | collective-permute-start | bytes 393224 | tf_op jit(solution)/shard_map/ppermute | solution.py:35
  130.0 2.8 %collective-permute-done.35 = bf16[2,128,128]{2,1,0:T(8,128)(2,1)S(1)} collective-permute-done((bf16[2,128,128]{2,1,0:T(8,128)(2,1)S(1)}, bf16[2,128,128]{2,1,0:T(8,128)(2,1)S(1)}, u32[]{:S(2)}, u32[]{:S(2)}) %collective-permute-start.35) | collective-permute-done | bytes 65568 | tf_op jit(solution)/shard_map/ppermute | solution.py:35
  132.8 2.1 %collective-permute-start.39 = (bf16[4,128,128]{2,1,0:T(8,128)(2,1)S(1)}, bf16[4,128,128]{2,1,0:T(8,128)(2,1)S(1)}, u32[]{:S(2)}, u32[]{:S(2)}) collective-permute-start(bf16[4,128,128]{2,1,0:T(8,128)(2,1)S(1)} %add_convert_fusion.3), channel_id=1, source_target_pairs={{0,192},{32,224},{64,0},{96,32},{128,64},{160,96},{192,128},{224,1... | collective-permute-start | bytes 393224 | tf_op jit(solution)/shard_map/ppermute | solution.py:35
  134.9 0.9 collective-permute-start.36
  135.9 4.7 %collective-permute-done.39.b2 = bf16[4,128,128]{2,1,0:T(8,128)(2,1)S(1)} collective-permute-done((bf16[4,128,128]{2,1,0:T(8,128)(2,1)S(1)}, bf16[4,128,128]{2,1,0:T(8,128)(2,1)S(1)}, u32[]{:S(2)}, u32[]{:S(2)}) %collective-permute-start.39) | collective-permute-done | bytes 131104 | tf_op jit(solution)/shard_map/ppermute | solution.py:35
  140.5 2.4 %collective-permute-done.36.f2 = bf16[4,128,128]{2,1,0:T(8,128)(2,1)S(1)} collective-permute-done((bf16[4,128,128]{2,1,0:T(8,128)(2,1)S(1)}, bf16[4,128,128]{2,1,0:T(8,128)(2,1)S(1)}, u32[]{:S(2)}, u32[]{:S(2)}) %collective-permute-start.36) | collective-permute-done | bytes 131104 | tf_op jit(solution)/shard_map/ppermute | solution.py:35
  143.0 0.6 copy-done.13
  143.6 2.2 %finish.1 = (f32[512,128]{1,0:T(8,128)}, f32[128,256]{1,0:T(8,128)}, f32[128,256]{1,0:T(8,128)}, f32[2,128]{1,0:T(2,128)}) custom-call(s32[1]{0:T(128)} %bitcast.core, f32[1]{0:T(128)} %constant.133.clone.1.scale, f32[512,128]{1,0:T(8,128)} %copy-done.3, f32[4,128,128]{2,1,0:T(8,128)} %copy-done.4, bf16[4,128,128]{2,1,0:T(8,128)(2,1)} %copy-done.10, ...), custom_call_target="tpu_custom_call" | custom-call | tf_op jit(solution)/shard_map/finish/pallas_call | solution.py:254
  (74 shorter events, 1.0 us)
Async XLA Ops:
  0.6 12.5 %collective-permute-start.3 = (bf16[512,128]{1,0:T(8,128)(2,1)}, bf16[512,128]{1,0:T(8,128)(2,1)S(1)}, u32[]{:S(2)}, u32[]{:S(2)}) collective-permute-start(bf16[512,128]{1,0:T(8,128)(2,1)} %feats.1), channel_id=1, source_target_pairs={{0,64},{32,96},{64,128},{96,160},{128,192},{160,224},{192,0},{224,... | collective-permute-start | bytes 393224 | tf_op jit(solution)/shard_map/ppermute | solution.py:35
  4.0 9.2 %collective-permute-start.1 = (bf16[512,128]{1,0:T(8,128)(2,1)}, bf16[512,128]{1,0:T(8,128)(2,1)S(1)}, u32[]{:S(2)}, u32[]{:S(2)}) collective-permute-start(bf16[512,128]{1,0:T(8,128)(2,1)} %feats.1), channel_id=1, source_target_pairs={{0,192},{32,224},{64,0},{96,32},{128,64},{160,96},{192,128},{224,1... | collective-permute-start | bytes 393224 | tf_op jit(solution)/shard_map/ppermute | solution.py:35
  6.2 12.0 %collective-permute-start.6 = (bf16[512,128]{1,0:T(8,128)(2,1)}, bf16[512,128]{1,0:T(8,128)(2,1)S(1)}, u32[]{:S(2)}, u32[]{:S(2)}) collective-permute-start(bf16[512,128]{1,0:T(8,128)(2,1)} %feats.1), channel_id=1, source_target_pairs={{0,32},{32,64},{64,96},{96,128},{128,160},{160,192},{192,224},{224... | collective-permute-start | bytes 393224 | tf_op jit(solution)/shard_map/ppermute | solution.py:35
  7.1 13.0 %collective-permute-start = (bf16[512,128]{1,0:T(8,128)(2,1)}, bf16[512,128]{1,0:T(8,128)(2,1)S(1)}, u32[]{:S(2)}, u32[]{:S(2)}) collective-permute-start(bf16[512,128]{1,0:T(8,128)(2,1)} %feats.1), channel_id=1, source_target_pairs={{0,224},{32,0},{64,32},{96,64},{128,96},{160,128},{192,160},{224,1... | collective-permute-start | bytes 393224 | tf_op jit(solution)/shard_map/ppermute | solution.py:35
  13.2 7.0 %collective-permute-start.4 = (bf16[256,128]{1,0:T(8,128)(2,1)S(1)}, bf16[256,128]{1,0:T(8,128)(2,1)S(1)}, u32[]{:S(2)}, u32[]{:S(2)}) collective-permute-start(bf16[256,128]{1,0:T(8,128)(2,1)S(1)} %slice.63), channel_id=1, source_target_pairs={{0,64},{32,96},{64,128},{96,160},{128,192},{160,224},{192,0},{224,... | collective-permute-start | bytes 196616 | tf_op jit(solution)/shard_map/ppermute | solution.py:35
  13.2 7.1 %collective-permute-start.7 = (bf16[256,128]{1,0:T(8,128)(2,1)S(1)}, bf16[256,128]{1,0:T(8,128)(2,1)S(1)}, u32[]{:S(2)}, u32[]{:S(2)}) collective-permute-start(bf16[256,128]{1,0:T(8,128)(2,1)S(1)} %slice.64), channel_id=1, source_target_pairs={{0,192},{32,224},{64,0},{96,32},{128,64},{160,96},{192,128},{224,1... | collective-permute-start | bytes 196616 | tf_op jit(solution)/shard_map/ppermute | solution.py:35
  17.4 5.0 %collective-permute-start.5 = (bf16[512,128]{1,0:T(8,128)(2,1)S(1)}, bf16[512,128]{1,0:T(8,128)(2,1)S(1)}, u32[]{:S(2)}, u32[]{:S(2)}) collective-permute-start(bf16[512,128]{1,0:T(8,128)(2,1)S(1)} %collective-permute-done.3), channel_id=1, source_target_pairs={{0,32},{32,64},{64,96},{96,128},{128,160},{160,192},{192,224},{224... | collective-permute-start | bytes 393224 | tf_op jit(solution)/shard_map/ppermute | solution.py:35
  18.2 5.2 %collective-permute-start.2 = (bf16[512,128]{1,0:T(8,128)(2,1)S(1)}, bf16[512,128]{1,0:T(8,128)(2,1)S(1)}, u32[]{:S(2)}, u32[]{:S(2)}) collective-permute-start(bf16[512,128]{1,0:T(8,128)(2,1)S(1)} %collective-permute-done.1), channel_id=1, source_target_pairs={{0,224},{32,0},{64,32},{96,64},{128,96},{160,128},{192,160},{224,1... | collective-permute-start | bytes 393224 | tf_op jit(solution)/shard_map/ppermute | solution.py:35
  23.4 0.9 copy-start
  24.3 39.5 %copy-start.1 = (bf16[512,128]{1,0:T(8,128)(2,1)S(1)}, bf16[512,128]{1,0:T(8,128)(2,1)}, u32[]{:S(2)}) copy-start(bf16[512,128]{1,0:T(8,128)(2,1)} %feats.1) | copy-start | bytes 393220
  24.3 39.5 %copy-start.2 = (bf16[512,256]{1,0:T(8,128)(2,1)S(1)}, bf16[512,256]{1,0:T(8,128)(2,1)}, u32[]{:S(2)}) copy-start(bf16[512,256]{1,0:T(8,128)(2,1)} %cot.1) | copy-start | bytes 786436
  24.3 39.5 %copy-start.5 = (bf16[128,256]{1,0:T(8,128)(2,1)S(1)}, bf16[128,256]{1,0:T(8,128)(2,1)}, u32[]{:S(2)}) copy-start(bf16[128,256]{1,0:T(8,128)(2,1)} %w_self.1) | copy-start | bytes 196612
  24.3 39.5 %copy-start.6 = (bf16[128,256]{1,0:T(8,128)(2,1)S(1)}, bf16[128,256]{1,0:T(8,128)(2,1)}, u32[]{:S(2)}) copy-start(bf16[128,256]{1,0:T(8,128)(2,1)} %w_neigh.1) | copy-start | bytes 196612
  24.3 39.5 %copy-start.7 = (f32[256]{0:T(256)S(1)}, f32[256]{0:T(256)}, u32[]{:S(2)}) copy-start(f32[256]{0:T(256)} %param.12) | copy-start | bytes 3076
  35.8 2.0 %collective-permute-start.9 = (bf16[16,128,128]{2,1,0:T(8,128)(2,1)S(1)}, bf16[16,128,128]{2,1,0:T(8,128)(2,1)S(1)}, u32[]{:S(2)}, u32[]{:S(2)}) collective-permute-start(bf16[16,128,128]{2,1,0:T(8,128)(2,1)S(1)} %get-tuple-element.47), channel_id=1, source_target_pairs={{0,1},{1,0},{2,3},{3,2},{4,5},{5,4},{6,7},{7,6},{8,9},{9,8},{10,11... | collective-permute-start | bytes 1572872 | tf_op jit(solution)/shard_map/ppermute | solution.py:27
  35.9 3.2 %collective-permute-start.11 = (bf16[16,128,128]{2,1,0:T(8,128)(2,1)S(1)}, bf16[16,128,128]{2,1,0:T(8,128)(2,1)S(1)}, u32[]{:S(2)}, u32[]{:S(2)}) collective-permute-start(bf16[16,128,128]{2,1,0:T(8,128)(2,1)S(1)} %get-tuple-element.49), channel_id=1, source_target_pairs={{0,1},{1,0},{2,3},{3,2},{4,5},{5,4},{6,7},{7,6},{8,9},{9,8},{10,11... | collective-permute-start | bytes 1572872 | tf_op jit(solution)/shard_map/ppermute | solution.py:27
  36.4 4.1 %collective-permute-start.13 = (bf16[16,128,128]{2,1,0:T(8,128)(2,1)S(1)}, bf16[16,128,128]{2,1,0:T(8,128)(2,1)S(1)}, u32[]{:S(2)}, u32[]{:S(2)}) collective-permute-start(bf16[16,128,128]{2,1,0:T(8,128)(2,1)S(1)} %get-tuple-element.51), channel_id=1, source_target_pairs={{0,1},{1,0},{2,3},{3,2},{4,5},{5,4},{6,7},{7,6},{8,9},{9,8},{10,11... | collective-permute-start | bytes 1572872 | tf_op jit(solution)/shard_map/ppermute | solution.py:27
  36.5 6.5 %collective-permute-start.8 = (bf16[16,128,128]{2,1,0:T(8,128)(2,1)S(1)}, bf16[16,128,128]{2,1,0:T(8,128)(2,1)S(1)}, u32[]{:S(2)}, u32[]{:S(2)}) collective-permute-start(bf16[16,128,128]{2,1,0:T(8,128)(2,1)S(1)} %get-tuple-element.45), channel_id=1, source_target_pairs={{0,1},{1,0},{2,3},{3,2},{4,5},{5,4},{6,7},{7,6},{8,9},{9,8},{10,11... | collective-permute-start | bytes 1572872 | tf_op jit(solution)/shard_map/ppermute | solution.py:27
  37.9 10.9 %collective-permute-start.10 = (bf16[16,128,128]{2,1,0:T(8,128)(2,1)S(1)}, bf16[16,128,128]{2,1,0:T(8,128)(2,1)S(1)}, u32[]{:S(2)}, u32[]{:S(2)}) collective-permute-start(bf16[16,128,128]{2,1,0:T(8,128)(2,1)S(1)} %add_convert_fusion.2), channel_id=1, source_target_pairs={{0,16},{1,5},{2,18},{3,7},{4,20},{5,1},{6,22},{7,3},{8,24},{9,13},... | collective-permute-start | bytes 1572872 | tf_op jit(solution)/shard_map/ppermute | solution.py:31
  39.2 13.3 %collective-permute-start.12 = (bf16[16,128,128]{2,1,0:T(8,128)(2,1)S(1)}, bf16[16,128,128]{2,1,0:T(8,128)(2,1)S(1)}, u32[]{:S(2)}, u32[]{:S(2)}) collective-permute-start(bf16[16,128,128]{2,1,0:T(8,128)(2,1)S(1)} %add_convert_fusion.1), channel_id=1, source_target_pairs={{0,8},{1,3},{2,10},{3,1},{4,12},{5,7},{6,14},{7,5},{8,0},{9,11},{1... | collective-permute-start | bytes 1572872 | tf_op jit(solution)/shard_map/ppermute | solution.py:31
  40.7 13.6 %collective-permute-start.14 = (bf16[16,128,128]{2,1,0:T(8,128)(2,1)S(1)}, bf16[16,128,128]{2,1,0:T(8,128)(2,1)S(1)}, u32[]{:S(2)}, u32[]{:S(2)}) collective-permute-start(bf16[16,128,128]{2,1,0:T(8,128)(2,1)S(1)} %add_convert_fusion), channel_id=1, source_target_pairs={{0,24},{1,7},{2,26},{3,5},{4,28},{5,3},{6,30},{7,1},{8,16},{9,15},... | collective-permute-start | bytes 1572872 | tf_op jit(solution)/shard_map/ppermute | solution.py:31
  54.8 5.2 %collective-permute-start.15 = (bf16[4,128,128]{2,1,0:T(8,128)(2,1)S(1)}, bf16[4,128,128]{2,1,0:T(8,128)(2,1)S(1)}, u32[]{:S(2)}, u32[]{:S(2)}) collective-permute-start(bf16[4,128,128]{2,1,0:T(8,128)(2,1)S(1)} %get-tuple-element.94), channel_id=1, source_target_pairs={{0,2},{1,9},{2,0},{3,11},{4,6},{5,13},{6,4},{7,15},{8,10},{9,1},{1... | collective-permute-start | bytes 393224 | tf_op jit(solution)/shard_map/ppermute | solution.py:31
  55.1 6.9 %collective-permute-start.16 = (bf16[4,128,128]{2,1,0:T(8,128)(2,1)S(1)}, bf16[4,128,128]{2,1,0:T(8,128)(2,1)S(1)}, u32[]{:S(2)}, u32[]{:S(2)}) collective-permute-start(bf16[4,128,128]{2,1,0:T(8,128)(2,1)S(1)} %get-tuple-element.93), channel_id=1, source_target_pairs={{0,4},{1,17},{2,6},{3,19},{4,0},{5,21},{6,2},{7,23},{8,12},{9,25},... | collective-permute-start | bytes 393224 | tf_op jit(solution)/shard_map/ppermute | solution.py:31
  57.6 6.2 %collective-permute-start.17 = (bf16[4,128,128]{2,1,0:T(8,128)(2,1)S(1)}, bf16[4,128,128]{2,1,0:T(8,128)(2,1)S(1)}, u32[]{:S(2)}, u32[]{:S(2)}) collective-permute-start(bf16[4,128,128]{2,1,0:T(8,128)(2,1)S(1)} %get-tuple-element.92), channel_id=1, source_target_pairs={{0,6},{1,25},{2,4},{3,27},{4,2},{5,29},{6,0},{7,31},{8,14},{9,17},... | collective-permute-start | bytes 393224 | tf_op jit(solution)/shard_map/ppermute | solution.py:31
  65.3 13.2 %copy-start.3 = (f32[512,128]{1,0:T(8,128)}, f32[512,128]{1,0:T(8,128)S(1)}, u32[]{:S(2)}) copy-start(f32[512,128]{1,0:T(8,128)S(1)} %get-tuple-element.53.base) | copy-start | bytes 786436
  65.3 1.3 collective-permute-start.18
  66.6 6.0 %collective-permute-start.19 = (bf16[784,128]{1,0:T(8,128)(2,1)S(1)}, bf16[784,128]{1,0:T(8,128)(2,1)S(1)}, u32[]{:S(2)}, u32[]{:S(2)}) collective-permute-start(bf16[784,128]{1,0:T(8,128)(2,1)S(1)} %pad_maximum_fusion), channel_id=1, source_target_pairs={{0,8},{1,3},{2,10},{3,1},{4,12},{5,7},{6,14},{7,5},{8,0},{9,11},{1... | collective-permute-start | bytes 602120 | tf_op jit(solution)/shard_map/ppermute | solution.py:31
  68.9 7.4 %collective-permute-start.20 = (bf16[784,128]{1,0:T(8,128)(2,1)S(1)}, bf16[784,128]{1,0:T(8,128)(2,1)S(1)}, u32[]{:S(2)}, u32[]{:S(2)}) collective-permute-start(bf16[784,128]{1,0:T(8,128)(2,1)S(1)} %pad_maximum_fusion), channel_id=1, source_target_pairs={{0,16},{1,5},{2,18},{3,7},{4,20},{5,1},{6,22},{7,3},{8,24},{9,13},... | collective-permute-start | bytes 602120 | tf_op jit(solution)/shard_map/ppermute | solution.py:31
  70.3 8.1 %collective-permute-start.21 = (bf16[784,128]{1,0:T(8,128)(2,1)S(1)}, bf16[784,128]{1,0:T(8,128)(2,1)S(1)}, u32[]{:S(2)}, u32[]{:S(2)}) collective-permute-start(bf16[784,128]{1,0:T(8,128)(2,1)S(1)} %pad_maximum_fusion), channel_id=1, source_target_pairs={{0,24},{1,7},{2,26},{3,5},{4,28},{5,3},{6,30},{7,1},{8,16},{9,15},... | collective-permute-start | bytes 602120 | tf_op jit(solution)/shard_map/ppermute | solution.py:31
  78.5 10.0 %collective-permute-start.22 = (bf16[2320,128]{1,0:T(8,128)(2,1)S(1)}, bf16[2320,128]{1,0:T(8,128)(2,1)S(1)}, u32[]{:S(2)}, u32[]{:S(2)}) collective-permute-start(bf16[2320,128]{1,0:T(8,128)(2,1)S(1)} %get-tuple-element.88.rest_0_), channel_id=1, source_target_pairs={{0,2},{1,9},{2,0},{3,11},{4,6},{5,13},{6,4},{7,15},{8,10},{9,1},{1... | collective-permute-start | bytes 1781768 | tf_op jit(solution)/shard_map/ppermute | solution.py:31
  78.7 17.4 %collective-permute-start.23 = (bf16[2320,128]{1,0:T(8,128)(2,1)S(1)}, bf16[2320,128]{1,0:T(8,128)(2,1)S(1)}, u32[]{:S(2)}, u32[]{:S(2)}) collective-permute-start(bf16[2320,128]{1,0:T(8,128)(2,1)S(1)} %get-tuple-element.88.rest_0_), channel_id=1, source_target_pairs={{0,4},{1,17},{2,6},{3,19},{4,0},{5,21},{6,2},{7,23},{8,12},{9,25},... | collective-permute-start | bytes 1781768 | tf_op jit(solution)/shard_map/ppermute | solution.py:31
  81.7 17.5 %collective-permute-start.24 = (bf16[2320,128]{1,0:T(8,128)(2,1)S(1)}, bf16[2320,128]{1,0:T(8,128)(2,1)S(1)}, u32[]{:S(2)}, u32[]{:S(2)}) collective-permute-start(bf16[2320,128]{1,0:T(8,128)(2,1)S(1)} %get-tuple-element.88.rest_0_), channel_id=1, source_target_pairs={{0,6},{1,25},{2,4},{3,27},{4,2},{5,29},{6,0},{7,31},{8,14},{9,17},... | collective-permute-start | bytes 1781768 | tf_op jit(solution)/shard_map/ppermute | solution.py:31
  83.3 21.4 %collective-permute-start.28 = (bf16[2320,128]{1,0:T(8,128)(2,1)S(1)}, bf16[2320,128]{1,0:T(8,128)(2,1)S(1)}, u32[]{:S(2)}, u32[]{:S(2)}) collective-permute-start(bf16[2320,128]{1,0:T(8,128)(2,1)S(1)} %get-tuple-element.88.rest_0_), channel_id=1, source_target_pairs={{0,1},{1,0},{2,3},{3,2},{4,5},{5,4},{6,7},{7,6},{8,9},{9,8},{10,11... | collective-permute-start | bytes 1781768 | tf_op jit(solution)/shard_map/ppermute | solution.py:27
  88.5 18.2 %collective-permute-start.29 = (bf16[2320,128]{1,0:T(8,128)(2,1)S(1)}, bf16[2320,128]{1,0:T(8,128)(2,1)S(1)}, u32[]{:S(2)}, u32[]{:S(2)}) collective-permute-start(bf16[2320,128]{1,0:T(8,128)(2,1)S(1)} %collective-permute-done.22.rest_1_), channel_id=1, source_target_pairs={{0,1},{1,0},{2,3},{3,2},{4,5},{5,4},{6,7},{7,6},{8,9},{9,8},{10,11... | collective-permute-start | bytes 1781768 | tf_op jit(solution)/shard_map/ppermute | solution.py:27
  96.0 12.3 %collective-permute-start.30 = (bf16[2320,128]{1,0:T(8,128)(2,1)S(1)}, bf16[2320,128]{1,0:T(8,128)(2,1)S(1)}, u32[]{:S(2)}, u32[]{:S(2)}) collective-permute-start(bf16[2320,128]{1,0:T(8,128)(2,1)S(1)} %collective-permute-done.23.rest_2_), channel_id=1, source_target_pairs={{0,1},{1,0},{2,3},{3,2},{4,5},{5,4},{6,7},{7,6},{8,9},{9,8},{10,11... | collective-permute-start | bytes 1781768 | tf_op jit(solution)/shard_map/ppermute | solution.py:27
  99.2 9.2 %collective-permute-start.31 = (bf16[2320,128]{1,0:T(8,128)(2,1)S(1)}, bf16[2320,128]{1,0:T(8,128)(2,1)S(1)}, u32[]{:S(2)}, u32[]{:S(2)}) collective-permute-start(bf16[2320,128]{1,0:T(8,128)(2,1)S(1)} %collective-permute-done.24.rest_3_), channel_id=1, source_target_pairs={{0,1},{1,0},{2,3},{3,2},{4,5},{5,4},{6,7},{7,6},{8,9},{9,8},{10,11... | collective-permute-start | bytes 1781768 | tf_op jit(solution)/shard_map/ppermute | solution.py:27
  99.2 20.5 %collective-permute-start.25 = (bf16[272,128]{1,0:T(8,128)(2,1)S(1)}, bf16[272,128]{1,0:T(8,128)(2,1)S(1)}, u32[]{:S(2)}, u32[]{:S(2)}) collective-permute-start(bf16[272,128]{1,0:T(8,128)(2,1)S(1)} %add_convert_fusion.6), channel_id=1, source_target_pairs={{0,64},{32,96},{64,0},{96,32},{128,192},{160,224},{192,128},{224,1... | collective-permute-start | bytes 208904 | tf_op jit(solution)/shard_map/ppermute | solution.py:39
  104.7 15.1 %collective-permute-start.26 = (bf16[272,128]{1,0:T(8,128)(2,1)S(1)}, bf16[272,128]{1,0:T(8,128)(2,1)S(1)}, u32[]{:S(2)}, u32[]{:S(2)}) collective-permute-start(bf16[272,128]{1,0:T(8,128)(2,1)S(1)} %add_convert_fusion.6), channel_id=1, source_target_pairs={{0,128},{32,160},{64,192},{96,224},{128,0},{160,32},{192,64},{224,... | collective-permute-start | bytes 208904 | tf_op jit(solution)/shard_map/ppermute | solution.py:39
  106.7 13.1 %collective-permute-start.27 = (bf16[272,128]{1,0:T(8,128)(2,1)S(1)}, bf16[272,128]{1,0:T(8,128)(2,1)S(1)}, u32[]{:S(2)}, u32[]{:S(2)}) collective-permute-start(bf16[272,128]{1,0:T(8,128)(2,1)S(1)} %add_convert_fusion.6), channel_id=1, source_target_pairs={{0,192},{32,224},{64,128},{96,160},{128,64},{160,96},{192,0},{224,... | collective-permute-start | bytes 208904 | tf_op jit(solution)/shard_map/ppermute | solution.py:39
  119.0 0.7 copy-start.4
  119.8 7.2 %collective-permute-start.40 = (bf16[272,128]{1,0:T(8,128)(2,1)S(1)}, bf16[272,128]{1,0:T(8,128)(2,1)S(1)}, u32[]{:S(2)}, u32[]{:S(2)}) collective-permute-start(bf16[272,128]{1,0:T(8,128)(2,1)S(1)} %add_convert_fusion.5), channel_id=1, source_target_pairs={{0,32},{32,0},{64,96},{96,64},{128,160},{160,128},{192,224},{224,1... | collective-permute-start | bytes 208904 | tf_op jit(solution)/shard_map/ppermute | solution.py:39
  120.8 9.1 %collective-permute-start.37 = (bf16[4,128,128]{2,1,0:T(8,128)(2,1)S(1)}, bf16[4,128,128]{2,1,0:T(8,128)(2,1)S(1)}, u32[]{:S(2)}, u32[]{:S(2)}) collective-permute-start(bf16[4,128,128]{2,1,0:T(8,128)(2,1)S(1)} %get-tuple-element.73), channel_id=1, source_target_pairs={{0,224},{32,0},{64,32},{96,64},{128,96},{160,128},{192,160},{224,1... | collective-permute-start | bytes 393224 | tf_op jit(solution)/shard_map/ppermute | solution.py:35
  121.9 6.1 %collective-permute-start.38 = (bf16[2,128,128]{2,1,0:T(8,128)(2,1)S(1)}, bf16[2,128,128]{2,1,0:T(8,128)(2,1)S(1)}, u32[]{:S(2)}, u32[]{:S(2)}) collective-permute-start(bf16[2,128,128]{2,1,0:T(8,128)(2,1)S(1)} %get-tuple-element.74), channel_id=1, source_target_pairs={{0,192},{32,224},{64,0},{96,32},{128,64},{160,96},{192,128},{224,1... | collective-permute-start | bytes 196616 | tf_op jit(solution)/shard_map/ppermute | solution.py:35
  121.9 13.0 %collective-permute-start.34 = (bf16[4,128,128]{2,1,0:T(8,128)(2,1)S(1)}, bf16[4,128,128]{2,1,0:T(8,128)(2,1)S(1)}, u32[]{:S(2)}, u32[]{:S(2)}) collective-permute-start(bf16[4,128,128]{2,1,0:T(8,128)(2,1)S(1)} %get-tuple-element.70), channel_id=1, source_target_pairs={{0,32},{32,64},{64,96},{96,128},{128,160},{160,192},{192,224},{224... | collective-permute-start | bytes 393224 | tf_op jit(solution)/shard_map/ppermute | solution.py:35
  123.4 9.4 %collective-permute-start.35 = (bf16[2,128,128]{2,1,0:T(8,128)(2,1)S(1)}, bf16[2,128,128]{2,1,0:T(8,128)(2,1)S(1)}, u32[]{:S(2)}, u32[]{:S(2)}) collective-permute-start(bf16[2,128,128]{2,1,0:T(8,128)(2,1)S(1)} %get-tuple-element.71), channel_id=1, source_target_pairs={{0,64},{32,96},{64,128},{96,160},{128,192},{160,224},{192,0},{224,... | collective-permute-start | bytes 196616 | tf_op jit(solution)/shard_map/ppermute | solution.py:35
  127.0 8.8 %collective-permute-start.32 = (bf16[4,128,128]{2,1,0:T(8,128)(2,1)S(1)}, bf16[4,128,128]{2,1,0:T(8,128)(2,1)S(1)}, u32[]{:S(2)}, u32[]{:S(2)}) collective-permute-start(bf16[4,128,128]{2,1,0:T(8,128)(2,1)S(1)} %get-tuple-element.67), channel_id=1, source_target_pairs={{0,32},{32,64},{64,96},{96,128},{128,160},{160,192},{192,224},{224... | collective-permute-start | bytes 393224 | tf_op jit(solution)/shard_map/ppermute | solution.py:35
  127.0 15.9 %copy-start.8 = (f32[272,128]{1,0:T(8,128)}, f32[272,128]{1,0:T(8,128)S(1)}, u32[]{:S(2)}) copy-start(f32[272,128]{1,0:T(8,128)S(1)} %convert_add_fusion.mine) | copy-start | bytes 417796
  128.0 7.8 %collective-permute-start.33 = (bf16[4,128,128]{2,1,0:T(8,128)(2,1)S(1)}, bf16[4,128,128]{2,1,0:T(8,128)(2,1)S(1)}, u32[]{:S(2)}, u32[]{:S(2)}) collective-permute-start(bf16[4,128,128]{2,1,0:T(8,128)(2,1)S(1)} %get-tuple-element.68), channel_id=1, source_target_pairs={{0,224},{32,0},{64,32},{96,64},{128,96},{160,128},{192,160},{224,1... | collective-permute-start | bytes 393224 | tf_op jit(solution)/shard_map/ppermute | solution.py:35
  129.9 5.9 %collective-permute-start.41 = (f32[272,128]{1,0:T(8,128)S(1)}, f32[272,128]{1,0:T(8,128)S(1)}, u32[]{:S(2)}, u32[]{:S(2)}) collective-permute-start(f32[272,128]{1,0:T(8,128)S(1)} %convert_add_fusion.mine), channel_id=1, source_target_pairs={{0,1},{1,0},{2,3},{3,2},{4,5},{5,4},{6,7},{7,6},{8,9},{9,8},{10,11... | collective-permute-start | bytes 417800 | tf_op jit(solution)/shard_map/ppermute | solution.py:27
  132.8 7.8 %collective-permute-start.39 = (bf16[4,128,128]{2,1,0:T(8,128)(2,1)S(1)}, bf16[4,128,128]{2,1,0:T(8,128)(2,1)S(1)}, u32[]{:S(2)}, u32[]{:S(2)}) collective-permute-start(bf16[4,128,128]{2,1,0:T(8,128)(2,1)S(1)} %add_convert_fusion.3), channel_id=1, source_target_pairs={{0,192},{32,224},{64,0},{96,32},{128,64},{160,96},{192,128},{224,1... | collective-permute-start | bytes 393224 | tf_op jit(solution)/shard_map/ppermute | solution.py:35
  134.9 8.0 %collective-permute-start.36 = (bf16[4,128,128]{2,1,0:T(8,128)(2,1)S(1)}, bf16[4,128,128]{2,1,0:T(8,128)(2,1)S(1)}, u32[]{:S(2)}, u32[]{:S(2)}) collective-permute-start(bf16[4,128,128]{2,1,0:T(8,128)(2,1)S(1)} %add_convert_fusion.4), channel_id=1, source_target_pairs={{0,64},{32,96},{64,128},{96,160},{128,192},{160,224},{192,0},{224,... | collective-permute-start | bytes 393224 | tf_op jit(solution)/shard_map/ppermute | solution.py:35
  135.8 7.1 %copy-start.10 = (bf16[4,128,128]{2,1,0:T(8,128)(2,1)}, bf16[4,128,128]{2,1,0:T(8,128)(2,1)S(1)}, u32[]{:S(2)}) copy-start(bf16[4,128,128]{2,1,0:T(8,128)(2,1)S(1)} %collective-permute-done.32.f1) | copy-start | bytes 393220
  135.8 7.1 %copy-start.11 = (bf16[4,128,128]{2,1,0:T(8,128)(2,1)}, bf16[4,128,128]{2,1,0:T(8,128)(2,1)S(1)}, u32[]{:S(2)}) copy-start(bf16[4,128,128]{2,1,0:T(8,128)(2,1)S(1)} %collective-permute-done.33.b1) | copy-start | bytes 393220
  135.8 7.1 %copy-start.9 = (f32[272,128]{1,0:T(8,128)}, f32[272,128]{1,0:T(8,128)S(1)}, u32[]{:S(2)}) copy-start(f32[272,128]{1,0:T(8,128)S(1)} %collective-permute-done.41.theirs) | copy-start | bytes 417796
  140.5 2.5 %copy-start.12 = (bf16[4,128,128]{2,1,0:T(8,128)(2,1)}, bf16[4,128,128]{2,1,0:T(8,128)(2,1)S(1)}, u32[]{:S(2)}) copy-start(bf16[4,128,128]{2,1,0:T(8,128)(2,1)S(1)} %collective-permute-done.39.b2) | copy-start | bytes 393220
  143.0 0.7 copy-start.13
